TPU v7x, 32 devices: a whole 2x2x4 slice. The times are simulated.
32 devices in a mesh: dp: 8 (over z, y), state: 4 (over x, core).
Axes of the slice: x: 2, y: 2, z: 4, core: 2. Of those that a mesh axis runs over, the one named last changes fastest.
Arguments:
- tokens: bfloat16 [2048, 2048], P('dp'), may hold values from -6 to 6
- norm_gain: float32 [2048], replicated, may hold values from 0.5 to 1.5
- w_x: bfloat16 [2048, 4096], P(None, 'state'), may hold values from -0.125 to 0.125
- w_z: bfloat16 [2048, 4096], P(None, 'state'), may hold values from -0.125 to 0.125
- conv_weight: float32 [4, 4096], P(None, 'state'), may hold values from -3 to 3
- conv_bias: float32 [4096], P('state'), may hold values from -3 to 3
- w_down: bfloat16 [4096, 128], P('state'), may hold values from -0.09375 to 0.09375
- w_up: bfloat16 [128, 4096], P(None, 'state'), may hold values from -0.5 to 0.5
- beta_bias: float32 [4096], P('state'), may hold values from -6 to 0
- w_keyq: bfloat16 [4096, 32], P('state'), may hold values from -0.09375 to 0.09375
- skip_gain: float32 [4096], P('state'), may hold values from 0.1 to 1.9
- w_out: bfloat16 [4096, 2048], P('state'), may hold values from -0.25 to 0.25
- cotangent: bfloat16 [2048, 2048], P('dp'), may hold values from -6 to 6
- group_ids: int32 [8], P('dp'), may hold values from 0 to 7
- group_weights: float32 [8], replicated, may hold values from 0.5 to 2
Outputs:
- block_out: bfloat16 [2048, 2048], P('dp', 'state')
- grad_tokens: float32 [2048, 2048], P('dp', 'state')
- grad_gain: float32 [2048], P('state')
- grad_wx: float32 [2048, 4096], P('dp', 'state')
- grad_wz: float32 [2048, 4096], P('dp', 'state')
- grad_conv_weight: float32 [4, 4096], P(None, 'state')
- grad_conv_bias: float32 [4096], P('state')
- grad_down: float32 [4096, 128], P('state')
- grad_up: float32 [128, 4096], P(None, 'state')
- grad_beta_bias: float32 [4096], P('state')
- grad_keyq: float32 [4096, 32], P('state')
- grad_skip: float32 [4096], P('state')
- grad_out: float32 [4096, 2048], P('state', 'dp')
- beta_max: float32 [], replicated
All inputs are finite; a program needn't handle non-finite values.
Results may differ from a plain program's by a relative error of at most 0.011.
Values may be sent and summed in bfloat16 or wider, within the bound.
No kernel may reach another device: no remote copies, remote signals or barrier semaphores. Data moves between devices by JAX's collectives and lax.ppermute only.
A program may use at most 256 MiB of HBM per device.

v0:
```python
import functools

import jax
import jax.numpy as jnp
from jax import lax
from jax.experimental import pallas as pl
from jax.experimental.pallas import tpu as pltpu
from jax.sharding import PartitionSpec as P

EPS = 1e-05
LANES = 128
SUB = 8
F32 = jnp.float32
BF16 = jnp.bfloat16
MIB = 2**20
WHOLE = pl.BlockSpec(memory_space=pltpu.VMEM)


def mm(left, right):
    return jnp.dot(left, right, preferred_element_type=F32)


def mm_nt(left, right):
    return lax.dot_general(left, right, (((1,), (1,)), ((), ())), preferred_element_type=F32)


def mm_tn(left, right):
    return lax.dot_general(left, right, (((0,), (0,)), ((), ())), preferred_element_type=F32)


def swap(value, axis, bit):
    size = lax.axis_size(axis)
    return lax.ppermute(value, axis, [(i, i ^ bit) for i in range(size)])


def bits_of(axis):
    size = lax.axis_size(axis)
    bits, bit = [], 1
    while bit < size:
        bits.append(bit)
        bit *= 2
    return bits


def all_sum(value, axis):
    for bit in bits_of(axis):
        value = value + swap(value, axis, bit)
    return value


def all_max(value, axis):
    for bit in bits_of(axis):
        value = jnp.maximum(value, swap(value, axis, bit))
    return value


def halves(value, dim, bit_set):
    kept = lax.dynamic_index_in_dim(value, bit_set, dim, keepdims=False)
    sent = lax.dynamic_index_in_dim(value, 1 - bit_set, dim, keepdims=False)
    return kept, sent


def all_but_last(value, axis):
    bits = bits_of(axis)
    for bit in bits[:-1]:
        value = value + swap(value, axis, bit)
    return value, swap(value, axis, bits[-1])


def shifted(value, by, rows):
    if by == 0:
        return value
    count = value.shape[0]
    moved = pltpu.roll(value, by % count, 0)
    keep = rows >= by if by > 0 else rows < count + by
    return jnp.where(keep, moved, 0.0)


def front_kernel(
    blocked, place, ids, weights, tok, cot, gain, wx, cw, cb, wd, wk,
    normed, up, prex, mixed, dsilu, part, *rest,
):
    step = pl.program_id(0)
    rows, width = tok.shape
    acc = rest[-1]

    @pl.when(step == 0)
    def _():
        value = tok[...].astype(F32)
        inv = lax.rsqrt(jnp.mean(value * value, axis=1, keepdims=True) + EPS)
        normed[...] = (value * inv * gain[...]).astype(BF16)
        part[...] = jnp.zeros_like(part)
        acc[...] = jnp.zeros_like(acc)

    pre = mm(normed[...], wx[...])
    prex[...] = pre
    row = lax.broadcasted_iota(jnp.int32, pre.shape, 0)
    taps = cw.shape[0]
    conv = cb[...] + sum(cw[j : j + 1, :] * shifted(pre, taps - 1 - j, row) for j in range(taps))
    sig = jax.nn.sigmoid(conv)
    mix = (conv * sig).astype(BF16)
    mixed[...] = mix
    dsilu[...] = sig * (1.0 + conv * (1.0 - sig))
    part[:rows, :] += mm(mix, wd[...])
    acc[...] += mm(mix, wk[...])

    @pl.when(step == pl.num_programs(0) - 1)
    def _():
        flat = jnp.transpose(acc[...])
        wide = flat.shape[0]
        for c in range(rows // LANES):
            part[rows + c * wide : rows + (c + 1) * wide, :] = flat[:, c * LANES : (c + 1) * LANES]
        up[...] = (cot[...].astype(F32) * weights[ids[0]]).astype(BF16)
        if blocked:
            far, near, own = rest[:3]
            own_rows = width // blocked
            for p in range(blocked):
                from_cols = pl.ds(pl.multiple_of((place[0] ^ p) * own_rows, own_rows), own_rows)
                dest = far.at[p & 1] if p & 2 else (near if p & 1 else own)
                for side, source in enumerate((normed, up)):
                    first = (side * (blocked // 4) + p // 4) * own_rows
                    dest[:, first : first + own_rows] = source[:, from_cols]


def front(
    place, group_ids, group_weights, tokens, cotangent, norm_gain, w_x,
    conv_weight, conv_bias, w_down, w_keyq, blocked,
):
    rows, width = tokens.shape
    inner = w_x.shape[1]
    rank, kq = w_down.shape[1], w_keyq.shape[1]
    blk = min(inner, 256)
    whole = lambda shape: pl.BlockSpec(shape, lambda i: (0,) * len(shape))
    cols = lambda height: pl.BlockSpec((height, blk), lambda i: (0, i))
    down = lambda wide: pl.BlockSpec((blk, wide), lambda i: (i, 0))
    smem = pl.BlockSpec(memory_space=pltpu.SMEM)
    part_rows = rows + kq * rows // LANES
    both = 2 * width // 4
    shapes = [(2, rows, both), (rows, both), (rows, both)] if blocked else []
    return pl.pallas_call(
        functools.partial(front_kernel, blocked),
        grid=(inner // blk,),
        in_specs=[
            smem,
            smem,
            smem,
            whole((rows, width)),
            whole((rows, width)),
            whole((1, width)),
            cols(width),
            cols(conv_weight.shape[0]),
            cols(1),
            down(rank),
            down(kq),
        ],
        out_specs=[
            whole((rows, width)),
            whole((rows, width)),
            cols(rows),
            cols(rows),
            cols(rows),
            whole((part_rows, LANES)),
        ]
        + [whole(shape) for shape in shapes],
        out_shape=[
            jax.ShapeDtypeStruct((rows, width), BF16),
            jax.ShapeDtypeStruct((rows, width), BF16),
            jax.ShapeDtypeStruct((rows, inner), F32),
            jax.ShapeDtypeStruct((rows, inner), BF16),
            jax.ShapeDtypeStruct((rows, inner), F32),
            jax.ShapeDtypeStruct((part_rows, LANES), F32),
        ]
        + [jax.ShapeDtypeStruct(shape, BF16) for shape in shapes],
        scratch_shapes=[pltpu.VMEM((rows, kq), F32)],
        compiler_params=pltpu.CompilerParams(vmem_limit_bytes=26 * MIB),
        name="front",
    )(
        place, group_ids, group_weights, tokens, cotangent, norm_gain[None], w_x,
        conv_weight, conv_bias[None], w_down, w_keyq,
    )


def gate_kernel(normed, up, wz, wo, silu, dgate, gy):
    pre = mm(normed[...], wz[...])
    back = mm_nt(up[...], wo[...])
    sig = jax.nn.sigmoid(pre)
    act = pre * sig
    silu[...] = act
    gy[...] = back * act
    dgate[...] = back * sig * (1.0 + pre * (1.0 - sig))


def gate(normed, upstream_b, w_z, w_out):
    rows, width = normed.shape
    inner = w_z.shape[1]
    blk = min(inner, 256)
    whole = lambda shape: pl.BlockSpec(shape, lambda i: (0, 0))
    cols = lambda height: pl.BlockSpec((height, blk), lambda i: (0, i))
    return pl.pallas_call(
        gate_kernel,
        grid=(inner // blk,),
        in_specs=[
            whole((rows, width)),
            whole((rows, width)),
            cols(width),
            pl.BlockSpec((blk, width), lambda i: (i, 0)),
        ],
        out_specs=[cols(rows)] * 3,
        out_shape=[jax.ShapeDtypeStruct((rows, inner), F32)] * 3,
        compiler_params=pltpu.CompilerParams(vmem_limit_bytes=24 * MIB),
        cost_estimate=pl.CostEstimate(
            flops=4 * rows * width * inner, bytes_accessed=14 * MIB, transcendentals=rows * inner
        ),
        name="gate",
    )(normed, upstream_b, w_z, w_out)


def key_query_of(one, two, rows, count):
    parts = []
    for c in range(rows // LANES):
        at = slice(rows + c * count, rows + (c + 1) * count)
        parts.append(one[at, :] + two[at, :])
    return jnp.transpose(jnp.concatenate(parts, axis=1))


def lay_tiles(dest, value, base=0):
    for j in range(SUB):
        dest[pl.ds(base * SUB + j, value.shape[0], stride=SUB), :] = value[
            :, j * LANES : (j + 1) * LANES
        ]


def lay_rows(source, count, j):
    return source[pl.ds(j, count, stride=SUB), :]


def spread(dest, key_query):
    rows, count = key_query.shape
    for n in range(count):
        dest[n * rows : (n + 1) * rows, :] = jnp.broadcast_to(
            key_query[:, n : n + 1], (rows, LANES)
        )


def pick(source, rows, n, t):
    return source[pl.ds(n * rows + t, SUB, stride=0), :]


def scan_kernel(
    unroll, one, two, mixed, wup, bias, silu, dgate, skip,
    gated, prez, step_out, raw_out, peak, hist, last, step_t, mix_t, out_t, kb,
):
    rows, inner = mixed.shape
    states = kb.shape[0] // rows // 2
    kq = key_query_of(one, two, rows, 2 * states)
    keys = kq[:, :states]
    norm = jnp.sum(keys * keys, axis=1, keepdims=True)
    spread(kb, kq)
    rank_b = (one[:rows, :] + two[:rows, :]).astype(BF16)
    raw = jax.nn.sigmoid(mm(rank_b, wup[...]) + bias[...])
    raw_out[...] = raw
    highest = jnp.max(jnp.max(raw, axis=0, keepdims=True), axis=1, keepdims=True)
    peak[...] = jnp.broadcast_to(highest, peak.shape)
    beta = raw.astype(BF16).astype(F32)
    size = beta / (1.0 + beta * norm)
    step_out[...] = size
    lay_tiles(step_t, size)
    lay_tiles(mix_t, mixed[...].astype(F32))

    def token(t, carried):
        at = pl.ds(pl.multiple_of(t * SUB, SUB), SUB)
        size = step_t[at, :]
        mix = mix_t[at, :]
        sums = [None] * 4
        following = []
        for n in range(states):
            key = pick(kb, rows, n, t)
            query = pick(kb, rows, states + n, t)
            state = carried[n]
            hist[t, n] = state
            state = state + (size * key) * (mix - key * state)
            term = query * state
            sums[n % 4] = term if sums[n % 4] is None else sums[n % 4] + term
            following.append(state)
        out_t[at, :] = (sums[0] + sums[1]) + (sums[2] + sums[3])
        return tuple(following)

    zero = jnp.zeros((SUB, LANES), F32)
    final = lax.fori_loop(0, rows, token, (zero,) * states, unroll=unroll)
    for n in range(states):
        last[n] = final[n]
    for j in range(SUB):
        at = slice(j * LANES, (j + 1) * LANES)
        y = lay_rows(out_t, rows, j) + skip[:, at] * mixed[:, at].astype(F32)
        gated[:, at] = (y * silu[:, at]).astype(BF16)
        prez[:, at] = (y * dgate[:, at]).astype(BF16)


def scan_forward(summed, mixed, w_up, beta_bias, silu, dgate, skip_gain, states):
    rows, inner = mixed.shape
    full = lambda dtype: jax.ShapeDtypeStruct((rows, inner), dtype)
    return pl.pallas_call(
        functools.partial(scan_kernel, 4),
        in_specs=[WHOLE] * 8,
        out_specs=[WHOLE] * 7,
        out_shape=[
            full(BF16),
            full(BF16),
            full(F32),
            full(F32),
            jax.ShapeDtypeStruct((SUB, LANES), F32),
            pltpu.VMEM((rows, states, SUB, LANES), F32),
            jax.ShapeDtypeStruct((states, SUB, LANES), F32),
        ],
        scratch_shapes=[pltpu.VMEM((rows * SUB, LANES), F32)] * 3
        + [pltpu.VMEM((2 * states * rows, LANES), F32)],
        compiler_params=pltpu.CompilerParams(vmem_limit_bytes=22 * MIB),
        cost_estimate=pl.CostEstimate(
            flops=60 * rows * inner * states, bytes_accessed=16 * MIB, transcendentals=0
        ),
        name="scan",
    )(*summed, mixed, w_up, beta_bias[None], silu, dgate, skip_gain[None])


def back_kernel(
    unroll, place, one, two, mixed, wup, step_in, raw_in, gy, hist, last, peak,
    gmix, pay, ups, preb, step_t, mix_t, gs_t, kb, sum_d, sum_s, prods, zk, zq,
):
    rows, inner = mixed.shape
    states = last.shape[0]
    rank = wup.shape[0]
    span = zk.shape[0] // states
    kq = key_query_of(one, two, rows, 2 * states)
    keys = kq[:, :states]
    norm = jnp.sum(keys * keys, axis=1, keepdims=True)
    spread(kb, kq)
    lay_tiles(step_t, step_in[...])
    lay_tiles(mix_t, mixed[...].astype(F32) * 0.5)
    gs_t[0:SUB, :] = jnp.zeros((SUB, LANES), F32)
    lay_tiles(gs_t, gy[...].astype(BF16).astype(F32), 1)

    def reduce_to(dest, row, terms, slot):
        base = slot * states * SUB
        for n in range(states):
            prods[pl.ds(base + n * SUB, SUB), :] = terms[n]
        for g in range(states // SUB):
            total = None
            for s in range(SUB):
                part = prods[pl.ds(base + g * SUB * SUB + s, SUB, stride=SUB), :]
                total = part if total is None else total + part
            dest[pl.ds(row + g * SUB * span, SUB, stride=span), :] = total

    tail = gs_t[pl.ds(rows * SUB, SUB), :]
    reduce_to(zq, rows, [last[n] * tail for n in range(states)], 0)

    def token(t, u, carried):
        at = pl.ds(pl.multiple_of(t * SUB, SUB), SUB)
        size = step_t[at, :]
        half = mix_t[at, :]
        before = gs_t[at, :]
        grad = gs_t[pl.ds(pl.multiple_of(t * SUB + SUB, SUB), SUB), :]
        drive = size * half
        total_d, total_s = [None] * 2, [None] * 2
        following, for_key, for_query = [], [], []
        for n in range(states):
            key = pick(kb, rows, n, t)
            query = pick(kb, rows, states + n, t)
            state = hist[t, n]
            full = query * grad + carried[n]
            by_key = full * key
            by_state = by_key * state
            term = key * by_state
            following.append(full - key * (size * by_key))
            for_key.append(full * drive - size * by_state)
            for_query.append(state * before)
            i = n % 2
            total_d[i] = by_key if total_d[i] is None else total_d[i] + by_key
            total_s[i] = term if total_s[i] is None else total_s[i] + term
        sum_d[at, :] = total_d[0] + total_d[1]
        sum_s[at, :] = total_s[0] + total_s[1]
        reduce_to(zk, t, for_key, 2 * u)
        reduce_to(zq, t, for_query, 2 * u + 1)
        return tuple(following)

    def some(i, carried):
        for u in range(unroll):
            carried = token(rows - 1 - (i * unroll + u), u, carried)
        return carried

    zero = jnp.zeros((SUB, LANES), F32)
    lax.fori_loop(0, rows // unroll, some, (zero,) * states)

    total_norm = jnp.zeros((rows, 1), F32)
    for j in range(SUB):
        at = slice(j * LANES, (j + 1) * LANES)
        drive_grad = lay_rows(sum_d, rows, j)
        size = step_in[:, at]
        grad_step = drive_grad * mixed[:, at].astype(F32) - lay_rows(sum_s, rows, j)
        gmix[:, at] = drive_grad * size
        total_norm = total_norm - jnp.sum(grad_step * size * size, axis=1, keepdims=True)
        raw = raw_in[:, at]
        plus = 1.0 + raw.astype(BF16).astype(F32) * norm
        pre = grad_step / (plus * plus) * raw * (1.0 - raw)
        ups[rank : rank + SUB, at] = jnp.broadcast_to(
            jnp.sum(pre, axis=0, keepdims=True), (SUB, LANES)
        )
        preb[:, at] = pre.astype(BF16)
    pay[:rows, :] = mm_nt(preb[...], wup[...])
    rank_b = (one[:rows, :] + two[:rows, :]).astype(BF16)
    ups[:rank, :] = mm_tn(rank_b, preb[...])

    source = lax.broadcasted_iota(jnp.int32, (LANES, LANES), 1)
    lane = lax.broadcasted_iota(jnp.int32, (rows, LANES), 1)
    row = lax.broadcasted_iota(jnp.int32, (rows, LANES), 0)
    table = jnp.where(lane == 2 * states, jnp.broadcast_to(total_norm, (rows, LANES)), 0.0)
    mark = (lane == 2 * states + 1) & (row == place[1])
    table = jnp.where(mark, jnp.broadcast_to(peak[0:1, :], (rows, LANES)), table)
    for n in range(states):
        table = table + mm(
            zk[pl.ds(n * span, rows), :], jnp.where(source == n, 2.0, 0.0)
        )
        table = table + mm(
            zq[pl.ds(n * span + 1, rows), :], jnp.where(source == states + n, 1.0, 0.0)
        )
    flat = jnp.transpose(table)
    high = (pay.shape[0] - rows) * LANES // rows
    for c in range(rows // LANES):
        pay[rows + c * high : rows + (c + 1) * high, :] = flat[:high, c * LANES : (c + 1) * LANES]


def scan_backward(place, summed, mixed, w_up, step_in, raw, gy, hist, last, peak):
    rows, inner = mixed.shape
    states = last.shape[0]
    unroll = 2
    span = rows + SUB
    high = 2 * states + SUB
    pay_rows = rows + high * rows // LANES
    return pl.pallas_call(
        functools.partial(back_kernel, unroll),
        in_specs=[pl.BlockSpec(memory_space=pltpu.SMEM)] + [WHOLE] * 10,
        out_specs=[WHOLE] * 3,
        out_shape=[
            jax.ShapeDtypeStruct((rows, inner), F32),
            jax.ShapeDtypeStruct((pay_rows, LANES), F32),
            jax.ShapeDtypeStruct((w_up.shape[0] + SUB, inner), F32),
        ],
        scratch_shapes=[
            pltpu.VMEM((rows, inner), BF16),
            pltpu.VMEM((rows * SUB, LANES), F32),
            pltpu.VMEM((rows * SUB, LANES), F32),
            pltpu.VMEM((rows * SUB + SUB, LANES), F32),
            pltpu.VMEM((2 * states * rows, LANES), F32),
            pltpu.VMEM((rows * SUB, LANES), F32),
            pltpu.VMEM((rows * SUB, LANES), F32),
            pltpu.VMEM((unroll * 2 * states * SUB, LANES), F32),
            pltpu.VMEM((states * span, LANES), F32),
            pltpu.VMEM((states * span, LANES), F32),
        ],
        compiler_params=pltpu.CompilerParams(vmem_limit_bytes=28 * MIB),
        cost_estimate=pl.CostEstimate(
            flops=60 * rows * inner * states, bytes_accessed=16 * MIB, transcendentals=0
        ),
        name="back",
    )(
        place, *summed, mixed, w_up, step_in, raw, gy,
        pltpu.with_memory_space_constraint(hist, pltpu.VMEM), last, peak,
    )


def conv_kernel(
    place, one, two, grad_one, grad_two, mixed, gy, gmix, dsilu, prex, cw, skip, wd, wk,
    prex_b, down, rest,
):
    rows, inner = mixed.shape
    count = wk.shape[1]
    states = count // 2
    high = (grad_one.shape[0] - rows) * LANES // rows
    kq = key_query_of(one, two, rows, count)
    gkq = key_query_of(grad_one, grad_two, rows, high)
    norm_grad = gkq[:, count : count + 1]
    peak = jnp.max(gkq[:, count + 1 : count + 2], axis=0, keepdims=True)
    lane = lax.broadcasted_iota(jnp.int32, (rows, count), 1)
    kq_b = (gkq[:, :count] + jnp.where(lane < states, 2.0 * kq * norm_grad, 0.0)).astype(BF16)
    rank_b = (grad_one[:rows, :] + grad_two[:rows, :]).astype(BF16)
    taps = cw.shape[0]
    blk = 256
    for c in range(inner // blk):
        at = slice(c * blk, (c + 1) * blk)
        mix = mixed[:, at].astype(F32)
        grad_y = gy[:, at]
        total = grad_y * skip[:, at] + gmix[:, at]
        total = total + mm_nt(kq_b, wk[at, :]) + mm_nt(rank_b, wd[at, :])
        grad = total * dsilu[:, at]
        pre = prex[:, at]
        row = lax.broadcasted_iota(jnp.int32, grad.shape, 0)
        out = None
        sums = []
        for j in range(taps):
            by = taps - 1 - j
            sums.append(jnp.sum(grad * shifted(pre, by, row), axis=0, keepdims=True))
            term = cw[j : j + 1, at] * shifted(grad, -by, row)
            out = term if out is None else out + term
        sums.append(jnp.sum(grad, axis=0, keepdims=True))
        sums.append(jnp.sum(grad_y * mix, axis=0, keepdims=True))
        channel = lax.broadcasted_iota(jnp.int32, (1, blk), 1) + c * blk
        sums.append(jnp.where(channel == place[0], jnp.broadcast_to(peak, (1, blk)), 0.0))
        for i, line in enumerate(sums):
            rest[count + i : count + i + 1, at] = line
        prex_b[:, at] = out.astype(BF16)
    for i in range(len(sums), SUB):
        rest[count + i : count + i + 1, :] = jnp.zeros((1, inner), F32)
    down[...] = mm_tn(mixed[...], rank_b)
    rest[:count, :] = mm_tn(kq_b, mixed[...])


def conv_back(
    place, summed, grads, mixed, gy, gmix, dsilu, prex, conv_weight, skip_gain, w_down, w_keyq
):
    rows, inner = mixed.shape
    return pl.pallas_call(
        conv_kernel,
        in_specs=[pl.BlockSpec(memory_space=pltpu.SMEM)] + [WHOLE] * 13,
        out_specs=[WHOLE] * 3,
        out_shape=[
            jax.ShapeDtypeStruct((rows, inner), BF16),
            jax.ShapeDtypeStruct((inner, w_down.shape[1]), F32),
            jax.ShapeDtypeStruct((w_keyq.shape[1] + SUB, inner), F32),
        ],
        compiler_params=pltpu.CompilerParams(vmem_limit_bytes=24 * MIB),
        name="conv",
    )(
        place, *summed, *grads, mixed, gy, gmix, dsilu, prex, conv_weight, skip_gain[None],
        w_down, w_keyq,
    )


def branch_kernel(place, gated, wo, tok, send, keep):
    i = pl.program_id(0)
    value = mm(gated[...], wo[...])

    @pl.when(i == 0)
    def _():
        keep[0] = value + tok[...].astype(F32)

    @pl.when(i == 2)
    def _():
        keep[0] = value

    @pl.when(i % 2 == 1)
    def _():
        send[0] = value.astype(BF16)


def branch(place, gated, w_out, tokens, parts):
    rows, inner = gated.shape
    width = w_out.shape[1]
    own = width // parts
    return pl.pallas_call(
        branch_kernel,
        grid_spec=pltpu.PrefetchScalarGridSpec(
            num_scalar_prefetch=1,
            grid=(parts,),
            in_specs=[
                pl.BlockSpec((rows, inner), lambda i, place: (0, 0)),
                pl.BlockSpec((inner, own), lambda i, place: (0, place[1] ^ i)),
                pl.BlockSpec((rows, own), lambda i, place: (0, place[1])),
            ],
            out_specs=[pl.BlockSpec((1, rows, own), lambda i, place: (i // 2, 0, 0))] * 2,
        ),
        out_shape=[
            jax.ShapeDtypeStruct((parts // 2, rows, own), BF16),
            jax.ShapeDtypeStruct((parts // 2, rows, own), F32),
        ],
        compiler_params=pltpu.CompilerParams(vmem_limit_bytes=16 * MIB),
        cost_estimate=pl.CostEstimate(
            flops=2 * rows * inner * width, bytes_accessed=8 * MIB, transcendentals=0
        ),
        name="branch",
    )(place, gated, w_out, tokens)


def input_kernel(
    place, ids, weights, prex, prez, wx, wz, tok, tok_own, cot, gain,
    send, keep, stats, slope, shift, base, inv, dots,
):
    i = pl.program_id(0)
    rows, width = tok.shape

    @pl.when(i == 0)
    def _():
        value = tok[...].astype(F32)
        inv[...] = jnp.broadcast_to(
            lax.rsqrt(jnp.mean(value * value, axis=1, keepdims=True) + EPS), inv.shape
        )
        dots[...] = jnp.zeros_like(dots)

    value = mm_nt(prex[...], wx[...]) + mm_nt(prez[...], wz[...])
    rms = inv[:, 0:1]
    unit = tok_own[...].astype(F32) * rms
    by_unit = value * unit
    dots[...] += jnp.sum(by_unit * gain[...], axis=1, keepdims=True)
    line = jnp.sum(by_unit, axis=0, keepdims=True)
    own = line.shape[1] // LANES
    first = rows // LANES + (place[1] ^ i) * own
    for j in range(own):
        stats[pl.ds(first + j, 1), :] = line[:, j * LANES : (j + 1) * LANES]

    @pl.when(i == 0)
    def _():
        slope[...] = rms * gain[...]
        shift[...] = unit * rms * (1.0 / width)
        base[...] = cot[...].astype(F32) * weights[ids[0]]

    @pl.when(i % 2 == 0)
    def _():
        keep[0] = value

    @pl.when(i % 2 == 1)
    def _():
        send[0] = value.astype(BF16)

    @pl.when(i == pl.num_programs(0) - 1)
    def _():
        flat = jnp.transpose(dots[...])
        for c in range(rows // LANES):
            stats[c : c + 1, :] = flat[0:1, c * LANES : (c + 1) * LANES]


def input_grad(
    place, group_ids, group_weights, prex, prez, w_x, w_z, tokens, cotangent, norm_gain, parts
):
    rows, inner = prex.shape
    width = tokens.shape[1]
    own = width // parts
    whole = lambda shape: pl.BlockSpec(shape, lambda i, place: (0, 0))
    part = pl.BlockSpec((own, inner), lambda i, place: (place[1] ^ i, 0))
    mine = pl.BlockSpec((rows, own), lambda i, place: (0, 0))
    smem = pl.BlockSpec(memory_space=pltpu.SMEM)
    stat_rows = rows // LANES + width // LANES
    return pl.pallas_call(
        input_kernel,
        grid_spec=pltpu.PrefetchScalarGridSpec(
            num_scalar_prefetch=1,
            grid=(parts,),
            in_specs=[
                smem,
                smem,
                whole((rows, inner)),
                whole((rows, inner)),
                part,
                part,
                whole((rows, width)),
                pl.BlockSpec((rows, own), lambda i, place: (0, place[1] ^ i)),
                pl.BlockSpec((rows, own), lambda i, place: (0, place[1])),
                pl.BlockSpec((1, own), lambda i, place: (0, place[1] ^ i)),
            ],
            out_specs=[pl.BlockSpec((1, rows, own), lambda i, place: (i // 2, 0, 0))] * 2
            + [whole((stat_rows, LANES)), mine, mine, mine],
            scratch_shapes=[pltpu.VMEM((rows, LANES), F32)] * 2,
        ),
        out_shape=[
            jax.ShapeDtypeStruct((parts // 2, rows, own), BF16),
            jax.ShapeDtypeStruct((parts // 2, rows, own), F32),
            jax.ShapeDtypeStruct((stat_rows, LANES), F32),
        ]
        + [jax.ShapeDtypeStruct((rows, own), F32)] * 3,
        compiler_params=pltpu.CompilerParams(vmem_limit_bytes=24 * MIB),
        cost_estimate=pl.CostEstimate(
            flops=4 * rows * inner * width, bytes_accessed=12 * MIB, transcendentals=0
        ),
        name="inputs",
    )(
        place, group_ids, group_weights, prex, prez, w_x, w_z, tokens, tokens, cotangent,
        norm_gain[None],
    )


def out_weight_kernel(l0, l1, l2, l3, r0, r1, r2, r3, keep, send):
    own = keep.shape[1]
    total = None
    for left, right in ((l0, r0[:, 2 * own :]), (l1, r1[0, :, 2 * own :]), (l2, r2[:, 2 * own :]), (l3, r3[:, 2 * own :])):
        term = mm_tn(left[...], right)
        total = term if total is None else total + term
    keep[...] = total[:, :own]
    send[...] = total[:, own:].astype(BF16)


def out_weight(lefts, rights):
    rows, inner = lefts[0].shape
    own = rights[0].shape[1] // 4
    blk = 256
    whole = lambda value: pl.BlockSpec(value.shape, lambda i: (0,) * value.ndim)
    return pl.pallas_call(
        out_weight_kernel,
        grid=(inner // blk,),
        in_specs=[pl.BlockSpec((rows, blk), lambda i: (0, i))] * 4 + [whole(r) for r in rights],
        out_specs=[pl.BlockSpec((blk, own), lambda i: (i, 0))] * 2,
        out_shape=[
            jax.ShapeDtypeStruct((inner, own), F32),
            jax.ShapeDtypeStruct((inner, own), BF16),
        ],
        compiler_params=pltpu.CompilerParams(vmem_limit_bytes=20 * MIB),
        cost_estimate=pl.CostEstimate(
            flops=16 * rows * inner * own, bytes_accessed=6 * MIB, transcendentals=0
        ),
        name="outw",
    )(*lefts, *rights)


def in_weight_kernel(l0, l1, l2, l3, r0, r1, r2, r3, keep, send):
    i = pl.program_id(0)
    total = None
    for left, right in ((l0[...], r0), (l1[0], r1), (l2[...], r2), (l3[...], r3)):
        term = mm_tn(left, right[...])
        total = term if total is None else total + term

    @pl.when(i == 0)
    def _():
        send[...] = total.astype(BF16)

    @pl.when(i == 1)
    def _():
        keep[...] = total


def in_weight(lefts, rights):
    rows, inner = rights[0].shape
    own = lefts[0].shape[1] // 4
    whole = lambda value: pl.BlockSpec(value.shape, lambda i: (0,) * value.ndim)
    side = pl.BlockSpec((rows, own), lambda i: (0, 1 - i))
    return pl.pallas_call(
        in_weight_kernel,
        grid=(2,),
        in_specs=[side, pl.BlockSpec((1, rows, own), lambda i: (0, 0, 1 - i)), side, side]
        + [whole(r) for r in rights],
        out_specs=[pl.BlockSpec((own, inner), lambda i: (0, 0))] * 2,
        out_shape=[
            jax.ShapeDtypeStruct((own, inner), F32),
            jax.ShapeDtypeStruct((own, inner), BF16),
        ],
        compiler_params=pltpu.CompilerParams(vmem_limit_bytes=20 * MIB),
        cost_estimate=pl.CostEstimate(
            flops=16 * rows * inner * own, bytes_accessed=6 * MIB, transcendentals=0
        ),
        name="inw",
    )(*lefts, *rights)


def split_bits(axis):
    bits = bits_of(axis)
    return [bit for bit in (2, 1) if bit in bits], [bit for bit in reversed(bits) if bit > 2]


def gather_tokens(value, axis):
    pieces = [value]
    for bit in split_bits(axis)[0]:
        pieces = pieces + [swap(piece, axis, bit) for piece in pieces]
    return pieces


def exchange_cols(value, axis):
    size = lax.axis_size(axis)
    me = lax.axis_index(axis)
    gather, scatter = split_bits(axis)
    rows, cols = value.shape
    outer = 2 ** len(scatter)
    pieces = [value.reshape((rows, outer) + (2,) * len(gather) + (cols // size,))]
    for bit in gather:
        kept, sent = zip(*(halves(piece, 2, (me // bit) % 2) for piece in pieces))
        pieces = list(kept) + [swap(piece, axis, bit) for piece in sent]
    return [piece.reshape(rows, -1) for piece in pieces]


def scatter_sum(value, axis, dim):
    me = lax.axis_index(axis)
    scatter = split_bits(axis)[1]
    for bit in scatter:
        shape = value.shape
        split = shape[:dim] + (2, shape[dim] // 2) + shape[dim + 1 :]
        kept, sent = halves(value.reshape(split), dim, (me // bit) % 2)
        value = kept + swap(sent.astype(BF16), axis, bit).astype(F32)
    return value


def per_device(
    tokens,
    norm_gain,
    w_x,
    w_z,
    conv_weight,
    conv_bias,
    w_down,
    w_up,
    beta_bias,
    w_keyq,
    skip_gain,
    w_out,
    cotangent,
    group_ids,
    group_weights,
):
    rows, width = tokens.shape
    states = w_keyq.shape[1] // 2
    taps = conv_weight.shape[0]
    assert group_ids.shape[0] == 1
    parts = lax.axis_size("state")
    assert parts == 4
    dp_size = lax.axis_size("dp")
    own_width = width // parts
    state_index = lax.axis_index("state")
    place = jnp.stack([lax.axis_index("dp"), state_index]).astype(jnp.int32)
    blocked = dp_size if dp_size == 8 and width % (8 * LANES) == 0 else 0

    normed, upstream_b, pre_x, mixed_b, dsilu, part, *blocks = front(
        place, group_ids, group_weights, tokens, cotangent, norm_gain, w_x,
        conv_weight, conv_bias, w_down, w_keyq, blocked,
    )
    summed = all_but_last(part, "state")
    if blocked:
        far, near, own = blocks
        far = swap(far, "dp", 2)
        sides = (own, far, swap(near, "dp", 1), swap(far[1], "dp", 1))
    else:
        norm_parts = exchange_cols(normed, "dp")
        up_parts = exchange_cols(upstream_b, "dp")
    silu_z, dgate, grad_y = gate(normed, upstream_b, w_z, w_out)

    gated_b, prez_b, step_size, raw, peak, hist, last = scan_forward(
        summed, mixed_b, w_up, beta_bias, silu_z, dgate, skip_gain, states
    )

    def weight_grad(value, left):
        if blocked:
            far = swap(value, "dp", 2)
            pieces = (value, far, swap(value, "dp", 1), swap(far, "dp", 1))
            keep, send = out_weight(pieces, sides) if left else in_weight(sides, pieces)
            return keep + swap(send, "dp", 4).astype(F32)
        pieces = gather_tokens(value, "dp")
        pairs = zip(pieces, up_parts) if left else zip(norm_parts, pieces)
        return scatter_sum(sum(mm_tn(a, b) for a, b in pairs), "dp", 1 if left else 0)

    grad_wout = weight_grad(gated_b, True)
    grad_wz = weight_grad(prez_b, False)

    gmix, pay, ups = scan_backward(
        place, summed, mixed_b, w_up, step_size, raw, grad_y, hist, last, peak
    )
    grads = all_but_last(pay, "state")
    ups = lax.psum(ups, "dp")

    def over_state(send, keep):
        come = swap(send, "state", 1)
        last_come = swap((keep[1] + come[1].astype(F32)).astype(BF16), "state", 2)
        return keep[0] + come[0].astype(F32) + last_come.astype(F32)

    block_out = over_state(*branch(place, gated_b, w_out, tokens, parts)).astype(BF16)

    prex_b, down, rest = conv_back(
        place, summed, grads, mixed_b, grad_y, gmix, dsilu, pre_x, conv_weight, skip_gain,
        w_down, w_keyq,
    )
    down, rest = lax.psum((down, rest), "dp")
    grad_wx = weight_grad(prex_b, False)

    send, keep, stats, slope, shift, base = input_grad(
        place, group_ids, group_weights, prex_b, prez_b, w_x, w_z, tokens, cotangent, norm_gain,
        parts,
    )
    norm_grad = over_state(send, keep)
    stats = all_sum(stats, "state")
    row_stat = stats[: rows // LANES].reshape(rows, 1)
    grad_in = norm_grad * slope - shift * row_stat + base
    gain_rows = own_width // LANES
    own_gain = lax.dynamic_slice_in_dim(
        stats, rows // LANES + state_index * gain_rows, gain_rows, 0
    )
    grad_gain = all_sum(own_gain, "dp").reshape(-1)

    count = 2 * states
    rank = w_up.shape[0]
    return (
        block_out,
        grad_in,
        grad_gain,
        grad_wx,
        grad_wz,
        rest[count : count + taps],
        rest[count + taps],
        down,
        ups[:rank],
        ups[rank],
        rest[:count].T,
        rest[count + taps + 1],
        grad_wout,
        jnp.max(rest[count + taps + 2]),
    )


def solution(mesh):
    placed = (
        P("dp", None),
        P(),
        P(None, "state"),
        P(None, "state"),
        P(None, "state"),
        P("state"),
        P("state", None),
        P(None, "state"),
        P("state"),
        P("state", None),
        P("state"),
        P("state", None),
        P("dp", None),
        P("dp"),
        P(),
    )
    return jax.shard_map(
        per_device,
        mesh=mesh,
        in_specs=placed,
        out_specs=(
            P("dp", "state"),
            P("dp", "state"),
            P("state"),
            P("dp", "state"),
            P("dp", "state"),
            P(None, "state"),
            P("state"),
            P("state", None),
            P(None, "state"),
            P("state"),
            P("state", None),
            P("state"),
            P("state", "dp"),
            P(),
        ),
        check_vma=False,
    )
```

profile of v0, /device:TPU:0, one launch (start us, length us, event | category | flops | bytes accessed | tf_op | source)
XLA Modules:
  0.0 308.6 jit_solution(4091316517446818584)
XLA Ops:
  9.0 2.2 copy-done.2
  17.3 6.9 %front.1 = (bf16[256,2048]{1,0:T(8,128)(2,1)S(1)}, bf16[256,2048]{1,0:T(8,128)(2,1)S(1)}, f32[256,1024]{1,0:T(8,128)S(1)}, bf16[256,1024]{1,0:T(8,128)(2,1)S(1)}...) custom-call(s32[2]{0:T(128)S(1)} %pad_add_fusion.place, ...), custom_call_target="tpu_custom_call" | custom-call | tf_op jit(solution)/shard_map/front/pallas_call | solution.py:140
  25.8 2.9 collective-permute-start.1
  28.7 2.2 copy-done.5
  30.9 3.8 %gate.1 = (f32[256,1024]{1,0:T(8,128)S(1)}, f32[256,1024]{1,0:T(8,128)S(1)}, f32[256,1024]{1,0:T(8,128)S(1)}) custom-call(bf16[256,2048]{1,0:T(8,128)(2,1)S(1)} %get-tuple-element.55.normed, bf16[256,2048]{1,0:T(8,128)(2,1)S(1)} %get-tuple-element.56.up, bf16[2048,1024]{1,0:T(8,128)(2,1)S(1)} %copy-done.4, bf16[1024,2048]{1,0:T(8,128)(2,1)S(1)} %copy-done.5), custom_call_target="tpu_custom_call" | custom-call | flops 2147483648 | bytes 14680064 | tf_op jit(solution)/shard_map/gate/pallas_call | solution.py:199
  34.7 7.5 %scan.1 = (bf16[256,1024]{1,0:T(8,128)(2,1)S(1)}, bf16[256,1024]{1,0:T(8,128)(2,1)}, f32[256,1024]{1,0:T(8,128)S(1)}, f32[256,1024]{1,0:T(8,128)S(1)}, f32[8,128...) custom-call(f32[320,128]{1,0:T(8,128)S(1)} %add.70.one, ...), custom_call_target="tpu_custom_call" | custom-call | flops 251658240 | bytes 16777216 | tf_op jit(solution)/shard_map/scan/pallas_call | solution.py:302
  42.2 5.8 %copy-done = f32[256,16,8,128]{3,2,1,0:T(8,128)} copy-done((f32[256,16,8,128]{3,2,1,0:T(8,128)}, f32[256,16,8,128]{3,2,1,0:T(8,128)S(1)}, u32[]{:S(2)}) %copy-start) | copy-done | bytes 16777240
  48.8 5.8 %copy-done.1 = f32[256,16,8,128]{3,2,1,0:T(8,128)S(1)} copy-done((f32[256,16,8,128]{3,2,1,0:T(8,128)S(1)}, f32[256,16,8,128]{3,2,1,0:T(8,128)}, u32[]{:S(2)}) %copy-start.1) | copy-done | bytes 16777240
  54.6 17.4 %back.1 = (f32[256,1024]{1,0:T(8,128)S(1)}, f32[336,128]{1,0:T(8,128)S(1)}, f32[136,1024]{1,0:T(8,128)S(1)}) custom-call(s32[2]{0:T(128)S(1)} %pad_add_fusion.place, f32[320,128]{1,0:T(8,128)S(1)} %add.70.one, f32[320,128]{1,0:T(8,128)S(1)} %collective-permute-done.1.two, bf16[256,1024]{1,0:T(8,128)(2,1)S(1)} %get-tuple-element.54.mixed, ...), custom_call_target="tpu_custom_call" | custom-call | flops 251658240 | bytes 16777216 | tf_op jit(solution)/shard_map/back/pallas_call | solution.py:438
  73.0 1.4 collective-permute-done.4
  74.7 1.8 collective-permute-start.14
  76.5 4.4 %collective-permute-done.5.grad_two = f32[336,128]{1,0:T(8,128)S(1)} collective-permute-done((f32[336,128]{1,0:T(8,128)S(1)}, f32[336,128]{1,0:T(8,128)S(1)}, u32[]{:S(2)}, u32[]{:S(2)}) %collective-permute-start.5) | collective-permute-done | bytes 172064 | tf_op jit(solution)/shard_map/ppermute | solution.py:33
  80.9 3.5 %conv.1 = (bf16[256,1024]{1,0:T(8,128)(2,1)S(1)}, f32[1024,128]{1,0:T(8,128)S(1)}, f32[40,1024]{1,0:T(8,128)}) custom-call(s32[2]{0:T(128)S(1)} %pad_add_fusion.place, f32[320,128]{1,0:T(8,128)S(1)} %add.70.one, f32[320,128]{1,0:T(8,128)S(1)} %collective-permute-done.1.two, f32[336,128]{1,0:T(8,128)S(1)} %add.75.grad_one, ...), custom_call_target="tpu_custom_call" | custom-call | tf_op jit(solution)/shard_map/conv/pallas_call | solution.py:520
  85.2 6.5 %inputs.1 = (bf16[2,256,512]{2,1,0:T(8,128)(2,1)}, f32[2,256,512]{2,1,0:T(8,128)S(1)}, f32[18,128]{1,0:T(8,128)S(1)}, f32[256,512]{1,0:T(8,128)S(1)}, f32[256,512]{1,0:T(8,128)S(1)}, /*index=5*/f32[256,512]{1,0:T(8,128)S(1)}) custom-call(s32[2]{0:T(128)S(1)} %pad_add_fusion.place, s32[1]{0:T(128)S(6)} %copy.34.ids, f32[8]{0:T(128)S(1)} %copy-done.43, ...), custom_call_target="tpu_custom_call" | custom-call | flops 2147483648 | bytes 12582912 | tf_op jit(solution)/shard_map/inputs/pallas_call | solution.py:640
  95.1 1.6 collective-permute-start.13
  97.2 2.2 copy-done.6
  100.5 3.7 %branch.1 = (bf16[2,256,512]{2,1,0:T(8,128)(2,1)}, f32[2,256,512]{2,1,0:T(8,128)S(1)}) custom-call(s32[2]{0:T(128)S(1)} %pad_add_fusion.place, bf16[256,1024]{1,0:T(8,128)(2,1)S(1)} %copy-done.12, bf16[1024,2048]{1,0:T(8,128)(2,1)S(1)} %copy-done.6, bf16[256,2048]{1,0:T(8,128)(2,1)S(1)} %copy-done.8), custom_call_target="tpu_custom_call" | custom-call | flops 1073741824 | bytes 8388608 | tf_op jit(solution)/shard_map/branch/pallas_call | solution.py:558
  105.2 1.6 collective-permute-start.10
  108.9 1.2 collective-permute-start.11
  110.2 36.0 %collective-permute-done.11 = f32[4,128]{1,0:T(4,128)S(1)} collective-permute-done((f32[4,128]{1,0:T(4,128)S(1)}, f32[4,128]{1,0:T(4,128)S(1)}, u32[]{:S(2)}, u32[]{:S(2)}) %collective-permute-start.11) | collective-permute-done | bytes 2080 | tf_op jit(solution)/shard_map/ppermute | solution.py:33
  146.1 1.5 collective-permute-start.21
  147.7 2.4 collective-permute-start.12
  152.2 1.3 collective-permute-start.24
  155.9 7.5 %collective-permute-done.21.r2 = bf16[256,1024]{1,0:T(8,128)(2,1)S(1)} collective-permute-done((bf16[256,1024]{1,0:T(8,128)(2,1)}, bf16[256,1024]{1,0:T(8,128)(2,1)S(1)}, u32[]{:S(2)}, u32[]{:S(2)}) %collective-permute-start.21) | collective-permute-done | bytes 524320 | tf_op jit(solution)/shard_map/ppermute | solution.py:33
  163.8 1.7 collective-permute-start.7
  166.1 3.6 %collective-permute-done.24.l1 = bf16[256,1024]{1,0:T(8,128)(2,1)S(1)} collective-permute-done((bf16[256,1024]{1,0:T(8,128)(2,1)}, bf16[256,1024]{1,0:T(8,128)(2,1)S(1)}, u32[]{:S(2)}, u32[]{:S(2)}) %collective-permute-start.24) | collective-permute-done | bytes 524320 | tf_op jit(solution)/shard_map/ppermute | solution.py:33
  170.3 1.9 collective-permute-done.3
  172.2 1.4 collective-permute-start.17
  173.6 8.0 %collective-permute-done.16.r1 = bf16[256,1024]{1,0:T(8,128)(2,1)S(1)} collective-permute-done((bf16[256,1024]{1,0:T(8,128)(2,1)}, bf16[256,1024]{1,0:T(8,128)(2,1)S(1)}, u32[]{:S(2)}, u32[]{:S(2)}) %collective-permute-start.16) | collective-permute-done | bytes 524320 | tf_op jit(solution)/shard_map/ppermute | solution.py:33
  181.8 1.8 collective-permute-start.15
  183.9 1.9 fusion.3
  185.8 1.9 fusion.2
  187.7 38.7 %collective-permute-done.15.l3.r3 = bf16[256,1024]{1,0:T(8,128)(2,1)S(1)} collective-permute-done((bf16[256,1024]{1,0:T(8,128)(2,1)S(1)}, bf16[256,1024]{1,0:T(8,128)(2,1)S(1)}, u32[]{:S(2)}, u32[]{:S(2)}) %collective-permute-start.15) | collective-permute-done | bytes 524320 | tf_op jit(solution)/shard_map/ppermute | solution.py:33
  226.4 3.7 %inw.3 = (f32[256,1024]{1,0:T(8,128)S(1)}, bf16[256,1024]{1,0:T(8,128)(2,1)}) custom-call(bf16[256,1024]{1,0:T(8,128)(2,1)S(1)} %get-tuple-element.80.l0.r0, bf16[2,256,1024]{2,1,0:T(8,128)(2,1)S(1)} %collective-permute-done.13.l1.r1, bf16[256,1024]{1,0:T(8,128)(2,1)S(1)} %collective-permute-done.14.l2.r2, ...), custom_call_target="tpu_custom_call" | custom-call | flops 1073741824 | bytes 6291456 | tf_op jit(solution)/shard_map/inw/pallas_call | solution.py:731
  231.1 2.3 collective-permute-start.23
  233.4 3.0 outw.1
  238.0 1.8 inw.2
  240.7 2.3 collective-permute-start.19
  243.1 2.1 slice_reduce_fusion
  245.2 1.4 slice.74
  246.5 1.9 slice.76
  248.4 1.4 slice.77
  249.8 1.6 slice_bitcast_fusion.1
  251.4 27.2 %collective-permute-done.23 = bf16[256,1024]{1,0:T(8,128)(2,1)} collective-permute-done((bf16[256,1024]{1,0:T(8,128)(2,1)}, bf16[256,1024]{1,0:T(8,128)(2,1)}, u32[]{:S(2)}, u32[]{:S(2)}) %collective-permute-start.23) | collective-permute-done | bytes 524320 | tf_op jit(solution)/shard_map/ppermute | solution.py:33
  278.6 2.5 convert_add_fusion.1
  281.1 8.7 %collective-permute-done.27 = bf16[1024,256]{1,0:T(8,128)(2,1)} collective-permute-done((bf16[1024,256]{1,0:T(8,128)(2,1)}, bf16[1024,256]{1,0:T(8,128)(2,1)}, u32[]{:S(2)}, u32[]{:S(2)}) %collective-permute-start.27) | collective-permute-done | bytes 524320 | tf_op jit(solution)/shard_map/ppermute | solution.py:33
  289.8 2.1 convert_add_fusion
  291.9 7.9 %collective-permute-done.19 = bf16[256,1024]{1,0:T(8,128)(2,1)S(1)} collective-permute-done((bf16[256,1024]{1,0:T(8,128)(2,1)S(1)}, bf16[256,1024]{1,0:T(8,128)(2,1)S(1)}, u32[]{:S(2)}, u32[]{:S(2)}) %collective-permute-start.19) | collective-permute-done | bytes 524320 | tf_op jit(solution)/shard_map/ppermute | solution.py:33
  (136 shorter events, 31.6 us)
Async XLA Ops:
  7.2 235.9 %all-reduce.3.cloned.1.call-start = ((), (), s32[]{:S(2)}) async-start(), calls=%async_computation | async-start | bytes 2490368 | tf_op jit(solution)/shard_map/psum | solution.py:862
  17.3 11.4 %copy-start.4 = (bf16[2048,1024]{1,0:T(8,128)(2,1)S(1)}, bf16[2048,1024]{1,0:T(8,128)(2,1)}, u32[]{:S(2)}) copy-start(bf16[2048,1024]{1,0:T(8,128)(2,1)} %wz.3) | copy-start | bytes 12582916
  24.3 1.5 collective-permute-start
  25.8 8.9 %collective-permute-start.1 = (f32[320,128]{1,0:T(8,128)S(1)}, f32[320,128]{1,0:T(8,128)S(1)}, u32[]{:S(2)}, u32[]{:S(2)}) collective-permute-start(f32[320,128]{1,0:T(8,128)S(1)} %add.70.one), channel_id=1, source_target_pairs={{0,2},{1,3},{2,0},{3,1},{4,6},{5,7},{6,4},{7,5},{8,10},{9,11},{10,... | collective-permute-start | bytes 491528 | tf_op jit(solution)/shard_map/ppermute | solution.py:33
  42.2 5.8 %copy-start = (f32[256,16,8,128]{3,2,1,0:T(8,128)}, f32[256,16,8,128]{3,2,1,0:T(8,128)S(1)}, u32[]{:S(2)}) copy-start(f32[256,16,8,128]{3,2,1,0:T(8,128)S(1)} %get-tuple-element.65.hist) | copy-start | bytes 50331652
  54.6 26.3 %copy-start.26 = (bf16[1024,128]{1,0:T(8,128)(2,1)S(1)}, bf16[1024,128]{1,0:T(8,128)(2,1)}, u32[]{:S(2)}) copy-start(bf16[1024,128]{1,0:T(8,128)(2,1)} %wd.3) | copy-start | bytes 786436
  54.6 26.3 %copy-start.36 = (f32[4,1024]{1,0:T(4,128)S(1)}, f32[4,1024]{1,0:T(4,128)}, u32[]{:S(2)}) copy-start(f32[4,1024]{1,0:T(4,128)} %cw.3) | copy-start | bytes 49156
  72.9 12.3 %copy-start.3 = (bf16[2048,1024]{1,0:T(8,128)(2,1)S(1)}, bf16[2048,1024]{1,0:T(8,128)(2,1)}, u32[]{:S(2)}) copy-start(bf16[2048,1024]{1,0:T(8,128)(2,1)} %wx.3) | copy-start | bytes 12582916
  72.9 12.3 %copy-start.8 = (bf16[256,2048]{1,0:T(8,128)(2,1)S(1)}, bf16[256,2048]{1,0:T(8,128)(2,1)}, u32[]{:S(2)}) copy-start(bf16[256,2048]{1,0:T(8,128)(2,1)} %tok_own.1) | copy-start | bytes 3145732
  72.9 12.3 %copy-start.10 = (bf16[256,2048]{1,0:T(8,128)(2,1)S(1)}, bf16[256,2048]{1,0:T(8,128)(2,1)}, u32[]{:S(2)}) copy-start(bf16[256,2048]{1,0:T(8,128)(2,1)} %cot.3) | copy-start | bytes 3145732
  72.9 12.3 %copy-start.38 = (f32[2048]{0:T(1024)S(1)}, f32[2048]{0:T(1024)}, u32[]{:S(2)}) copy-start(f32[2048]{0:T(1024)} %param.16) | copy-start | bytes 24580
  72.9 12.3 %copy-start.43 = (f32[8]{0:T(128)S(1)}, f32[8]{0:T(128)}, u32[]{:S(2)}) copy-start(f32[8]{0:T(128)} %weights.3) | copy-start | bytes 100
  72.9 1.5 collective-permute-start.4
  74.4 6.5 %collective-permute-start.5 = (f32[336,128]{1,0:T(8,128)S(1)}, f32[336,128]{1,0:T(8,128)S(1)}, u32[]{:S(2)}, u32[]{:S(2)}) collective-permute-start(f32[336,128]{1,0:T(8,128)S(1)} %add.75.grad_one), channel_id=1, source_target_pairs={{0,2},{1,3},{2,0},{3,1},{4,6},{5,7},{6,4},{7,5},{8,10},{9,11},{10,... | collective-permute-start | bytes 516104 | tf_op jit(solution)/shard_map/ppermute | solution.py:33
  74.7 34.2 %collective-permute-start.14 = (bf16[256,1024]{1,0:T(8,128)(2,1)}, bf16[256,1024]{1,0:T(8,128)(2,1)S(1)}, u32[]{:S(2)}, u32[]{:S(2)}) collective-permute-start(bf16[256,1024]{1,0:T(8,128)(2,1)} %get-tuple-element.82), channel_id=1, source_target_pairs={{0,4},{4,0},{8,12},{12,8},{16,20},{20,16},{24,28},{28,24},{1,5},{5... | collective-permute-start | bytes 1572872 | tf_op jit(solution)/shard_map/ppermute | solution.py:33
  85.1 6.6 %copy-start.14 = (bf16[256,1024]{1,0:T(8,128)(2,1)}, bf16[256,1024]{1,0:T(8,128)(2,1)S(1)}, u32[]{:S(2)}) copy-start(bf16[256,1024]{1,0:T(8,128)(2,1)S(1)} %get-tuple-element.72.prex.r0) | copy-start | bytes 1572868
  95.1 1.6 collective-permute-start.8
  95.1 68.7 %collective-permute-start.13 = (bf16[2,256,1024]{2,1,0:T(8,128)(2,1)}, bf16[2,256,1024]{2,1,0:T(8,128)(2,1)S(1)}, u32[]{:S(2)}, u32[]{:S(2)}) collective-permute-start(bf16[2,256,1024]{2,1,0:T(8,128)(2,1)} %get-tuple-element.81), channel_id=1, source_target_pairs={{0,8},{4,12},{8,0},{12,4},{16,24},{20,28},{24,16},{28,20},{1,9},{5... | collective-permute-start | bytes 3145736 | tf_op jit(solution)/shard_map/ppermute | solution.py:33
  96.7 8.4 %collective-permute-start.9 = (f32[18,128]{1,0:T(8,128)S(1)}, f32[18,128]{1,0:T(8,128)S(1)}, u32[]{:S(2)}, u32[]{:S(2)}) collective-permute-start(f32[18,128]{1,0:T(8,128)S(1)} %add.80), channel_id=1, source_target_pairs={{0,2},{1,3},{2,0},{3,1},{4,6},{5,7},{6,4},{7,5},{8,10},{9,11},{10,... | collective-permute-start | bytes 27656 | tf_op jit(solution)/shard_map/ppermute | solution.py:33
  105.1 64.6 %copy-start.13 = (bf16[256,1024]{1,0:T(8,128)(2,1)S(1)}, bf16[256,1024]{1,0:T(8,128)(2,1)}, u32[]{:S(2)}) copy-start(bf16[256,1024]{1,0:T(8,128)(2,1)} %copy-done.11) | copy-start | bytes 1572868
  105.1 67.1 %copy-start.15 = (bf16[256,1024]{1,0:T(8,128)(2,1)S(1)}, bf16[256,1024]{1,0:T(8,128)(2,1)}, u32[]{:S(2)}) copy-start(bf16[256,1024]{1,0:T(8,128)(2,1)} %copy-done.14) | copy-start | bytes 1572868
  105.1 42.5 %collective-permute-start.2 = (bf16[2,256,512]{2,1,0:T(8,128)(2,1)}, bf16[2,256,512]{2,1,0:T(8,128)(2,1)}, u32[]{:S(2)}, u32[]{:S(2)}) collective-permute-start(bf16[2,256,512]{2,1,0:T(8,128)(2,1)} %get-tuple-element.61), channel_id=1, source_target_pairs={{0,1},{1,0},{2,3},{3,2},{4,5},{5,4},{6,7},{7,6},{8,9},{9,8},{10,11... | collective-permute-start | bytes 1572872 | tf_op jit(solution)/shard_map/ppermute | solution.py:33
  105.2 3.7 %collective-permute-start.10 = (f32[4,128]{1,0:T(4,128)S(1)}, f32[4,128]{1,0:T(4,128)S(1)}, u32[]{:S(2)}, u32[]{:S(2)}) collective-permute-start(f32[4,128]{1,0:T(4,128)S(1)} %constant_dynamic-slice_fusion), channel_id=1, source_target_pairs={{0,4},{4,0},{8,12},{12,8},{16,20},{20,16},{24,28},{28,24},{1,5},{5... | collective-permute-start | bytes 6152 | tf_op jit(solution)/shard_map/ppermute | solution.py:33
  106.8 46.8 %collective-permute-start.20 = (bf16[256,1024]{1,0:T(8,128)(2,1)}, bf16[256,1024]{1,0:T(8,128)(2,1)}, u32[]{:S(2)}, u32[]{:S(2)}) collective-permute-start(bf16[256,1024]{1,0:T(8,128)(2,1)} %get-tuple-element.73.prez.r0), channel_id=1, source_target_pairs={{0,8},{4,12},{8,0},{12,4},{16,24},{20,28},{24,16},{28,20},{1,9},{5... | collective-permute-start | bytes 1572872 | tf_op jit(solution)/shard_map/ppermute | solution.py:33
  108.8 45.4 %collective-permute-start.6 = (bf16[2,256,512]{2,1,0:T(8,128)(2,1)}, bf16[2,256,512]{2,1,0:T(8,128)(2,1)}, u32[]{:S(2)}, u32[]{:S(2)}) collective-permute-start(bf16[2,256,512]{2,1,0:T(8,128)(2,1)} %get-tuple-element.75), channel_id=1, source_target_pairs={{0,1},{1,0},{2,3},{3,2},{4,5},{5,4},{6,7},{7,6},{8,9},{9,8},{10,11... | collective-permute-start | bytes 1572872 | tf_op jit(solution)/shard_map/ppermute | solution.py:33
  108.9 37.3 %collective-permute-start.11 = (f32[4,128]{1,0:T(4,128)S(1)}, f32[4,128]{1,0:T(4,128)S(1)}, u32[]{:S(2)}, u32[]{:S(2)}) collective-permute-start(f32[4,128]{1,0:T(4,128)S(1)} %fusion.6), channel_id=1, source_target_pairs={{0,8},{4,12},{8,0},{12,4},{16,24},{20,28},{24,16},{28,20},{1,9},{5... | collective-permute-start | bytes 6152 | tf_op jit(solution)/shard_map/ppermute | solution.py:33
  110.1 75.7 %copy-start.24 = (f32[2,256,512]{2,1,0:T(8,128)S(1)}, f32[2,256,512]{2,1,0:T(8,128)}, u32[]{:S(2)}) copy-start(f32[2,256,512]{2,1,0:T(8,128)} %copy-done.23) | copy-start | bytes 3145732
  110.1 75.6 %copy-start.30 = (f32[256,512]{1,0:T(8,128)S(1)}, f32[256,512]{1,0:T(8,128)}, u32[]{:S(2)}) copy-start(f32[256,512]{1,0:T(8,128)} %copy-done.29) | copy-start | bytes 1572868
  110.1 75.6 %copy-start.32 = (f32[256,512]{1,0:T(8,128)S(1)}, f32[256,512]{1,0:T(8,128)}, u32[]{:S(2)}) copy-start(f32[256,512]{1,0:T(8,128)} %copy-done.31) | copy-start | bytes 1572868
  110.1 75.6 %copy-start.34 = (f32[256,512]{1,0:T(8,128)S(1)}, f32[256,512]{1,0:T(8,128)}, u32[]{:S(2)}) copy-start(f32[256,512]{1,0:T(8,128)} %copy-done.33) | copy-start | bytes 1572868
  146.1 17.3 %collective-permute-start.21 = (bf16[256,1024]{1,0:T(8,128)(2,1)}, bf16[256,1024]{1,0:T(8,128)(2,1)S(1)}, u32[]{:S(2)}, u32[]{:S(2)}) collective-permute-start(bf16[256,1024]{1,0:T(8,128)(2,1)} %get-tuple-element.73.prez.r0), channel_id=1, source_target_pairs={{0,4},{4,0},{8,12},{12,8},{16,20},{20,16},{24,28},{28,24},{1,5},{5... | collective-permute-start | bytes 1572872 | tf_op jit(solution)/shard_map/ppermute | solution.py:33
  147.7 4.5 %collective-permute-start.12 = (f32[4,128]{1,0:T(4,128)S(1)}, f32[4,128]{1,0:T(4,128)S(1)}, u32[]{:S(2)}, u32[]{:S(2)}) collective-permute-start(f32[4,128]{1,0:T(4,128)S(1)} %add.85), channel_id=1, source_target_pairs={{0,16},{4,20},{8,24},{12,28},{16,0},{20,4},{24,8},{28,12},{1,17},{... | collective-permute-start | bytes 6152 | tf_op jit(solution)/shard_map/ppermute | solution.py:33
  152.2 17.5 %collective-permute-start.24 = (bf16[256,1024]{1,0:T(8,128)(2,1)}, bf16[256,1024]{1,0:T(8,128)(2,1)S(1)}, u32[]{:S(2)}, u32[]{:S(2)}) collective-permute-start(bf16[256,1024]{1,0:T(8,128)(2,1)} %copy-done.11), channel_id=1, source_target_pairs={{0,8},{4,12},{8,0},{12,4},{16,24},{20,28},{24,16},{28,20},{1,9},{5... | collective-permute-start | bytes 1572872 | tf_op jit(solution)/shard_map/ppermute | solution.py:33
  153.5 28.1 %collective-permute-start.16 = (bf16[256,1024]{1,0:T(8,128)(2,1)}, bf16[256,1024]{1,0:T(8,128)(2,1)S(1)}, u32[]{:S(2)}, u32[]{:S(2)}) collective-permute-start(bf16[256,1024]{1,0:T(8,128)(2,1)} %copy-done.14), channel_id=1, source_target_pairs={{0,8},{4,12},{8,0},{12,4},{16,24},{20,28},{24,16},{28,20},{1,9},{5... | collective-permute-start | bytes 1572872 | tf_op jit(solution)/shard_map/ppermute | solution.py:33
  154.3 27.6 %collective-permute-start.22 = (bf16[256,1024]{1,0:T(8,128)(2,1)}, bf16[256,1024]{1,0:T(8,128)(2,1)S(1)}, u32[]{:S(2)}, u32[]{:S(2)}) collective-permute-start(bf16[256,1024]{1,0:T(8,128)(2,1)} %collective-permute-done.20.r1), channel_id=1, source_target_pairs={{0,4},{4,0},{8,12},{12,8},{16,20},{20,16},{24,28},{28,24},{1,5},{5... | collective-permute-start | bytes 1572872 | tf_op jit(solution)/shard_map/ppermute | solution.py:33
  163.5 8.7 %collective-permute-start.3 = (bf16[256,512]{1,0:T(8,128)(2,1)S(1)}, bf16[256,512]{1,0:T(8,128)(2,1)S(1)}, u32[]{:S(2)}, u32[]{:S(2)}) collective-permute-start(bf16[256,512]{1,0:T(8,128)(2,1)S(1)} %fusion.4), channel_id=1, source_target_pairs={{0,2},{1,3},{2,0},{3,1},{4,6},{5,7},{6,4},{7,5},{8,10},{9,11},{10,... | collective-permute-start | bytes 786440 | tf_op jit(solution)/shard_map/ppermute | solution.py:33
  163.8 19.8 %collective-permute-start.7 = (bf16[256,512]{1,0:T(8,128)(2,1)S(1)}, bf16[256,512]{1,0:T(8,128)(2,1)S(1)}, u32[]{:S(2)}, u32[]{:S(2)}) collective-permute-start(bf16[256,512]{1,0:T(8,128)(2,1)S(1)} %fusion.5), channel_id=1, source_target_pairs={{0,2},{1,3},{2,0},{3,1},{4,6},{5,7},{6,4},{7,5},{8,10},{9,11},{10,... | collective-permute-start | bytes 786440 | tf_op jit(solution)/shard_map/ppermute | solution.py:33
  169.8 63.7 %collective-permute-start.25 = (bf16[256,1024]{1,0:T(8,128)(2,1)S(1)}, bf16[256,1024]{1,0:T(8,128)(2,1)S(1)}, u32[]{:S(2)}, u32[]{:S(2)}) collective-permute-start(bf16[256,1024]{1,0:T(8,128)(2,1)S(1)} %copy-done.13), channel_id=1, source_target_pairs={{0,4},{4,0},{8,12},{12,8},{16,20},{20,16},{24,28},{28,24},{1,5},{5... | collective-permute-start | bytes 1572872 | tf_op jit(solution)/shard_map/ppermute | solution.py:33
  172.2 65.8 %collective-permute-start.17 = (bf16[256,1024]{1,0:T(8,128)(2,1)S(1)}, bf16[256,1024]{1,0:T(8,128)(2,1)S(1)}, u32[]{:S(2)}, u32[]{:S(2)}) collective-permute-start(bf16[256,1024]{1,0:T(8,128)(2,1)S(1)} %copy-done.15), channel_id=1, source_target_pairs={{0,4},{4,0},{8,12},{12,8},{16,20},{20,16},{24,28},{28,24},{1,5},{5... | collective-permute-start | bytes 1572872 | tf_op jit(solution)/shard_map/ppermute | solution.py:33
  181.6 51.8 %collective-permute-start.26 = (bf16[256,1024]{1,0:T(8,128)(2,1)S(1)}, bf16[256,1024]{1,0:T(8,128)(2,1)S(1)}, u32[]{:S(2)}, u32[]{:S(2)}) collective-permute-start(bf16[256,1024]{1,0:T(8,128)(2,1)S(1)} %collective-permute-done.24.l1), channel_id=1, source_target_pairs={{0,4},{4,0},{8,12},{12,8},{16,20},{20,16},{24,28},{28,24},{1,5},{5... | collective-permute-start | bytes 1572872 | tf_op jit(solution)/shard_map/ppermute | solution.py:33
  181.8 44.6 %collective-permute-start.15 = (bf16[256,1024]{1,0:T(8,128)(2,1)S(1)}, bf16[256,1024]{1,0:T(8,128)(2,1)S(1)}, u32[]{:S(2)}, u32[]{:S(2)}) collective-permute-start(bf16[256,1024]{1,0:T(8,128)(2,1)S(1)} %slice_bitcast_fusion), channel_id=1, source_target_pairs={{0,4},{4,0},{8,12},{12,8},{16,20},{20,16},{24,28},{28,24},{1,5},{5... | collective-permute-start | bytes 1572872 | tf_op jit(solution)/shard_map/ppermute | solution.py:33
  183.7 54.3 %collective-permute-start.18 = (bf16[256,1024]{1,0:T(8,128)(2,1)S(1)}, bf16[256,1024]{1,0:T(8,128)(2,1)S(1)}, u32[]{:S(2)}, u32[]{:S(2)}) collective-permute-start(bf16[256,1024]{1,0:T(8,128)(2,1)S(1)} %collective-permute-done.16.r1), channel_id=1, source_target_pairs={{0,4},{4,0},{8,12},{12,8},{16,20},{20,16},{24,28},{28,24},{1,5},{5... | collective-permute-start | bytes 1572872 | tf_op jit(solution)/shard_map/ppermute | solution.py:33
  231.1 47.5 %collective-permute-start.23 = (bf16[256,1024]{1,0:T(8,128)(2,1)}, bf16[256,1024]{1,0:T(8,128)(2,1)}, u32[]{:S(2)}, u32[]{:S(2)}) collective-permute-start(bf16[256,1024]{1,0:T(8,128)(2,1)} %get-tuple-element.86), channel_id=1, source_target_pairs={{0,16},{4,20},{8,24},{12,28},{16,0},{20,4},{24,8},{28,12},{1,17},{... | collective-permute-start | bytes 1572872 | tf_op jit(solution)/shard_map/ppermute | solution.py:33
  237.4 52.4 %collective-permute-start.27 = (bf16[1024,256]{1,0:T(8,128)(2,1)}, bf16[1024,256]{1,0:T(8,128)(2,1)}, u32[]{:S(2)}, u32[]{:S(2)}) collective-permute-start(bf16[1024,256]{1,0:T(8,128)(2,1)} %get-tuple-element.91), channel_id=1, source_target_pairs={{0,16},{4,20},{8,24},{12,28},{16,0},{20,4},{24,8},{28,12},{1,17},{... | collective-permute-start | bytes 1572872 | tf_op jit(solution)/shard_map/ppermute | solution.py:33
  240.7 49.1 %copy-start.20 = (f32[1024,256]{1,0:T(8,128)S(1)}, f32[1024,256]{1,0:T(8,128)}, u32[]{:S(2)}) copy-start(f32[1024,256]{1,0:T(8,128)} %copy-done.19) | copy-start | bytes 3145732
  240.7 59.1 %copy-start.22 = (f32[256,1024]{1,0:T(8,128)S(1)}, f32[256,1024]{1,0:T(8,128)}, u32[]{:S(2)}) copy-start(f32[256,1024]{1,0:T(8,128)} %copy-done.21) | copy-start | bytes 3145732
  240.7 59.1 %collective-permute-start.19 = (bf16[256,1024]{1,0:T(8,128)(2,1)S(1)}, bf16[256,1024]{1,0:T(8,128)(2,1)S(1)}, u32[]{:S(2)}, u32[]{:S(2)}) collective-permute-start(bf16[256,1024]{1,0:T(8,128)(2,1)S(1)} %get-tuple-element.84), channel_id=1, source_target_pairs={{0,16},{4,20},{8,24},{12,28},{16,0},{20,4},{24,8},{28,12},{1,17},{... | collective-permute-start | bytes 1572872 | tf_op jit(solution)/shard_map/ppermute | solution.py:33
  248.4 52.5 %copy-start.44 = (f32[1024,128]{1,0:T(8,128)S(1)}, f32[1024,128]{1,0:T(8,128)}, u32[]{:S(2)}) copy-start(f32[1024,128]{1,0:T(8,128)} %get-tuple-element.105) | copy-start | bytes 1572868
  (26 other events, 40.7 us)
Sparse Core Ops, SparseCore 0:
  110.2 102.3 all-reduce.2
where the time goes:
time: 310 us; the launch traced here: 309 us
  waiting for transfers between devices  148 us (48%)
  Pallas kernels  57.8 us (19%)
  local copies, waits for them, and re-layouts  43.2 us (14%)
  starting transfers between devices  29.7 us (10%)
  between operations  15 us (5%)
  other arithmetic  14.7 us (5%)
    ppermute x28, waiting for transfers between devices, swap(): return lax.ppermute(value, axis, [(i, i ^ bit) for i in range(size)])  148 us
    unnamed x92, local copies, waits for them, and re-layouts  36.9 us
    ppermute x28, starting transfers between devices, swap(): return lax.ppermute(value, axis, [(i, i ^ bit) for i in range(size)])  29.6 us
    pallas_call x1, Pallas kernels, scan_backward(): pl.pallas_call(functools.partial(back_kernel, unroll), in_specs=[pl.Block...  17.4 us
    pallas_call x1, Pallas kernels, scan_forward(): pl.pallas_call(functools.partial(scan_kernel, 4), in_specs=[WHOLE] * 8, o...  7.49 us
    pallas_call x1, Pallas kernels, front(): pl.pallas_call(functools.partial(front_kernel, blocked), grid=(inner // b...  6.95 us
    pallas_call x1, Pallas kernels, input_grad(): pl.pallas_call(input_kernel, grid_spec=pltpu.PrefetchScalarGridSpec(num_s...  6.53 us
  transfers between devices with their start and end apart: 29, of which 14 were waited for; matrix products, arithmetic and copies ran while one was open for 6% of the time, Pallas kernels for 8%

commit v1 on v0

--- a/solution.py
+++ b/solution.py
@@ -14,6 +14,8 @@
 BF16 = jnp.bfloat16
 MIB = 2**20
 WHOLE = pl.BlockSpec(memory_space=pltpu.VMEM)
+ANY = pl.BlockSpec(memory_space=pl.ANY)
+SMALL = 40
 
 
 def mm(left, right):
@@ -65,6 +67,10 @@
     for bit in bits[:-1]:
         value = value + swap(value, axis, bit)
     return value, swap(value, axis, bits[-1])
+
+
+def in_hbm(value):
+    return pltpu.with_memory_space_constraint(value, pltpu.HBM)
 
 
 def shifted(value, by, rows):
@@ -102,24 +108,23 @@
     mixed[...] = mix
     dsilu[...] = sig * (1.0 + conv * (1.0 - sig))
     part[:rows, :] += mm(mix, wd[...])
-    acc[...] += mm(mix, wk[...])
+    acc[...] += mm_nt(wk[...], mix)
 
     @pl.when(step == pl.num_programs(0) - 1)
     def _():
-        flat = jnp.transpose(acc[...])
-        wide = flat.shape[0]
+        wide = acc.shape[0]
         for c in range(rows // LANES):
-            part[rows + c * wide : rows + (c + 1) * wide, :] = flat[:, c * LANES : (c + 1) * LANES]
+            part[rows + c * wide : rows + (c + 1) * wide, :] = acc[:, c * LANES : (c + 1) * LANES]
         up[...] = (cot[...].astype(F32) * weights[ids[0]]).astype(BF16)
         if blocked:
-            far, near, own = rest[:3]
-            own_rows = width // blocked
+            far, near, own, up_far, up_own = rest[:5]
+            size = width // blocked
             for p in range(blocked):
-                from_cols = pl.ds(pl.multiple_of((place[0] ^ p) * own_rows, own_rows), own_rows)
+                cols = pl.ds(pl.multiple_of((place[0] ^ p) * size, size), size)
                 dest = far.at[p & 1] if p & 2 else (near if p & 1 else own)
-                for side, source in enumerate((normed, up)):
-                    first = (side * (blocked // 4) + p // 4) * own_rows
-                    dest[:, first : first + own_rows] = source[:, from_cols]
+                dest[:, (p // 4) * size : (p // 4 + 1) * size] = normed[:, cols]
+                at = (p & 1) * 2 + (p >> 1 & 1)
+                (up_far if p & 4 else up_own)[:, at * size : (at + 1) * size] = up[:, cols]
 
 
 def front(
@@ -128,15 +133,16 @@
 ):
     rows, width = tokens.shape
     inner = w_x.shape[1]
-    rank, kq = w_down.shape[1], w_keyq.shape[1]
+    rank, kq = w_down.shape[1], w_keyq.shape[0]
     blk = min(inner, 256)
     whole = lambda shape: pl.BlockSpec(shape, lambda i: (0,) * len(shape))
     cols = lambda height: pl.BlockSpec((height, blk), lambda i: (0, i))
-    down = lambda wide: pl.BlockSpec((blk, wide), lambda i: (i, 0))
     smem = pl.BlockSpec(memory_space=pltpu.SMEM)
     part_rows = rows + kq * rows // LANES
-    both = 2 * width // 4
-    shapes = [(2, rows, both), (rows, both), (rows, both)] if blocked else []
+    shapes = []
+    if blocked:
+        quarter, half = width // 4, width // 2
+        shapes = [(2, rows, quarter), (rows, quarter), (rows, quarter), (rows, half), (rows, half)]
     return pl.pallas_call(
         functools.partial(front_kernel, blocked),
         grid=(inner // blk,),
@@ -150,8 +156,8 @@
             cols(width),
             cols(conv_weight.shape[0]),
             cols(1),
-            down(rank),
-            down(kq),
+            pl.BlockSpec((blk, rank), lambda i: (i, 0)),
+            cols(kq),
         ],
         out_specs=[
             whole((rows, width)),
@@ -163,20 +169,21 @@
         ]
         + [whole(shape) for shape in shapes],
         out_shape=[
-            jax.ShapeDtypeStruct((rows, width), BF16),
-            jax.ShapeDtypeStruct((rows, width), BF16),
-            jax.ShapeDtypeStruct((rows, inner), F32),
-            jax.ShapeDtypeStruct((rows, inner), BF16),
-            jax.ShapeDtypeStruct((rows, inner), F32),
+            pltpu.HBM((rows, width), BF16),
+            pltpu.HBM((rows, width), BF16),
+            pltpu.HBM((rows, inner), F32),
+            pltpu.HBM((rows, inner), BF16),
+            pltpu.HBM((rows, inner), F32),
             jax.ShapeDtypeStruct((part_rows, LANES), F32),
         ]
-        + [jax.ShapeDtypeStruct(shape, BF16) for shape in shapes],
-        scratch_shapes=[pltpu.VMEM((rows, kq), F32)],
+        + [pltpu.HBM(shape, BF16) for shape in shapes],
+        scratch_shapes=[pltpu.VMEM((kq, rows), F32)],
         compiler_params=pltpu.CompilerParams(vmem_limit_bytes=26 * MIB),
         name="front",
     )(
-        place, group_ids, group_weights, tokens, cotangent, norm_gain[None], w_x,
-        conv_weight, conv_bias[None], w_down, w_keyq,
+        place, group_ids, group_weights, in_hbm(tokens), in_hbm(cotangent),
+        in_hbm(norm_gain[None]), in_hbm(w_x), in_hbm(conv_weight), in_hbm(conv_bias[None]),
+        in_hbm(w_down), in_hbm(w_keyq),
     )
 
 
@@ -208,11 +215,8 @@
         out_specs=[cols(rows)] * 3,
         out_shape=[jax.ShapeDtypeStruct((rows, inner), F32)] * 3,
         compiler_params=pltpu.CompilerParams(vmem_limit_bytes=24 * MIB),
-        cost_estimate=pl.CostEstimate(
-            flops=4 * rows * width * inner, bytes_accessed=14 * MIB, transcendentals=rows * inner
-        ),
         name="gate",
-    )(normed, upstream_b, w_z, w_out)
+    )(in_hbm(normed), in_hbm(upstream_b), in_hbm(w_z), in_hbm(w_out))
 
 
 def key_query_of(one, two, rows, count):
@@ -248,9 +252,10 @@
 
 def scan_kernel(
     unroll, one, two, mixed, wup, bias, silu, dgate, skip,
-    gated, prez, step_out, raw_out, peak, hist, last, step_t, mix_t, out_t, kb,
+    gated, prez, step_out, raw_out, peak, hist, last, step_t, mix_t, out_t, kb, slots, sems,
 ):
     rows, inner = mixed.shape
+    span = slots.shape[1]
     states = kb.shape[0] // rows // 2
     kq = key_query_of(one, two, rows, 2 * states)
     keys = kq[:, :states]
@@ -267,7 +272,8 @@
     lay_tiles(step_t, size)
     lay_tiles(mix_t, mixed[...].astype(F32))
 
-    def token(t, carried):
+    def token(block, i, carried):
+        t = block * span + i
         at = pl.ds(pl.multiple_of(t * SUB, SUB), SUB)
         size = step_t[at, :]
         mix = mix_t[at, :]
@@ -277,7 +283,7 @@
             key = pick(kb, rows, n, t)
             query = pick(kb, rows, states + n, t)
             state = carried[n]
-            hist[t, n] = state
+            slots[block % 2, i, n] = state
             state = state + (size * key) * (mix - key * state)
             term = query * state
             sums[n % 4] = term if sums[n % 4] is None else sums[n % 4] + term
@@ -286,7 +292,18 @@
         return tuple(following)
 
     zero = jnp.zeros((SUB, LANES), F32)
-    final = lax.fori_loop(0, rows, token, (zero,) * states, unroll=unroll)
+    final = (zero,) * states
+    copies = []
+    for block in range(rows // span):
+        if block >= 2:
+            copies[block - 2].wait()
+        final = lax.fori_loop(0, span, functools.partial(token, block), final, unroll=unroll)
+        copies.append(
+            pltpu.make_async_copy(
+                slots.at[block % 2], hist.at[pl.ds(block * span, span)], sems.at[block % 2]
+            )
+        )
+        copies[-1].start()
     for n in range(states):
         last[n] = final[n]
     for j in range(SUB):
@@ -294,6 +311,8 @@
         y = lay_rows(out_t, rows, j) + skip[:, at] * mixed[:, at].astype(F32)
         gated[:, at] = (y * silu[:, at]).astype(BF16)
         prez[:, at] = (y * dgate[:, at]).astype(BF16)
+    for copy in copies[-2:]:
+        copy.wait()
 
 
 def scan_forward(summed, mixed, w_up, beta_bias, silu, dgate, skip_gain, states):
@@ -302,34 +321,46 @@
     return pl.pallas_call(
         functools.partial(scan_kernel, 4),
         in_specs=[WHOLE] * 8,
-        out_specs=[WHOLE] * 7,
+        out_specs=[WHOLE] * 5 + [pl.BlockSpec(memory_space=pl.ANY), WHOLE],
         out_shape=[
-            full(BF16),
-            full(BF16),
+            pltpu.HBM((rows, inner), BF16),
+            pltpu.HBM((rows, inner), BF16),
             full(F32),
             full(F32),
             jax.ShapeDtypeStruct((SUB, LANES), F32),
-            pltpu.VMEM((rows, states, SUB, LANES), F32),
+            pltpu.HBM((rows, states, SUB, LANES), F32),
             jax.ShapeDtypeStruct((states, SUB, LANES), F32),
         ],
         scratch_shapes=[pltpu.VMEM((rows * SUB, LANES), F32)] * 3
-        + [pltpu.VMEM((2 * states * rows, LANES), F32)],
+        + [
+            pltpu.VMEM((2 * states * rows, LANES), F32),
+            pltpu.VMEM((2, rows // 8, states, SUB, LANES), F32),
+            pltpu.SemaphoreType.DMA((2,)),
+        ],
         compiler_params=pltpu.CompilerParams(vmem_limit_bytes=22 * MIB),
-        cost_estimate=pl.CostEstimate(
-            flops=60 * rows * inner * states, bytes_accessed=16 * MIB, transcendentals=0
-        ),
         name="scan",
-    )(*summed, mixed, w_up, beta_bias[None], silu, dgate, skip_gain[None])
+    )(*summed, mixed, in_hbm(w_up), in_hbm(beta_bias[None]), silu, dgate, in_hbm(skip_gain[None]))
 
 
 def back_kernel(
-    unroll, place, one, two, mixed, wup, step_in, raw_in, gy, hist, last, peak,
-    gmix, pay, ups, preb, step_t, mix_t, gs_t, kb, sum_d, sum_s, prods, zk, zq,
-):
+    unroll, pins, place, one, two, mixed, wup, step_in, raw_in, gy, hist, last, peak, *rest, ):
+    gmix, pay, ups, preb, step_t, mix_t, gs_t, kb, sum_d, sum_s, prods, zk, zq, slots, sems = rest[
+        pins:
+    ]
     rows, inner = mixed.shape
     states = last.shape[0]
     rank = wup.shape[0]
     span = zk.shape[0] // states
+    chunk = slots.shape[1]
+    chunks = rows // chunk
+
+    def fetch(block):
+        return pltpu.make_async_copy(
+            hist.at[pl.ds(block * chunk, chunk)], slots.at[block % 2], sems.at[block % 2]
+        )
+
+    fetch(chunks - 1).start()
+    fetch(chunks - 2).start()
     kq = key_query_of(one, two, rows, 2 * states)
     keys = kq[:, :states]
     norm = jnp.sum(keys * keys, axis=1, keepdims=True)
@@ -353,7 +384,8 @@
     tail = gs_t[pl.ds(rows * SUB, SUB), :]
     reduce_to(zq, rows, [last[n] * tail for n in range(states)], 0)
 
-    def token(t, u, carried):
+    def token(block, i, u, carried):
+        t = block * chunk + i
         at = pl.ds(pl.multiple_of(t * SUB, SUB), SUB)
         size = step_t[at, :]
         half = mix_t[at, :]
@@ -365,7 +397,7 @@
         for n in range(states):
             key = pick(kb, rows, n, t)
             query = pick(kb, rows, states + n, t)
-            state = hist[t, n]
+            state = slots[block % 2, i, n]
             full = query * grad + carried[n]
             by_key = full * key
             by_state = by_key * state
@@ -373,22 +405,27 @@
             following.append(full - key * (size * by_key))
             for_key.append(full * drive - size * by_state)
             for_query.append(state * before)
-            i = n % 2
-            total_d[i] = by_key if total_d[i] is None else total_d[i] + by_key
-            total_s[i] = term if total_s[i] is None else total_s[i] + term
+            h = n % 2
+            total_d[h] = by_key if total_d[h] is None else total_d[h] + by_key
+            total_s[h] = term if total_s[h] is None else total_s[h] + term
         sum_d[at, :] = total_d[0] + total_d[1]
         sum_s[at, :] = total_s[0] + total_s[1]
         reduce_to(zk, t, for_key, 2 * u)
         reduce_to(zq, t, for_query, 2 * u + 1)
         return tuple(following)
 
-    def some(i, carried):
+    def some(block, i, carried):
         for u in range(unroll):
-            carried = token(rows - 1 - (i * unroll + u), u, carried)
+            carried = token(block, chunk - 1 - (i * unroll + u), u, carried)
         return carried
 
     zero = jnp.zeros((SUB, LANES), F32)
-    lax.fori_loop(0, rows // unroll, some, (zero,) * states)
+    carried = (zero,) * states
+    for block in reversed(range(chunks)):
+        fetch(block).wait()
+        carried = lax.fori_loop(0, chunk // unroll, functools.partial(some, block), carried)
+        if block >= 2:
+            fetch(block - 2).start()
 
     total_norm = jnp.zeros((rows, 1), F32)
     for j in range(SUB):
@@ -428,7 +465,7 @@
         pay[rows + c * high : rows + (c + 1) * high, :] = flat[:high, c * LANES : (c + 1) * LANES]
 
 
-def scan_backward(place, summed, mixed, w_up, step_in, raw, gy, hist, last, peak):
+def scan_backward(place, summed, mixed, w_up, step_in, raw, gy, hist, last, peak, pins):
     rows, inner = mixed.shape
     states = last.shape[0]
     unroll = 2
@@ -436,13 +473,17 @@
     high = 2 * states + SUB
     pay_rows = rows + high * rows // LANES
     return pl.pallas_call(
-        functools.partial(back_kernel, unroll),
-        in_specs=[pl.BlockSpec(memory_space=pltpu.SMEM)] + [WHOLE] * 10,
+        functools.partial(back_kernel, unroll, len(pins)),
+        in_specs=[pl.BlockSpec(memory_space=pltpu.SMEM)]
+        + [WHOLE] * 7
+        + [ANY]
+        + [WHOLE] * 2
+        + [ANY] * len(pins),
         out_specs=[WHOLE] * 3,
         out_shape=[
-            jax.ShapeDtypeStruct((rows, inner), F32),
+            pltpu.HBM((rows, inner), F32),
             jax.ShapeDtypeStruct((pay_rows, LANES), F32),
-            jax.ShapeDtypeStruct((w_up.shape[0] + SUB, inner), F32),
+            pltpu.HBM((w_up.shape[0] + SUB, inner), F32),
         ],
         scratch_shapes=[
             pltpu.VMEM((rows, inner), BF16),
@@ -455,41 +496,47 @@
             pltpu.VMEM((unroll * 2 * states * SUB, LANES), F32),
             pltpu.VMEM((states * span, LANES), F32),
             pltpu.VMEM((states * span, LANES), F32),
+            pltpu.VMEM((2, rows // 8, states, SUB, LANES), F32),
+            pltpu.SemaphoreType.DMA((2,)),
         ],
         compiler_params=pltpu.CompilerParams(vmem_limit_bytes=28 * MIB),
-        cost_estimate=pl.CostEstimate(
-            flops=60 * rows * inner * states, bytes_accessed=16 * MIB, transcendentals=0
-        ),
         name="back",
     )(
-        place, *summed, mixed, w_up, step_in, raw, gy,
-        pltpu.with_memory_space_constraint(hist, pltpu.VMEM), last, peak,
+        place, *summed, mixed, in_hbm(w_up), step_in, raw, gy,
+        in_hbm(hist), last, peak, *pins,
     )
 
 
 def conv_kernel(
-    place, one, two, grad_one, grad_two, mixed, gy, gmix, dsilu, prex, cw, skip, wd, wk,
-    prex_b, down, rest,
+    pins, parts, place, one, two, grad_one, grad_two, mixed, gy, gmix, dsilu, prex, ups, cw, skip,
+    wd, wk, *rest,
 ):
+    prex_b, keep, send, table = rest[pins:]
     rows, inner = mixed.shape
-    count = wk.shape[1]
+    rank = wd.shape[1]
+    count = wk.shape[0]
     states = count // 2
     high = (grad_one.shape[0] - rows) * LANES // rows
     kq = key_query_of(one, two, rows, count)
     gkq = key_query_of(grad_one, grad_two, rows, high)
     norm_grad = gkq[:, count : count + 1]
     peak = jnp.max(gkq[:, count + 1 : count + 2], axis=0, keepdims=True)
+    peak_high = peak.astype(BF16).astype(F32)
     lane = lax.broadcasted_iota(jnp.int32, (rows, count), 1)
     kq_b = (gkq[:, :count] + jnp.where(lane < states, 2.0 * kq * norm_grad, 0.0)).astype(BF16)
     rank_b = (grad_one[:rows, :] + grad_two[:rows, :]).astype(BF16)
     taps = cw.shape[0]
     blk = 256
+    first = 2 * rank + count
+    table[:rank, :] = ups[:rank, :]
+    table[rank : 2 * rank, :] = mm_tn(rank_b, mixed[...])
+    table[2 * rank : first, :] = mm_tn(kq_b, mixed[...])
     for c in range(inner // blk):
         at = slice(c * blk, (c + 1) * blk)
         mix = mixed[:, at].astype(F32)
         grad_y = gy[:, at]
         total = grad_y * skip[:, at] + gmix[:, at]
-        total = total + mm_nt(kq_b, wk[at, :]) + mm_nt(rank_b, wd[at, :])
+        total = total + mm(kq_b, wk[:, at]) + mm_nt(rank_b, wd[at, :])
         grad = total * dsilu[:, at]
         pre = prex[:, at]
         row = lax.broadcasted_iota(jnp.int32, grad.shape, 0)
@@ -502,36 +549,80 @@
             out = term if out is None else out + term
         sums.append(jnp.sum(grad, axis=0, keepdims=True))
         sums.append(jnp.sum(grad_y * mix, axis=0, keepdims=True))
+        sums.append(ups[rank : rank + 1, at])
         channel = lax.broadcasted_iota(jnp.int32, (1, blk), 1) + c * blk
-        sums.append(jnp.where(channel == place[0], jnp.broadcast_to(peak, (1, blk)), 0.0))
+        for value in (peak_high, peak - peak_high):
+            sums.append(jnp.where(channel == place[0], jnp.broadcast_to(value, (1, blk)), 0.0))
         for i, line in enumerate(sums):
-            rest[count + i : count + i + 1, at] = line
+            table[first + i : first + i + 1, at] = line
         prex_b[:, at] = out.astype(BF16)
-    for i in range(len(sums), SUB):
-        rest[count + i : count + i + 1, :] = jnp.zeros((1, inner), F32)
-    down[...] = mm_tn(mixed[...], rank_b)
-    rest[:count, :] = mm_tn(kq_b, mixed[...])
+    table[first + len(sums) :, :] = jnp.zeros((table.shape[0] - first - len(sums), inner), F32)
+    size = table.shape[0] // parts
+    if parts != 8:
+        keep[...] = table[...]
+        return
+    for dest, order in ((keep, (0, 4, 2, 6)), (send, (1, 5, 3, 7))):
+        for i, p in enumerate(order):
+            at = pl.ds(pl.multiple_of((place[0] ^ p) * size, SUB), size)
+            dest[i] = table[at, :].astype(dest.dtype)
 
 
 def conv_back(
-    place, summed, grads, mixed, gy, gmix, dsilu, prex, conv_weight, skip_gain, w_down, w_keyq
+    place, summed, grads, mixed, gy, gmix, dsilu, prex, ups, conv_weight, skip_gain, w_down,
+    w_keyq, parts, pins,
 ):
     rows, inner = mixed.shape
+    table = (8 * SMALL, inner)
+    half = (4, SMALL, inner) if parts == 8 else table
     return pl.pallas_call(
-        conv_kernel,
-        in_specs=[pl.BlockSpec(memory_space=pltpu.SMEM)] + [WHOLE] * 13,
+        functools.partial(conv_kernel, len(pins), parts),
+        in_specs=[pl.BlockSpec(memory_space=pltpu.SMEM)] + [WHOLE] * 14 + [ANY] * len(pins),
         out_specs=[WHOLE] * 3,
         out_shape=[
-            jax.ShapeDtypeStruct((rows, inner), BF16),
-            jax.ShapeDtypeStruct((inner, w_down.shape[1]), F32),
-            jax.ShapeDtypeStruct((w_keyq.shape[1] + SUB, inner), F32),
+            pltpu.HBM((rows, inner), BF16),
+            pltpu.HBM(half, F32),
+            pltpu.HBM(half, BF16),
         ],
-        compiler_params=pltpu.CompilerParams(vmem_limit_bytes=24 * MIB),
+        scratch_shapes=[pltpu.VMEM(table, F32)],
+        compiler_params=pltpu.CompilerParams(vmem_limit_bytes=26 * MIB),
         name="conv",
     )(
-        place, *summed, *grads, mixed, gy, gmix, dsilu, prex, conv_weight, skip_gain[None],
-        w_down, w_keyq,
-    )
+        place, *summed, *grads, mixed, gy, gmix, dsilu, prex, ups, in_hbm(conv_weight),
+        in_hbm(skip_gain[None]), in_hbm(w_down), in_hbm(w_keyq), *pins,
+    )
+
+
+def unpack_kernel(place, rank, count, taps, g0, g1, g2, g3, up, down, keyq, lines, table):
+    size = g0.shape[0]
+    pieces = [(0, g0, 0), (4, g1, 0), (2, g2, 0), (6, g2, 1)]
+    pieces += [(p, g3, i) for i, p in enumerate((1, 5, 3, 7))]
+    for p, source, i in pieces:
+        at = pl.ds(pl.multiple_of((place[0] ^ p) * size, SUB), size)
+        table[at, :] = source[i * size : (i + 1) * size, :].astype(F32)
+    up[...] = table[:rank, :]
+    down[...] = jnp.transpose(table[rank : 2 * rank, :])
+    keyq[...] = table[2 * rank : 2 * rank + count, :]
+    first = 2 * rank + count
+    lines[...] = table[first : first + lines.shape[0], :]
+
+
+def unpack(place, pieces, rank, count, taps):
+    inner = pieces[0].shape[1]
+    kernel = lambda place, *refs: unpack_kernel(place, rank, count, taps, *refs)
+    return pl.pallas_call(
+        kernel,
+        in_specs=[pl.BlockSpec(memory_space=pltpu.SMEM)] + [WHOLE] * 4,
+        out_specs=[WHOLE] * 4,
+        out_shape=[
+            jax.ShapeDtypeStruct((rank, inner), F32),
+            jax.ShapeDtypeStruct((inner, rank), F32),
+            jax.ShapeDtypeStruct((count, inner), F32),
+            jax.ShapeDtypeStruct((2 * SUB, inner), F32),
+        ],
+        scratch_shapes=[pltpu.VMEM((8 * SMALL, inner), F32)],
+        compiler_params=pltpu.CompilerParams(vmem_limit_bytes=16 * MIB),
+        name="unpack",
+    )(place, *pieces)
 
 
 def branch_kernel(place, gated, wo, tok, send, keep):
@@ -548,7 +639,7 @@
 
     @pl.when(i % 2 == 1)
     def _():
-        send[0] = value.astype(BF16)
+        send[0, 0] = value.astype(BF16)
 
 
 def branch(place, gated, w_out, tokens, parts):
@@ -565,22 +656,22 @@
                 pl.BlockSpec((inner, own), lambda i, place: (0, place[1] ^ i)),
                 pl.BlockSpec((rows, own), lambda i, place: (0, place[1])),
             ],
-            out_specs=[pl.BlockSpec((1, rows, own), lambda i, place: (i // 2, 0, 0))] * 2,
+            out_specs=[
+                pl.BlockSpec((1, 1, rows, own), lambda i, place: (i // 2, 0, 0, 0)),
+                pl.BlockSpec((1, rows, own), lambda i, place: (i // 2, 0, 0)),
+            ],
         ),
         out_shape=[
-            jax.ShapeDtypeStruct((parts // 2, rows, own), BF16),
-            jax.ShapeDtypeStruct((parts // 2, rows, own), F32),
+            pltpu.HBM((parts // 2, 2, rows, own), BF16),
+            pltpu.HBM((parts // 2, rows, own), F32),
         ],
         compiler_params=pltpu.CompilerParams(vmem_limit_bytes=16 * MIB),
-        cost_estimate=pl.CostEstimate(
-            flops=2 * rows * inner * width, bytes_accessed=8 * MIB, transcendentals=0
-        ),
         name="branch",
-    )(place, gated, w_out, tokens)
+    )(place, in_hbm(gated), in_hbm(w_out), in_hbm(tokens))
 
 
 def input_kernel(
-    place, ids, weights, prex, prez, wx, wz, tok, tok_own, cot, gain,
+    place, ids, weights, half_sent, prex, prez, wx, wz, tok, tok_own, cot, gain,
     send, keep, stats, slope, shift, base, inv, dots,
 ):
     i = pl.program_id(0)
@@ -617,7 +708,7 @@
 
     @pl.when(i % 2 == 1)
     def _():
-        send[0] = value.astype(BF16)
+        send[0, 0] = value.astype(BF16)
 
     @pl.when(i == pl.num_programs(0) - 1)
     def _():
@@ -627,7 +718,8 @@
 
 
 def input_grad(
-    place, group_ids, group_weights, prex, prez, w_x, w_z, tokens, cotangent, norm_gain, parts
+    place, group_ids, group_weights, half_sent, prex, prez, w_x, w_z, tokens, cotangent, norm_gain,
+    parts,
 ):
     rows, inner = prex.shape
     width = tokens.shape[1]
@@ -645,6 +737,7 @@
             in_specs=[
                 smem,
                 smem,
+                ANY,
                 whole((rows, inner)),
                 whole((rows, inner)),
                 part,
@@ -654,57 +747,58 @@
                 pl.BlockSpec((rows, own), lambda i, place: (0, place[1])),
                 pl.BlockSpec((1, own), lambda i, place: (0, place[1] ^ i)),
             ],
-            out_specs=[pl.BlockSpec((1, rows, own), lambda i, place: (i // 2, 0, 0))] * 2
+            out_specs=[
+                pl.BlockSpec((1, 1, rows, own), lambda i, place: (i // 2, 1, 0, 0)),
+                pl.BlockSpec((1, rows, own), lambda i, place: (i // 2, 0, 0)),
+            ]
             + [whole((stat_rows, LANES)), mine, mine, mine],
             scratch_shapes=[pltpu.VMEM((rows, LANES), F32)] * 2,
         ),
         out_shape=[
-            jax.ShapeDtypeStruct((parts // 2, rows, own), BF16),
-            jax.ShapeDtypeStruct((parts // 2, rows, own), F32),
+            pltpu.HBM((parts // 2, 2, rows, own), BF16),
+            pltpu.HBM((parts // 2, rows, own), F32),
             jax.ShapeDtypeStruct((stat_rows, LANES), F32),
         ]
-        + [jax.ShapeDtypeStruct((rows, own), F32)] * 3,
+        + [pltpu.HBM((rows, own), F32)] * 3,
         compiler_params=pltpu.CompilerParams(vmem_limit_bytes=24 * MIB),
-        cost_estimate=pl.CostEstimate(
-            flops=4 * rows * inner * width, bytes_accessed=12 * MIB, transcendentals=0
-        ),
+        input_output_aliases={3: 0},
         name="inputs",
     )(
-        place, group_ids, group_weights, prex, prez, w_x, w_z, tokens, tokens, cotangent,
-        norm_gain[None],
-    )
-
-
-def out_weight_kernel(l0, l1, l2, l3, r0, r1, r2, r3, keep, send):
+        place, group_ids, group_weights, in_hbm(half_sent), in_hbm(prex), in_hbm(prez), in_hbm(w_x), in_hbm(w_z), in_hbm(tokens),
+        in_hbm(tokens), in_hbm(cotangent), in_hbm(norm_gain[None]),
+    )
+
+
+def out_weight_kernel(pins, l0, l1, r0, r1, *rest):
+    keep, later, send = rest[pins:]
     own = keep.shape[1]
-    total = None
-    for left, right in ((l0, r0[:, 2 * own :]), (l1, r1[0, :, 2 * own :]), (l2, r2[:, 2 * own :]), (l3, r3[:, 2 * own :])):
-        term = mm_tn(left[...], right)
-        total = term if total is None else total + term
+    total = mm_tn(l0[...], r0[...]) + mm_tn(l1[...], r1[...])
     keep[...] = total[:, :own]
-    send[...] = total[:, own:].astype(BF16)
-
-
-def out_weight(lefts, rights):
+    later[...] = total[:, own : 2 * own]
+    send[...] = total[:, 2 * own :].astype(BF16)
+
+
+def out_weight(lefts, rights, pins):
     rows, inner = lefts[0].shape
     own = rights[0].shape[1] // 4
     blk = 256
     whole = lambda value: pl.BlockSpec(value.shape, lambda i: (0,) * value.ndim)
+    down = lambda wide: pl.BlockSpec((blk, wide), lambda i: (i, 0))
     return pl.pallas_call(
-        out_weight_kernel,
+        functools.partial(out_weight_kernel, len(pins)),
         grid=(inner // blk,),
-        in_specs=[pl.BlockSpec((rows, blk), lambda i: (0, i))] * 4 + [whole(r) for r in rights],
-        out_specs=[pl.BlockSpec((blk, own), lambda i: (i, 0))] * 2,
+        in_specs=[pl.BlockSpec((rows, blk), lambda i: (0, i))] * 2
+        + [whole(r) for r in rights]
+        + [ANY] * len(pins),
+        out_specs=[down(own), down(own), down(2 * own)],
         out_shape=[
-            jax.ShapeDtypeStruct((inner, own), F32),
-            jax.ShapeDtypeStruct((inner, own), BF16),
+            pltpu.HBM((inner, own), F32),
+            pltpu.HBM((inner, own), F32),
+            pltpu.HBM((inner, 2 * own), BF16),
         ],
         compiler_params=pltpu.CompilerParams(vmem_limit_bytes=20 * MIB),
-        cost_estimate=pl.CostEstimate(
-            flops=16 * rows * inner * own, bytes_accessed=6 * MIB, transcendentals=0
-        ),
         name="outw",
-    )(*lefts, *rights)
+    )(*[in_hbm(value) for value in (*lefts, *rights)], *pins)
 
 
 def in_weight_kernel(l0, l1, l2, l3, r0, r1, r2, r3, keep, send):
@@ -725,7 +819,7 @@
 
 def in_weight(lefts, rights):
     rows, inner = rights[0].shape
-    own = lefts[0].shape[1] // 4
+    own = lefts[0].shape[1] // 2
     whole = lambda value: pl.BlockSpec(value.shape, lambda i: (0,) * value.ndim)
     side = pl.BlockSpec((rows, own), lambda i: (0, 1 - i))
     return pl.pallas_call(
@@ -735,15 +829,12 @@
         + [whole(r) for r in rights],
         out_specs=[pl.BlockSpec((own, inner), lambda i: (0, 0))] * 2,
         out_shape=[
-            jax.ShapeDtypeStruct((own, inner), F32),
-            jax.ShapeDtypeStruct((own, inner), BF16),
+            pltpu.HBM((own, inner), F32),
+            pltpu.HBM((own, inner), BF16),
         ],
         compiler_params=pltpu.CompilerParams(vmem_limit_bytes=20 * MIB),
-        cost_estimate=pl.CostEstimate(
-            flops=16 * rows * inner * own, bytes_accessed=6 * MIB, transcendentals=0
-        ),
         name="inw",
-    )(*lefts, *rights)
+    )(*[in_hbm(value) for value in (*lefts, *rights)])
 
 
 def split_bits(axis):
@@ -810,16 +901,20 @@
     state_index = lax.axis_index("state")
     place = jnp.stack([lax.axis_index("dp"), state_index]).astype(jnp.int32)
     blocked = dp_size if dp_size == 8 and width % (8 * LANES) == 0 else 0
+    keyq_t = w_keyq.T
 
     normed, upstream_b, pre_x, mixed_b, dsilu, part, *blocks = front(
         place, group_ids, group_weights, tokens, cotangent, norm_gain, w_x,
-        conv_weight, conv_bias, w_down, w_keyq, blocked,
+        conv_weight, conv_bias, w_down, keyq_t, blocked,
     )
     summed = all_but_last(part, "state")
+    pins_back = pins_conv = ()
     if blocked:
-        far, near, own = blocks
+        far, near, own, up_far, up_own = blocks
         far = swap(far, "dp", 2)
-        sides = (own, far, swap(near, "dp", 1), swap(far[1], "dp", 1))
+        near = swap(near, "dp", 1)
+        up_far = swap(up_far, "dp", 4)
+        pins_back = (far, near)
     else:
         norm_parts = exchange_cols(normed, "dp")
         up_parts = exchange_cols(upstream_b, "dp")
@@ -828,71 +923,109 @@
     gated_b, prez_b, step_size, raw, peak, hist, last = scan_forward(
         summed, mixed_b, w_up, beta_bias, silu_z, dgate, skip_gain, states
     )
-
-    def weight_grad(value, left):
-        if blocked:
-            far = swap(value, "dp", 2)
-            pieces = (value, far, swap(value, "dp", 1), swap(far, "dp", 1))
-            keep, send = out_weight(pieces, sides) if left else in_weight(sides, pieces)
-            return keep + swap(send, "dp", 4).astype(F32)
-        pieces = gather_tokens(value, "dp")
-        pairs = zip(pieces, up_parts) if left else zip(norm_parts, pieces)
-        return scatter_sum(sum(mm_tn(a, b) for a, b in pairs), "dp", 1 if left else 0)
-
-    grad_wout = weight_grad(gated_b, True)
-    grad_wz = weight_grad(prez_b, False)
+    if blocked:
+        gated_far = swap(gated_b, "dp", 4)
+        prez_far = swap(prez_b, "dp", 2)
+        prez_near = swap(prez_b, "dp", 1)
+        sides = (own, far, near, swap(far[1], "dp", 1))
+        pins_conv = (gated_far, prez_far, prez_near, up_far, sides[3])
 
     gmix, pay, ups = scan_backward(
-        place, summed, mixed_b, w_up, step_size, raw, grad_y, hist, last, peak
+        place, summed, mixed_b, w_up, step_size, raw, grad_y, hist, last, peak, pins_back
     )
     grads = all_but_last(pay, "state")
-    ups = lax.psum(ups, "dp")
-
-    def over_state(send, keep):
-        come = swap(send, "state", 1)
-        last_come = swap((keep[1] + come[1].astype(F32)).astype(BF16), "state", 2)
-        return keep[0] + come[0].astype(F32) + last_come.astype(F32)
-
-    block_out = over_state(*branch(place, gated_b, w_out, tokens, parts)).astype(BF16)
-
-    prex_b, down, rest = conv_back(
-        place, summed, grads, mixed_b, grad_y, gmix, dsilu, pre_x, conv_weight, skip_gain,
-        w_down, w_keyq,
-    )
-    down, rest = lax.psum((down, rest), "dp")
-    grad_wx = weight_grad(prex_b, False)
+    half_sent, out_keep = branch(place, gated_b, w_out, tokens, parts)
+
+    prex_b, small, small_send = conv_back(
+        place, summed, grads, mixed_b, grad_y, gmix, dsilu, pre_x, ups, conv_weight, skip_gain,
+        w_down, keyq_t, dp_size, pins_conv,
+    )
+
+    def in_grad(value, far, near):
+        pieces = (value, far, near, swap(far, "dp", 1))
+        keep, send = in_weight(sides, pieces)
+        return keep + swap(send, "dp", 4).astype(F32)
+
+    if blocked:
+        prex_far = swap(prex_b, "dp", 2)
+        prex_near = swap(prex_b, "dp", 1)
+        keep, later, send = out_weight((gated_b, gated_far), (up_own, up_far), ())
+        come = swap(send, "dp", 1).astype(F32)
+        cut = later.shape[1]
+        come_far = swap((later + come[:, cut:]).astype(BF16), "dp", 2)
+        grad_wout = keep + come[:, :cut] + come_far.astype(F32)
+        grad_wz = in_grad(prez_b, prez_far, prez_near)
+        grad_wx = in_grad(prex_b, prex_far, prex_near)
+    else:
+
+        def weight_grad(value, left):
+            pieces = gather_tokens(value, "dp")
+            pairs = zip(pieces, up_parts) if left else zip(norm_parts, pieces)
+            return scatter_sum(sum(mm_tn(a, b) for a, b in pairs), "dp", 1 if left else 0)
+
+        grad_wout = weight_grad(gated_b, True)
+        grad_wz = weight_grad(prez_b, False)
+        grad_wx = weight_grad(prex_b, False)
 
     send, keep, stats, slope, shift, base = input_grad(
-        place, group_ids, group_weights, prex_b, prez_b, w_x, w_z, tokens, cotangent, norm_gain,
-        parts,
-    )
-    norm_grad = over_state(send, keep)
+        place, group_ids, group_weights, half_sent, prex_b, prez_b, w_x, w_z, tokens, cotangent,
+        norm_gain, parts,
+    )
+    come = swap(send, "state", 1)
+    pair = jnp.stack([out_keep[1], keep[1]]) + come[1].astype(F32)
+    come_far = swap(pair.astype(BF16), "state", 2).astype(F32)
+    block_out = (out_keep[0] + come[0, 0].astype(F32) + come_far[0]).astype(BF16)
+    norm_grad = keep[0] + come[0, 1].astype(F32) + come_far[1]
     stats = all_sum(stats, "state")
     row_stat = stats[: rows // LANES].reshape(rows, 1)
     grad_in = norm_grad * slope - shift * row_stat + base
     gain_rows = own_width // LANES
-    own_gain = lax.dynamic_slice_in_dim(
+    gain = lax.dynamic_slice_in_dim(
         stats, rows // LANES + state_index * gain_rows, gain_rows, 0
     )
-    grad_gain = all_sum(own_gain, "dp").reshape(-1)
 
     count = 2 * states
     rank = w_up.shape[0]
+    if blocked:
+        small = small + swap(small_send, "dp", 1).astype(F32)
+        small = small[:2] + swap(small[2:].astype(BF16), "dp", 2).astype(F32)
+        small = small[0] + swap(small[1].astype(BF16), "dp", 4).astype(F32)
+        pieces = [small.astype(BF16)]
+        gathered = pieces[0]
+        for bit in (4, 2, 1):
+            high = lax.reduce_precision(gain, 8, 7)
+            rest = lax.reduce_precision(gain - high, 8, 7)
+            line = jnp.concatenate([high.reshape(1, -1), rest.reshape(1, -1)], axis=1)
+            tail = jnp.pad(line.astype(BF16), ((0, SUB - 1), (0, 0)))
+            come = swap(jnp.concatenate([gathered, tail], axis=0), "dp", bit)
+            pieces.append(come[:-SUB])
+            gathered = jnp.concatenate([gathered, come[:-SUB]], axis=0)
+            other = come[-SUB].astype(F32)
+            gain = (high + rest) + (other[:own_width] + other[own_width:]).reshape(gain.shape)
+        grad_gain = gain.reshape(-1)
+        grad_up, down, keyq, lines = unpack(place, pieces, rank, count, taps)
+    else:
+        small = all_sum(small, "dp")
+        grad_up = small[:rank]
+        down = small[rank : 2 * rank].T
+        keyq = small[2 * rank : 2 * rank + count]
+        lines = small[2 * rank + count :]
+        grad_gain = all_sum(gain, "dp").reshape(-1)
     return (
         block_out,
         grad_in,
         grad_gain,
         grad_wx,
         grad_wz,
-        rest[count : count + taps],
-        rest[count + taps],
+        lines[:taps],
+        lines[taps],
         down,
-        ups[:rank],
-        ups[rank],
-        rest[:count].T,
-        rest[count + taps + 1],
+        grad_up,
+        lines[taps + 2],
+        keyq.T,
+        lines[taps + 1],
         grad_wout,
-        jnp.max(rest[count + taps + 2]),
+        jnp.max(lines[taps + 3] + lines[taps + 4]),
     )
 
 

time: 310 us -> 222 us (0.72)
  waiting for transfers between devices: 148 us -> 89 us
  local copies, waits for them, and re-layouts: 43.2 us -> 6.8 us
  Pallas kernels: 57.8 us -> 82.6 us
  between operations: 15 us -> 1.87 us
  other arithmetic: 14.7 us -> 8.69 us
    ppermute x28 -> x29, waiting for transfers between devices: 148 us -> 89 us  [swap(): return lax.ppermute(value, axis, [(i, i ^ bit) for i in range(size)])]
    unnamed x92 -> x62, local copies, waits for them, and re-layouts: 36.9 us -> 6.02 us
    pallas_call x3 -> x4, Pallas kernels: 23.9 us -> 29.9 us  [the longest x1 18.9 us: scan_backward(): pl.pallas_call(functools.partial(back_kernel, unroll, len(pins)), in_spec...]
    pallas_call x1, Pallas kernels: 7.49 us -> 12 us  [scan_forward(): pl.pallas_call(functools.partial(scan_kernel, 4), in_specs=[WHOLE] * 8, o...]
    slice x3 -> x7, local copies, waits for them, and re-layouts: 4.66 us -> 0.74 us  [the longest x1 0.61 us: per_device(): lines[:taps]]
    pallas_call x2, Pallas kernels: 5.44 us -> 9.18 us  [in_weight(): pl.pallas_call(in_weight_kernel, grid=(2,), in_specs=[side, pl.BlockSpec(...]
    convert_element_type x3 -> x8, other arithmetic: 4.27 us -> 0.82 us  [the longest x2 0.29 us: per_device(): come_far = swap(pair.astype(BF16), 'state', 2).astype(F32)]
    pallas_call x1, Pallas kernels: 6.53 us -> 9.86 us  [input_grad(): pl.pallas_call(input_kernel, grid_spec=pltpu.PrefetchScalarGridSpec(num_s...]
  transfers between devices with their start and end apart: 29 -> 29, of which waited for: 14 -> 10; matrix products, arithmetic and copies ran while one was open for 6% -> 3% of each run, Pallas kernels for 8% -> 31%
where the time goes in v1:
time: 222 us; the launch traced here: 221 us
  waiting for transfers between devices  89 us (40%)
  Pallas kernels  82.6 us (37%)
  starting transfers between devices  32.1 us (14%)
  other arithmetic  8.69 us (4%)
  local copies, waits for them, and re-layouts  6.8 us (3%)
    ppermute x29, waiting for transfers between devices, swap(): return lax.ppermute(value, axis, [(i, i ^ bit) for i in range(size)])  89 us
    ppermute x29, starting transfers between devices, swap(): return lax.ppermute(value, axis, [(i, i ^ bit) for i in range(size)])  32.1 us
    pallas_call x1, Pallas kernels, scan_backward(): pl.pallas_call(functools.partial(back_kernel, unroll, len(pins)), in_spec...  18.9 us
    pallas_call x1, Pallas kernels, scan_forward(): pl.pallas_call(functools.partial(scan_kernel, 4), in_specs=[WHOLE] * 8, o...  12 us
    pallas_call x1, Pallas kernels, input_grad(): pl.pallas_call(input_kernel, grid_spec=pltpu.PrefetchScalarGridSpec(num_s...  9.86 us
    pallas_call x1, Pallas kernels, front(): pl.pallas_call(functools.partial(front_kernel, blocked), grid=(inner // b...  9.28 us
    pallas_call x2, Pallas kernels, in_weight(): pl.pallas_call(in_weight_kernel, grid=(2,), in_specs=[side, pl.BlockSpec(...  9.18 us
    pallas_call x1, Pallas kernels, gate(): pl.pallas_call(gate_kernel, grid=(inner // blk,), in_specs=[whole((rows,...  6.42 us
  transfers between devices with their start and end apart: 29, of which 10 were waited for; matrix products, arithmetic and copies ran while one was open for 3% of the time, Pallas kernels for 31%

profile of v1, /device:TPU:0, one launch (start us, length us, event | category | flops | bytes accessed | tf_op | source)
XLA Modules:
  0.0 221.1 jit_solution(14347251890430052600)
XLA Ops:
  1.4 0.7 copy-done.12
  2.0 9.3 %front.1 = (bf16[256,2048]{1,0:T(8,128)(2,1)}, bf16[256,2048]{1,0:T(8,128)(2,1)}, f32[256,1024]{1,0:T(8,128)}, bf16[256,1024]{1,0:T(8,128)(2,1)}, f32[256,1024]{...) custom-call(s32[2]{0:T(128)S(1)} %pad_add_fusion.place, ...), custom_call_target="tpu_custom_call" | custom-call | tf_op jit(solution)/shard_map/front/pallas_call | solution.py:146
  11.3 3.1 %collective-permute-start.2 = (bf16[2,256,512]{2,1,0:T(8,128)(2,1)}, bf16[2,256,512]{2,1,0:T(8,128)(2,1)S(1)}, u32[]{:S(2)}, u32[]{:S(2)}) collective-permute-start(bf16[2,256,512]{2,1,0:T(8,128)(2,1)} %get-tuple-element.75), channel_id=1, source_target_pairs={{0,8},{4,12},{8,0},{12,4},{16,24},{20,28},{24,16},{28,20},{1,9},{5... | collective-permute-start | bytes 1572872 | tf_op jit(solution)/shard_map/ppermute | solution.py:35
  14.4 1.5 collective-permute-start.3
  15.9 2.6 %collective-permute-start.9 = (bf16[256,1024]{1,0:T(8,128)(2,1)}, bf16[256,1024]{1,0:T(8,128)(2,1)S(1)}, u32[]{:S(2)}, u32[]{:S(2)}) collective-permute-start(bf16[256,1024]{1,0:T(8,128)(2,1)} %get-tuple-element.83), channel_id=1, source_target_pairs={{0,16},{4,20},{8,24},{12,28},{16,0},{20,4},{24,8},{28,12},{1,17},{... | collective-permute-start | bytes 1572872 | tf_op jit(solution)/shard_map/ppermute | solution.py:35
  18.6 1.6 collective-permute-start.1
  20.1 6.4 %gate.1 = (f32[256,1024]{1,0:T(8,128)S(1)}, f32[256,1024]{1,0:T(8,128)S(1)}, f32[256,1024]{1,0:T(8,128)S(1)}) custom-call(bf16[256,2048]{1,0:T(8,128)(2,1)} %get-tuple-element.62.normed, bf16[256,2048]{1,0:T(8,128)(2,1)} %get-tuple-element.63.up, bf16[2048,1024]{1,0:T(8,128)(2,1)} %wz.3, bf16[1024,2048]{1,0:T(8,128)(2,1)} %wo.3), custom_call_target="tpu_custom_call" | custom-call | tf_op jit(solution)/shard_map/gate/pallas_call | solution.py:206
  26.6 12.0 %scan.1 = (bf16[256,1024]{1,0:T(8,128)(2,1)}, bf16[256,1024]{1,0:T(8,128)(2,1)}, f32[256,1024]{1,0:T(8,128)S(1)}, f32[256,1024]{1,0:T(8,128)S(1)}, f32[8,128]{1,...) custom-call(f32[320,128]{1,0:T(8,128)S(1)} %add.108.one, ...), custom_call_target="tpu_custom_call" | custom-call | tf_op jit(solution)/shard_map/scan/pallas_call | solution.py:321
  39.0 1.1 collective-permute-start.8
  40.4 18.9 %back.1 = (f32[256,1024]{1,0:T(8,128)}, f32[336,128]{1,0:T(8,128)S(1)}, f32[136,1024]{1,0:T(8,128)}) custom-call(s32[2]{0:T(128)S(1)} %pad_add_fusion.place, f32[320,128]{1,0:T(8,128)S(1)} %add.108.one, f32[320,128]{1,0:T(8,128)S(1)} %collective-permute-done.1.two, bf16[256,1024]{1,0:T(8,128)(2,1)S(1)} %copy-done.1, bf16[128,1024]{1,0:T(8,128)(2,1)} %wup.3, ...), custom_call_target="tpu_custom_call" | custom-call | tf_op jit(solution)/shard_map/back/pallas_call | solution.py:475
  59.5 1.4 collective-permute-done.4
  60.9 1.0 collective-permute-start.10
  62.5 6.7 %collective-permute-done.10.rest_4_.l3 = bf16[256,512]{1,0:T(8,128)(2,1)S(1)} collective-permute-done((bf16[256,512]{1,0:T(8,128)(2,1)S(1)}, bf16[256,512]{1,0:T(8,128)(2,1)S(1)}, u32[]{:S(2)}, u32[]{:S(2)}) %collective-permute-start.10) | collective-permute-done | bytes 262176 | tf_op jit(solution)/shard_map/ppermute | solution.py:35
  69.3 1.8 copy-done.10
  71.1 1.1 copy-done.11
  72.2 4.3 %conv.1 = (bf16[256,1024]{1,0:T(8,128)(2,1)}, f32[4,40,1024]{2,1,0:T(8,128)}, bf16[4,40,1024]{2,1,0:T(8,128)(2,1)}) custom-call(s32[2]{0:T(128)S(1)} %pad_add_fusion.place, f32[320,128]{1,0:T(8,128)S(1)} %add.108.one, f32[320,128]{1,0:T(8,128)S(1)} %collective-permute-done.1.two, f32[336,128]{1,0:T(8,128)S(1)} %add.109.grad_one, ...), custom_call_target="tpu_custom_call" | custom-call | tf_op jit(solution)/shard_map/conv/pallas_call | solution.py:577
  76.5 1.0 collective-permute-start.15
  77.5 6.0 %branch.1 = (bf16[2,2,256,512]{3,2,1,0:T(8,128)(2,1)}, f32[2,256,512]{2,1,0:T(8,128)}) custom-call(s32[2]{0:T(128)S(1)} %pad_add_fusion.place, bf16[256,1024]{1,0:T(8,128)(2,1)} %get-tuple-element.66.gated.l0, bf16[1024,2048]{1,0:T(8,128)(2,1)} %wo.3, bf16[256,2048]{1,0:T(8,128)(2,1)} %tok_own.1), custom_call_target="tpu_custom_call" | custom-call | tf_op jit(solution)/shard_map/branch/pallas_call | solution.py:649
  83.5 9.9 %inputs.1 = (bf16[2,2,256,512]{3,2,1,0:T(8,128)(2,1)}, f32[2,256,512]{2,1,0:T(8,128)}, f32[18,128]{1,0:T(8,128)S(1)}, f32[256,512]{1,0:T(8,128)}, f32[256,512]{1,0:T(8,128)}, /*index=5*/f32[256,512]{1,0:T(8,128)}) custom-call(s32[2]{0:T(128)S(1)} %pad_add_fusion.place, s32[1]{0:T(128)S(6)} %copy.47.ids, ...), custom_call_target="tpu_custom_call", output_to_operand_aliasing={{0}: (3, {})} | custom-call | tf_op jit(solution)/shard_map/inputs/pallas_call | solution.py:732
  93.5 1.2 collective-permute-done.13
  95.2 3.2 %collective-permute-done.14 = f32[18,128]{1,0:T(8,128)S(1)} collective-permute-done((f32[18,128]{1,0:T(8,128)S(1)}, f32[18,128]{1,0:T(8,128)S(1)}, u32[]{:S(2)}, u32[]{:S(2)}) %collective-permute-start.14) | collective-permute-done | bytes 9248 | tf_op jit(solution)/shard_map/ppermute | solution.py:35
  98.3 1.2 convert_add_fusion.2
  99.6 1.7 collective-permute-start.16
  101.2 3.7 %collective-permute-done.16 = bf16[2,40,1024]{2,1,0:T(8,128)(2,1)S(1)} collective-permute-done((bf16[2,40,1024]{2,1,0:T(8,128)(2,1)S(1)}, bf16[2,40,1024]{2,1,0:T(8,128)(2,1)S(1)}, u32[]{:S(2)}, u32[]{:S(2)}) %collective-permute-start.16) | collective-permute-done | bytes 163872 | tf_op jit(solution)/shard_map/ppermute | solution.py:35
  105.0 2.6 %collective-permute-start.17 = (bf16[40,1024]{1,0:T(8,128)(2,1)S(1)}, bf16[40,1024]{1,0:T(8,128)(2,1)S(1)}, u32[]{:S(2)}, u32[]{:S(2)}) collective-permute-start(bf16[40,1024]{1,0:T(8,128)(2,1)S(1)} %fusion.11), channel_id=1, source_target_pairs={{0,16},{4,20},{8,24},{12,28},{16,0},{20,4},{24,8},{28,12},{1,17},{... | collective-permute-start | bytes 245768 | tf_op jit(solution)/shard_map/ppermute | solution.py:35
  107.7 2.7 %collective-permute-done.17 = bf16[40,1024]{1,0:T(8,128)(2,1)S(1)} collective-permute-done((bf16[40,1024]{1,0:T(8,128)(2,1)S(1)}, bf16[40,1024]{1,0:T(8,128)(2,1)S(1)}, u32[]{:S(2)}, u32[]{:S(2)}) %collective-permute-start.17) | collective-permute-done | bytes 81952 | tf_op jit(solution)/shard_map/ppermute | solution.py:35
  110.4 2.7 %collective-permute-start.18 = (bf16[48,1024]{1,0:T(8,128)(2,1)S(1)}, bf16[48,1024]{1,0:T(8,128)(2,1)S(1)}, u32[]{:S(2)}, u32[]{:S(2)}) collective-permute-start(bf16[48,1024]{1,0:T(8,128)(2,1)S(1)} %pad_maximum_fusion.2), channel_id=1, source_target_pairs={{0,16},{4,20},{8,24},{12,28},{16,0},{20,4},{24,8},{28,12},{1,17},{... | collective-permute-start | bytes 294920 | tf_op jit(solution)/shard_map/ppermute | solution.py:35
  113.2 4.9 %outw.1 = (f32[1024,256]{1,0:T(8,128)}, f32[1024,256]{1,0:T(8,128)}, bf16[1024,512]{1,0:T(8,128)(2,1)}) custom-call(bf16[256,1024]{1,0:T(8,128)(2,1)} %get-tuple-element.66.gated.l0, bf16[256,1024]{1,0:T(8,128)(2,1)} %copy-done.7, bf16[256,1024]{1,0:T(8,128)(2,1)} %get-tuple-element.102.r0, bf16[256,1024]{1,0:T(8,128)(2,1)} %copy-done.6), custom_call_target="tpu_custom_call" | custom-call | tf_op jit(solution)/shard_map/outw/pallas_call | solution.py:787
  118.7 1.5 collective-permute-start.25
  120.7 3.7 %collective-permute-start.21 = (bf16[256,1024]{1,0:T(8,128)(2,1)S(1)}, bf16[256,1024]{1,0:T(8,128)(2,1)S(1)}, u32[]{:S(2)}, u32[]{:S(2)}) collective-permute-start(bf16[256,1024]{1,0:T(8,128)(2,1)S(1)} %copy-done.14), channel_id=1, source_target_pairs={{0,8},{4,12},{8,0},{12,4},{16,24},{20,28},{24,16},{28,20},{1,9},{5... | collective-permute-start | bytes 1572872 | tf_op jit(solution)/shard_map/ppermute | solution.py:35
  124.7 31.0 %collective-permute-done.25.r3 = bf16[256,1024]{1,0:T(8,128)(2,1)S(1)} collective-permute-done((bf16[256,1024]{1,0:T(8,128)(2,1)S(1)}, bf16[256,1024]{1,0:T(8,128)(2,1)S(1)}, u32[]{:S(2)}, u32[]{:S(2)}) %collective-permute-start.25) | collective-permute-done | bytes 524320 | tf_op jit(solution)/shard_map/ppermute | solution.py:35
  155.7 0.8 copy-done.25
  156.5 4.6 %inw.3 = (f32[256,1024]{1,0:T(8,128)}, bf16[256,1024]{1,0:T(8,128)(2,1)}) custom-call(bf16[256,512]{1,0:T(8,128)(2,1)} %get-tuple-element.93.l0, bf16[2,256,512]{2,1,0:T(8,128)(2,1)} %copy-done, bf16[256,512]{1,0:T(8,128)(2,1)} %copy-done.3, bf16[256,512]{1,0:T(8,128)(2,1)} %copy-done.2, bf16[256,1024]{1,0:T(8,128)(2,1)} %get-tuple-element.82.prez.r0, ...), custom_call_target="tpu_custom_call" | custom-call | tf_op jit(solution)/shard_map/inw/pallas_call | solution.py:825
  161.4 1.0 collective-permute-start.23
  162.6 1.0 collective-permute-start.20
  164.1 22.9 %collective-permute-done.26 = bf16[256,1024]{1,0:T(8,128)(2,1)S(1)} collective-permute-done((bf16[256,1024]{1,0:T(8,128)(2,1)}, bf16[256,1024]{1,0:T(8,128)(2,1)S(1)}, u32[]{:S(2)}, u32[]{:S(2)}) %collective-permute-start.26) | collective-permute-done | bytes 524320 | tf_op jit(solution)/shard_map/ppermute | solution.py:35
  187.0 1.1 convert_add_fusion
  189.0 0.8 copy-done.22
  189.8 0.8 copy-done.24
  190.6 4.6 %inw.2 = (f32[256,1024]{1,0:T(8,128)}, bf16[256,1024]{1,0:T(8,128)(2,1)}) custom-call(bf16[256,512]{1,0:T(8,128)(2,1)} %get-tuple-element.93.l0, bf16[2,256,512]{2,1,0:T(8,128)(2,1)} %copy-done, bf16[256,512]{1,0:T(8,128)(2,1)} %copy-done.3, bf16[256,512]{1,0:T(8,128)(2,1)} %copy-done.2, bf16[256,1024]{1,0:T(8,128)(2,1)} %get-tuple-element.84.prex.r0, ...), custom_call_target="tpu_custom_call" | custom-call | tf_op jit(solution)/shard_map/inw/pallas_call | solution.py:825
  195.2 1.7 collective-permute-start.24
  197.0 1.8 unpack.1
  199.3 1.2 add_reduce_fusion
  201.1 1.5 collective-permute-done.28
  202.7 1.2 fusion.1
  204.0 1.2 fusion.6
  205.2 14.8 %collective-permute-done.24 = bf16[256,1024]{1,0:T(8,128)(2,1)S(1)} collective-permute-done((bf16[256,1024]{1,0:T(8,128)(2,1)}, bf16[256,1024]{1,0:T(8,128)(2,1)S(1)}, u32[]{:S(2)}, u32[]{:S(2)}) %collective-permute-start.24) | collective-permute-done | bytes 524320 | tf_op jit(solution)/shard_map/ppermute | solution.py:35
  219.9 1.1 convert_add_fusion.1
  (128 shorter events, 6.8 us)
Async XLA Ops:
  11.3 29.1 %collective-permute-start.2 = (bf16[2,256,512]{2,1,0:T(8,128)(2,1)}, bf16[2,256,512]{2,1,0:T(8,128)(2,1)S(1)}, u32[]{:S(2)}, u32[]{:S(2)}) collective-permute-start(bf16[2,256,512]{2,1,0:T(8,128)(2,1)} %get-tuple-element.75), channel_id=1, source_target_pairs={{0,8},{4,12},{8,0},{12,4},{16,24},{20,28},{24,16},{28,20},{1,9},{5... | collective-permute-start | bytes 1572872 | tf_op jit(solution)/shard_map/ppermute | solution.py:35
  14.4 4.1 %collective-permute-start = (f32[320,128]{1,0:T(8,128)S(1)}, f32[320,128]{1,0:T(8,128)S(1)}, u32[]{:S(2)}, u32[]{:S(2)}) collective-permute-start(f32[320,128]{1,0:T(8,128)S(1)} %get-tuple-element.60), channel_id=1, source_target_pairs={{0,1},{1,0},{2,3},{3,2},{4,5},{5,4},{6,7},{7,6},{8,9},{9,8},{10,11... | collective-permute-start | bytes 491528 | tf_op jit(solution)/shard_map/ppermute | solution.py:35
  14.4 25.6 %collective-permute-start.3 = (bf16[256,512]{1,0:T(8,128)(2,1)}, bf16[256,512]{1,0:T(8,128)(2,1)S(1)}, u32[]{:S(2)}, u32[]{:S(2)}) collective-permute-start(bf16[256,512]{1,0:T(8,128)(2,1)} %get-tuple-element.76), channel_id=1, source_target_pairs={{0,4},{4,0},{8,12},{12,8},{16,20},{20,16},{24,28},{28,24},{1,5},{5... | collective-permute-start | bytes 786440 | tf_op jit(solution)/shard_map/ppermute | solution.py:35
  15.9 45.9 %collective-permute-start.9 = (bf16[256,1024]{1,0:T(8,128)(2,1)}, bf16[256,1024]{1,0:T(8,128)(2,1)S(1)}, u32[]{:S(2)}, u32[]{:S(2)}) collective-permute-start(bf16[256,1024]{1,0:T(8,128)(2,1)} %get-tuple-element.83), channel_id=1, source_target_pairs={{0,16},{4,20},{8,24},{12,28},{16,0},{20,4},{24,8},{28,12},{1,17},{... | collective-permute-start | bytes 1572872 | tf_op jit(solution)/shard_map/ppermute | solution.py:35
  18.6 8.0 %collective-permute-start.1 = (f32[320,128]{1,0:T(8,128)S(1)}, f32[320,128]{1,0:T(8,128)S(1)}, u32[]{:S(2)}, u32[]{:S(2)}) collective-permute-start(f32[320,128]{1,0:T(8,128)S(1)} %add.108.one), channel_id=1, source_target_pairs={{0,2},{1,3},{2,0},{3,1},{4,6},{5,7},{6,4},{7,5},{8,10},{9,11},{10,... | collective-permute-start | bytes 491528 | tf_op jit(solution)/shard_map/ppermute | solution.py:35
  38.6 30.7 %collective-permute-start.6 = (bf16[256,1024]{1,0:T(8,128)(2,1)}, bf16[256,1024]{1,0:T(8,128)(2,1)S(1)}, u32[]{:S(2)}, u32[]{:S(2)}) collective-permute-start(bf16[256,1024]{1,0:T(8,128)(2,1)} %get-tuple-element.66.gated.l0), channel_id=1, source_target_pairs={{0,16},{4,20},{8,24},{12,28},{16,0},{20,4},{24,8},{28,12},{1,17},{... | collective-permute-start | bytes 1572872 | tf_op jit(solution)/shard_map/ppermute | solution.py:35
  39.0 30.3 %collective-permute-start.8 = (bf16[256,1024]{1,0:T(8,128)(2,1)}, bf16[256,1024]{1,0:T(8,128)(2,1)S(1)}, u32[]{:S(2)}, u32[]{:S(2)}) collective-permute-start(bf16[256,1024]{1,0:T(8,128)(2,1)} %get-tuple-element.82.prez.r0), channel_id=1, source_target_pairs={{0,4},{4,0},{8,12},{12,8},{16,20},{20,16},{24,28},{28,24},{1,5},{5... | collective-permute-start | bytes 1572872 | tf_op jit(solution)/shard_map/ppermute | solution.py:35
  40.0 19.4 %copy-start.3 = (bf16[256,512]{1,0:T(8,128)(2,1)}, bf16[256,512]{1,0:T(8,128)(2,1)S(1)}, u32[]{:S(2)}) copy-start(bf16[256,512]{1,0:T(8,128)(2,1)S(1)} %collective-permute-done.3.rest_1_.l2) | copy-start | bytes 786436
  40.0 29.2 %collective-permute-start.7 = (bf16[256,1024]{1,0:T(8,128)(2,1)}, bf16[256,1024]{1,0:T(8,128)(2,1)S(1)}, u32[]{:S(2)}, u32[]{:S(2)}) collective-permute-start(bf16[256,1024]{1,0:T(8,128)(2,1)} %get-tuple-element.82.prez.r0), channel_id=1, source_target_pairs={{0,8},{4,12},{8,0},{12,4},{16,24},{20,28},{24,16},{28,20},{1,9},{5... | collective-permute-start | bytes 1572872 | tf_op jit(solution)/shard_map/ppermute | solution.py:35
  40.4 19.0 %copy-start = (bf16[2,256,512]{2,1,0:T(8,128)(2,1)}, bf16[2,256,512]{2,1,0:T(8,128)(2,1)S(1)}, u32[]{:S(2)}) copy-start(bf16[2,256,512]{2,1,0:T(8,128)(2,1)S(1)} %collective-permute-done.2.rest_0_.l1) | copy-start | bytes 1572868
  40.4 28.8 %copy-start.8 = (f32[256,1024]{1,0:T(8,128)S(1)}, f32[256,1024]{1,0:T(8,128)}, u32[]{:S(2)}) copy-start(f32[256,1024]{1,0:T(8,128)} %get-tuple-element.80.prex) | copy-start | bytes 3145732
  40.4 28.8 %copy-start.9 = (f32[256,1024]{1,0:T(8,128)S(1)}, f32[256,1024]{1,0:T(8,128)}, u32[]{:S(2)}) copy-start(f32[256,1024]{1,0:T(8,128)} %get-tuple-element.79.dsilu) | copy-start | bytes 3145732
  59.4 1.5 collective-permute-start.4
  60.9 8.4 %collective-permute-start.10 = (bf16[256,512]{1,0:T(8,128)(2,1)S(1)}, bf16[256,512]{1,0:T(8,128)(2,1)S(1)}, u32[]{:S(2)}, u32[]{:S(2)}) collective-permute-start(bf16[256,512]{1,0:T(8,128)(2,1)S(1)} %slice_bitcast_fusion.5), channel_id=1, source_target_pairs={{0,4},{4,0},{8,12},{12,8},{16,20},{20,16},{24,28},{28,24},{1,5},{5... | collective-permute-start | bytes 786440 | tf_op jit(solution)/shard_map/ppermute | solution.py:35
  61.9 14.6 %copy-start.6 = (bf16[256,1024]{1,0:T(8,128)(2,1)}, bf16[256,1024]{1,0:T(8,128)(2,1)S(1)}, u32[]{:S(2)}) copy-start(bf16[256,1024]{1,0:T(8,128)(2,1)S(1)} %collective-permute-done.9.rest_3_.r1) | copy-start | bytes 1572868
  61.9 7.4 %collective-permute-start.5 = (f32[336,128]{1,0:T(8,128)S(1)}, f32[336,128]{1,0:T(8,128)S(1)}, u32[]{:S(2)}, u32[]{:S(2)}) collective-permute-start(f32[336,128]{1,0:T(8,128)S(1)} %add.109.grad_one), channel_id=1, source_target_pairs={{0,2},{1,3},{2,0},{3,1},{4,6},{5,7},{6,4},{7,5},{8,10},{9,11},{10,... | collective-permute-start | bytes 516104 | tf_op jit(solution)/shard_map/ppermute | solution.py:35
  69.2 7.2 %copy-start.2 = (bf16[256,512]{1,0:T(8,128)(2,1)}, bf16[256,512]{1,0:T(8,128)(2,1)S(1)}, u32[]{:S(2)}) copy-start(bf16[256,512]{1,0:T(8,128)(2,1)S(1)} %collective-permute-done.10.rest_4_.l3) | copy-start | bytes 786436
  69.2 49.4 %copy-start.5 = (bf16[256,1024]{1,0:T(8,128)(2,1)}, bf16[256,1024]{1,0:T(8,128)(2,1)S(1)}, u32[]{:S(2)}) copy-start(bf16[256,1024]{1,0:T(8,128)(2,1)S(1)} %collective-permute-done.7.rest_1_.r1) | copy-start | bytes 1572868
  76.5 21.9 %collective-permute-start.15 = (bf16[4,40,1024]{2,1,0:T(8,128)(2,1)}, bf16[4,40,1024]{2,1,0:T(8,128)(2,1)S(1)}, u32[]{:S(2)}, u32[]{:S(2)}) collective-permute-start(bf16[4,40,1024]{2,1,0:T(8,128)(2,1)} %get-tuple-element.92), channel_id=1, source_target_pairs={{0,4},{4,0},{8,12},{12,8},{16,20},{20,16},{24,28},{28,24},{1,5},{5... | collective-permute-start | bytes 983048 | tf_op jit(solution)/shard_map/ppermute | solution.py:35
  83.5 29.7 %copy-start.20 = (f32[2,256,512]{2,1,0:T(8,128)S(1)}, f32[2,256,512]{2,1,0:T(8,128)}, u32[]{:S(2)}) copy-start(f32[2,256,512]{2,1,0:T(8,128)} %get-tuple-element.67) | copy-start | bytes 3145732
  93.3 26.8 %copy-start.14 = (bf16[256,1024]{1,0:T(8,128)(2,1)S(1)}, bf16[256,1024]{1,0:T(8,128)(2,1)}, u32[]{:S(2)}) copy-start(bf16[256,1024]{1,0:T(8,128)(2,1)} %get-tuple-element.84.prex.r0) | copy-start | bytes 1572868
  93.4 62.3 %copy-start.16 = (bf16[2,2,256,512]{3,2,1,0:T(8,128)(2,1)S(1)}, bf16[2,2,256,512]{3,2,1,0:T(8,128)(2,1)}, u32[]{:S(2)}) copy-start(bf16[2,2,256,512]{3,2,1,0:T(8,128)(2,1)} %get-tuple-element.85) | copy-start | bytes 3145732
  93.4 1.2 collective-permute-start.13
  94.6 3.7 %collective-permute-start.14 = (f32[18,128]{1,0:T(8,128)S(1)}, f32[18,128]{1,0:T(8,128)S(1)}, u32[]{:S(2)}, u32[]{:S(2)}) collective-permute-start(f32[18,128]{1,0:T(8,128)S(1)} %add.115), channel_id=1, source_target_pairs={{0,2},{1,3},{2,0},{3,1},{4,6},{5,7},{6,4},{7,5},{8,10},{9,11},{10,... | collective-permute-start | bytes 27656 | tf_op jit(solution)/shard_map/ppermute | solution.py:35
  95.1 29.3 %copy-start.21 = (f32[2,256,512]{2,1,0:T(8,128)S(1)}, f32[2,256,512]{2,1,0:T(8,128)}, u32[]{:S(2)}) copy-start(f32[2,256,512]{2,1,0:T(8,128)} %get-tuple-element.86) | copy-start | bytes 3145732
  99.6 5.4 %collective-permute-start.16 = (bf16[2,40,1024]{2,1,0:T(8,128)(2,1)S(1)}, bf16[2,40,1024]{2,1,0:T(8,128)(2,1)S(1)}, u32[]{:S(2)}, u32[]{:S(2)}) collective-permute-start(bf16[2,40,1024]{2,1,0:T(8,128)(2,1)S(1)} %slice.247), channel_id=1, source_target_pairs={{0,8},{4,12},{8,0},{12,4},{16,24},{20,28},{24,16},{28,20},{1,9},{5... | collective-permute-start | bytes 491528 | tf_op jit(solution)/shard_map/ppermute | solution.py:35
  105.0 5.4 %collective-permute-start.17 = (bf16[40,1024]{1,0:T(8,128)(2,1)S(1)}, bf16[40,1024]{1,0:T(8,128)(2,1)S(1)}, u32[]{:S(2)}, u32[]{:S(2)}) collective-permute-start(bf16[40,1024]{1,0:T(8,128)(2,1)S(1)} %fusion.11), channel_id=1, source_target_pairs={{0,16},{4,20},{8,24},{12,28},{16,0},{20,4},{24,8},{28,12},{1,17},{... | collective-permute-start | bytes 245768 | tf_op jit(solution)/shard_map/ppermute | solution.py:35
  110.4 14.0 %collective-permute-start.18 = (bf16[48,1024]{1,0:T(8,128)(2,1)S(1)}, bf16[48,1024]{1,0:T(8,128)(2,1)S(1)}, u32[]{:S(2)}, u32[]{:S(2)}) collective-permute-start(bf16[48,1024]{1,0:T(8,128)(2,1)S(1)} %pad_maximum_fusion.2), channel_id=1, source_target_pairs={{0,16},{4,20},{8,24},{12,28},{16,0},{20,4},{24,8},{28,12},{1,17},{... | collective-permute-start | bytes 294920 | tf_op jit(solution)/shard_map/ppermute | solution.py:35
  118.1 44.4 %collective-permute-start.27 = (bf16[1024,512]{1,0:T(8,128)(2,1)}, bf16[1024,512]{1,0:T(8,128)(2,1)S(1)}, u32[]{:S(2)}, u32[]{:S(2)}) collective-permute-start(bf16[1024,512]{1,0:T(8,128)(2,1)} %get-tuple-element.104), channel_id=1, source_target_pairs={{0,4},{4,0},{8,12},{12,8},{16,20},{20,16},{24,28},{28,24},{1,5},{5... | collective-permute-start | bytes 3145736 | tf_op jit(solution)/shard_map/ppermute | solution.py:35
  118.7 37.0 %collective-permute-start.25 = (bf16[256,1024]{1,0:T(8,128)(2,1)S(1)}, bf16[256,1024]{1,0:T(8,128)(2,1)S(1)}, u32[]{:S(2)}, u32[]{:S(2)}) collective-permute-start(bf16[256,1024]{1,0:T(8,128)(2,1)S(1)} %collective-permute-done.7.rest_1_.r1), channel_id=1, source_target_pairs={{0,4},{4,0},{8,12},{12,8},{16,20},{20,16},{24,28},{28,24},{1,5},{5... | collective-permute-start | bytes 1572872 | tf_op jit(solution)/shard_map/ppermute | solution.py:35
  120.1 68.8 %collective-permute-start.22 = (bf16[256,1024]{1,0:T(8,128)(2,1)S(1)}, bf16[256,1024]{1,0:T(8,128)(2,1)S(1)}, u32[]{:S(2)}, u32[]{:S(2)}) collective-permute-start(bf16[256,1024]{1,0:T(8,128)(2,1)S(1)} %copy-done.14), channel_id=1, source_target_pairs={{0,4},{4,0},{8,12},{12,8},{16,20},{20,16},{24,28},{28,24},{1,5},{5... | collective-permute-start | bytes 1572872 | tf_op jit(solution)/shard_map/ppermute | solution.py:35
  120.7 40.4 %collective-permute-start.21 = (bf16[256,1024]{1,0:T(8,128)(2,1)S(1)}, bf16[256,1024]{1,0:T(8,128)(2,1)S(1)}, u32[]{:S(2)}, u32[]{:S(2)}) collective-permute-start(bf16[256,1024]{1,0:T(8,128)(2,1)S(1)} %copy-done.14), channel_id=1, source_target_pairs={{0,8},{4,12},{8,0},{12,4},{16,24},{20,28},{24,16},{28,20},{1,9},{5... | collective-permute-start | bytes 1572872 | tf_op jit(solution)/shard_map/ppermute | solution.py:35
  124.5 39.5 %copy-start.17 = (f32[1024,256]{1,0:T(8,128)S(1)}, f32[1024,256]{1,0:T(8,128)}, u32[]{:S(2)}) copy-start(f32[1024,256]{1,0:T(8,128)} %get-tuple-element.105) | copy-start | bytes 3145732
  124.6 36.8 %collective-permute-start.19 = (bf16[88,1024]{1,0:T(8,128)(2,1)S(1)}, bf16[88,1024]{1,0:T(8,128)(2,1)S(1)}, u32[]{:S(2)}, u32[]{:S(2)}) collective-permute-start(bf16[88,1024]{1,0:T(8,128)(2,1)S(1)} %pad_maximum_fusion.1), channel_id=1, source_target_pairs={{0,8},{4,12},{8,0},{12,4},{16,24},{20,28},{24,16},{28,20},{1,9},{5... | collective-permute-start | bytes 540680 | tf_op jit(solution)/shard_map/ppermute | solution.py:35
  155.7 32.5 %collective-permute-start.11 = (bf16[2,2,256,512]{3,2,1,0:T(8,128)(2,1)S(1)}, bf16[2,2,256,512]{3,2,1,0:T(8,128)(2,1)S(1)}, u32[]{:S(2)}, u32[]{:S(2)}) collective-permute-start(bf16[2,2,256,512]{3,2,1,0:T(8,128)(2,1)S(1)} %copy-done.16), channel_id=1, source_target_pairs={{0,1},{1,0},{2,3},{3,2},{4,5},{5,4},{6,7},{7,6},{8,9},{9,8},{10,11... | collective-permute-start | bytes 3145736 | tf_op jit(solution)/shard_map/ppermute | solution.py:35
  161.0 26.0 %copy-start.19 = (f32[256,1024]{1,0:T(8,128)S(1)}, f32[256,1024]{1,0:T(8,128)}, u32[]{:S(2)}) copy-start(f32[256,1024]{1,0:T(8,128)} %get-tuple-element.96) | copy-start | bytes 3145732
  161.0 27.1 %copy-start.23 = (bf16[256,1024]{1,0:T(8,128)(2,1)}, bf16[256,1024]{1,0:T(8,128)(2,1)S(1)}, u32[]{:S(2)}) copy-start(bf16[256,1024]{1,0:T(8,128)(2,1)S(1)} %collective-permute-done.21.r1) | copy-start | bytes 1572868
  161.1 26.0 %collective-permute-start.26 = (bf16[256,1024]{1,0:T(8,128)(2,1)}, bf16[256,1024]{1,0:T(8,128)(2,1)S(1)}, u32[]{:S(2)}, u32[]{:S(2)}) collective-permute-start(bf16[256,1024]{1,0:T(8,128)(2,1)} %get-tuple-element.97), channel_id=1, source_target_pairs={{0,16},{4,20},{8,24},{12,28},{16,0},{20,4},{24,8},{28,12},{1,17},{... | collective-permute-start | bytes 1572872 | tf_op jit(solution)/shard_map/ppermute | solution.py:35
  161.4 27.6 %collective-permute-start.23 = (bf16[256,1024]{1,0:T(8,128)(2,1)S(1)}, bf16[256,1024]{1,0:T(8,128)(2,1)S(1)}, u32[]{:S(2)}, u32[]{:S(2)}) collective-permute-start(bf16[256,1024]{1,0:T(8,128)(2,1)S(1)} %collective-permute-done.21.r1), channel_id=1, source_target_pairs={{0,4},{4,0},{8,12},{12,8},{16,20},{20,16},{24,28},{28,24},{1,5},{5... | collective-permute-start | bytes 1572872 | tf_op jit(solution)/shard_map/ppermute | solution.py:35
  162.6 34.3 %collective-permute-start.20 = (bf16[168,1024]{1,0:T(8,128)(2,1)S(1)}, bf16[168,1024]{1,0:T(8,128)(2,1)S(1)}, u32[]{:S(2)}, u32[]{:S(2)}) collective-permute-start(bf16[168,1024]{1,0:T(8,128)(2,1)S(1)} %pad_maximum_fusion), channel_id=1, source_target_pairs={{0,4},{4,0},{8,12},{12,8},{16,20},{20,16},{24,28},{28,24},{1,5},{5... | collective-permute-start | bytes 1032200 | tf_op jit(solution)/shard_map/ppermute | solution.py:35
  187.0 15.6 %collective-permute-start.28 = (bf16[1024,256]{1,0:T(8,128)(2,1)S(1)}, bf16[1024,256]{1,0:T(8,128)(2,1)S(1)}, u32[]{:S(2)}, u32[]{:S(2)}) collective-permute-start(bf16[1024,256]{1,0:T(8,128)(2,1)S(1)} %fusion), channel_id=1, source_target_pairs={{0,8},{4,12},{8,0},{12,4},{16,24},{20,28},{24,16},{28,20},{1,9},{5... | collective-permute-start | bytes 1572872 | tf_op jit(solution)/shard_map/ppermute | solution.py:35
  187.0 15.6 %copy-start.15 = (f32[1024,256]{1,0:T(8,128)S(1)}, f32[1024,256]{1,0:T(8,128)}, u32[]{:S(2)}) copy-start(f32[1024,256]{1,0:T(8,128)} %get-tuple-element.103) | copy-start | bytes 3145732
  188.3 15.7 %copy-start.26 = (f32[256,512]{1,0:T(8,128)S(1)}, f32[256,512]{1,0:T(8,128)}, u32[]{:S(2)}) copy-start(f32[256,512]{1,0:T(8,128)} %get-tuple-element.87) | copy-start | bytes 1572868
  188.3 15.7 %copy-start.27 = (f32[256,512]{1,0:T(8,128)S(1)}, f32[256,512]{1,0:T(8,128)}, u32[]{:S(2)}) copy-start(f32[256,512]{1,0:T(8,128)} %get-tuple-element.88) | copy-start | bytes 1572868
  188.3 15.7 %copy-start.28 = (f32[256,512]{1,0:T(8,128)S(1)}, f32[256,512]{1,0:T(8,128)}, u32[]{:S(2)}) copy-start(f32[256,512]{1,0:T(8,128)} %get-tuple-element.90) | copy-start | bytes 1572868
  188.4 15.5 %collective-permute-start.12 = (bf16[2,256,512]{2,1,0:T(8,128)(2,1)S(1)}, bf16[2,256,512]{2,1,0:T(8,128)(2,1)S(1)}, u32[]{:S(2)}, u32[]{:S(2)}) collective-permute-start(bf16[2,256,512]{2,1,0:T(8,128)(2,1)S(1)} %fusion.2), channel_id=1, source_target_pairs={{0,2},{1,3},{2,0},{3,1},{4,6},{5,7},{6,4},{7,5},{8,10},{9,11},{10,... | collective-permute-start | bytes 1572872 | tf_op jit(solution)/shard_map/ppermute | solution.py:35
  195.2 24.8 %collective-permute-start.24 = (bf16[256,1024]{1,0:T(8,128)(2,1)}, bf16[256,1024]{1,0:T(8,128)(2,1)S(1)}, u32[]{:S(2)}, u32[]{:S(2)}) collective-permute-start(bf16[256,1024]{1,0:T(8,128)(2,1)} %get-tuple-element.95), channel_id=1, source_target_pairs={{0,16},{4,20},{8,24},{12,28},{16,0},{20,4},{24,8},{28,12},{1,17},{... | collective-permute-start | bytes 1572872 | tf_op jit(solution)/shard_map/ppermute | solution.py:35
  203.9 16.1 %copy-start.18 = (f32[256,1024]{1,0:T(8,128)S(1)}, f32[256,1024]{1,0:T(8,128)}, u32[]{:S(2)}) copy-start(f32[256,1024]{1,0:T(8,128)} %get-tuple-element.94) | copy-start | bytes 3145732
  (10 other events, 33.8 us)

commit v2 on v1

--- a/solution.py
+++ b/solution.py
@@ -67,6 +67,20 @@
     for bit in bits[:-1]:
         value = value + swap(value, axis, bit)
     return value, swap(value, axis, bits[-1])
+
+
+def after(values, pins):
+    def nothing(*refs):
+        pass
+
+    return pl.pallas_call(
+        nothing,
+        in_specs=[ANY] * (len(values) + len(pins)),
+        out_specs=[ANY] * len(values),
+        out_shape=[jax.ShapeDtypeStruct(value.shape, value.dtype) for value in values],
+        input_output_aliases={i: i for i in range(len(values))},
+        name="after",
+    )(*values, *pins)
 
 
 def in_hbm(value):
@@ -121,10 +135,16 @@
             size = width // blocked
             for p in range(blocked):
                 cols = pl.ds(pl.multiple_of((place[0] ^ p) * size, size), size)
-                dest = far.at[p & 1] if p & 2 else (near if p & 1 else own)
+                dest = near.at[p >> 1 & 1] if p & 1 else (far if p & 2 else own)
                 dest[:, (p // 4) * size : (p // 4 + 1) * size] = normed[:, cols]
                 at = (p & 1) * 2 + (p >> 1 & 1)
-                (up_far if p & 4 else up_own)[:, at * size : (at + 1) * size] = up[:, cols]
+                at = slice(at * size, (at + 1) * size)
+                if p & 4:
+                    half = rows // 2
+                    some = pl.ds(pl.multiple_of((place[1] & 1) * half, half), half)
+                    up_far[:, at] = up[some, cols]
+                else:
+                    up_own[:, at] = up[:, cols]
 
 
 def front(
@@ -142,7 +162,8 @@
     shapes = []
     if blocked:
         quarter, half = width // 4, width // 2
-        shapes = [(2, rows, quarter), (rows, quarter), (rows, quarter), (rows, half), (rows, half)]
+        shapes = [(rows, quarter), (2, rows, quarter), (rows, quarter), (rows // 2, half)]
+        shapes += [(rows, half)]
     return pl.pallas_call(
         functools.partial(front_kernel, blocked),
         grid=(inner // blk,),
@@ -213,7 +234,7 @@
             pl.BlockSpec((blk, width), lambda i: (i, 0)),
         ],
         out_specs=[cols(rows)] * 3,
-        out_shape=[jax.ShapeDtypeStruct((rows, inner), F32)] * 3,
+        out_shape=[jax.ShapeDtypeStruct((rows, inner), F32)] * 2 + [pltpu.HBM((rows, inner), F32)],
         compiler_params=pltpu.CompilerParams(vmem_limit_bytes=24 * MIB),
         name="gate",
     )(in_hbm(normed), in_hbm(upstream_b), in_hbm(w_z), in_hbm(w_out))
@@ -334,12 +355,12 @@
         scratch_shapes=[pltpu.VMEM((rows * SUB, LANES), F32)] * 3
         + [
             pltpu.VMEM((2 * states * rows, LANES), F32),
-            pltpu.VMEM((2, rows // 8, states, SUB, LANES), F32),
+            pltpu.VMEM((2, rows // 4, states, SUB, LANES), F32),
             pltpu.SemaphoreType.DMA((2,)),
         ],
-        compiler_params=pltpu.CompilerParams(vmem_limit_bytes=22 * MIB),
+        compiler_params=pltpu.CompilerParams(vmem_limit_bytes=26 * MIB),
         name="scan",
-    )(*summed, mixed, in_hbm(w_up), in_hbm(beta_bias[None]), silu, dgate, in_hbm(skip_gain[None]))
+    )(*summed, in_hbm(mixed), in_hbm(w_up), in_hbm(beta_bias[None]), silu, dgate, in_hbm(skip_gain[None]))
 
 
 def back_kernel(
@@ -496,13 +517,13 @@
             pltpu.VMEM((unroll * 2 * states * SUB, LANES), F32),
             pltpu.VMEM((states * span, LANES), F32),
             pltpu.VMEM((states * span, LANES), F32),
-            pltpu.VMEM((2, rows // 8, states, SUB, LANES), F32),
+            pltpu.VMEM((2, rows // 4, states, SUB, LANES), F32),
             pltpu.SemaphoreType.DMA((2,)),
         ],
-        compiler_params=pltpu.CompilerParams(vmem_limit_bytes=28 * MIB),
+        compiler_params=pltpu.CompilerParams(vmem_limit_bytes=32 * MIB),
         name="back",
     )(
-        place, *summed, mixed, in_hbm(w_up), step_in, raw, gy,
+        place, *summed, in_hbm(mixed), in_hbm(w_up), step_in, raw, in_hbm(gy),
         in_hbm(hist), last, peak, *pins,
     )
 
@@ -511,56 +532,62 @@
     pins, parts, place, one, two, grad_one, grad_two, mixed, gy, gmix, dsilu, prex, ups, cw, skip,
     wd, wk, *rest,
 ):
-    prex_b, keep, send, table = rest[pins:]
-    rows, inner = mixed.shape
+    prex_b, keep, send, table, keys, ranks, top = rest[pins:]
+    step = pl.program_id(0)
+    rows, blk = mixed.shape
     rank = wd.shape[1]
     count = wk.shape[0]
-    states = count // 2
-    high = (grad_one.shape[0] - rows) * LANES // rows
-    kq = key_query_of(one, two, rows, count)
-    gkq = key_query_of(grad_one, grad_two, rows, high)
-    norm_grad = gkq[:, count : count + 1]
-    peak = jnp.max(gkq[:, count + 1 : count + 2], axis=0, keepdims=True)
+
+    @pl.when(step == 0)
+    def _():
+        high = (grad_one.shape[0] - rows) * LANES // rows
+        kq = key_query_of(one, two, rows, count)
+        gkq = key_query_of(grad_one, grad_two, rows, high)
+        norm_grad = gkq[:, count : count + 1]
+        lane = lax.broadcasted_iota(jnp.int32, (rows, count), 1)
+        by_norm = jnp.where(lane < count // 2, 2.0 * kq * norm_grad, 0.0)
+        keys[...] = (gkq[:, :count] + by_norm).astype(BF16)
+        ranks[...] = (grad_one[:rows, :] + grad_two[:rows, :]).astype(BF16)
+        peak = jnp.max(gkq[:, count + 1 : count + 2], axis=0, keepdims=True)
+        top[...] = jnp.broadcast_to(peak, top.shape)
+
+    kq_b = keys[...]
+    rank_b = ranks[...]
+    peak = top[0:1, 0:1]
     peak_high = peak.astype(BF16).astype(F32)
-    lane = lax.broadcasted_iota(jnp.int32, (rows, count), 1)
-    kq_b = (gkq[:, :count] + jnp.where(lane < states, 2.0 * kq * norm_grad, 0.0)).astype(BF16)
-    rank_b = (grad_one[:rows, :] + grad_two[:rows, :]).astype(BF16)
     taps = cw.shape[0]
-    blk = 256
     first = 2 * rank + count
     table[:rank, :] = ups[:rank, :]
     table[rank : 2 * rank, :] = mm_tn(rank_b, mixed[...])
     table[2 * rank : first, :] = mm_tn(kq_b, mixed[...])
-    for c in range(inner // blk):
-        at = slice(c * blk, (c + 1) * blk)
-        mix = mixed[:, at].astype(F32)
-        grad_y = gy[:, at]
-        total = grad_y * skip[:, at] + gmix[:, at]
-        total = total + mm(kq_b, wk[:, at]) + mm_nt(rank_b, wd[at, :])
-        grad = total * dsilu[:, at]
-        pre = prex[:, at]
-        row = lax.broadcasted_iota(jnp.int32, grad.shape, 0)
-        out = None
-        sums = []
-        for j in range(taps):
-            by = taps - 1 - j
-            sums.append(jnp.sum(grad * shifted(pre, by, row), axis=0, keepdims=True))
-            term = cw[j : j + 1, at] * shifted(grad, -by, row)
-            out = term if out is None else out + term
-        sums.append(jnp.sum(grad, axis=0, keepdims=True))
-        sums.append(jnp.sum(grad_y * mix, axis=0, keepdims=True))
-        sums.append(ups[rank : rank + 1, at])
-        channel = lax.broadcasted_iota(jnp.int32, (1, blk), 1) + c * blk
-        for value in (peak_high, peak - peak_high):
-            sums.append(jnp.where(channel == place[0], jnp.broadcast_to(value, (1, blk)), 0.0))
-        for i, line in enumerate(sums):
-            table[first + i : first + i + 1, at] = line
-        prex_b[:, at] = out.astype(BF16)
-    table[first + len(sums) :, :] = jnp.zeros((table.shape[0] - first - len(sums), inner), F32)
-    size = table.shape[0] // parts
+    mix = mixed[...].astype(F32)
+    grad_y = gy[...]
+    total = grad_y * skip[...] + gmix[...]
+    total = total + mm(kq_b, wk[...]) + mm_nt(rank_b, wd[...])
+    grad = total * dsilu[...]
+    pre = prex[...]
+    row = lax.broadcasted_iota(jnp.int32, grad.shape, 0)
+    out = None
+    sums = []
+    for j in range(taps):
+        by = taps - 1 - j
+        sums.append(jnp.sum(grad * shifted(pre, by, row), axis=0, keepdims=True))
+        term = cw[j : j + 1, :] * shifted(grad, -by, row)
+        out = term if out is None else out + term
+    sums.append(jnp.sum(grad, axis=0, keepdims=True))
+    sums.append(jnp.sum(grad_y * mix, axis=0, keepdims=True))
+    sums.append(ups[rank : rank + 1, :])
+    channel = lax.broadcasted_iota(jnp.int32, (1, blk), 1) + step * blk
+    for value in (peak_high, peak - peak_high):
+        sums.append(jnp.where(channel == place[0], jnp.broadcast_to(value, (1, blk)), 0.0))
+    for i, line in enumerate(sums):
+        table[first + i : first + i + 1, :] = line
+    table[first + len(sums) :, :] = jnp.zeros((table.shape[0] - first - len(sums), blk), F32)
+    prex_b[...] = out.astype(BF16)
     if parts != 8:
         keep[...] = table[...]
         return
+    size = table.shape[0] // parts
     for dest, order in ((keep, (0, 4, 2, 6)), (send, (1, 5, 3, 7))):
         for i, p in enumerate(order):
             at = pl.ds(pl.multiple_of((place[0] ^ p) * size, SUB), size)
@@ -572,60 +599,49 @@
     w_keyq, parts, pins,
 ):
     rows, inner = mixed.shape
-    table = (8 * SMALL, inner)
-    half = (4, SMALL, inner) if parts == 8 else table
+    rank, count = w_down.shape[1], w_keyq.shape[0]
+    blk = min(inner, 256)
+    high = 8 * SMALL
+    whole = lambda value: pl.BlockSpec(value.shape, lambda i: (0,) * value.ndim)
+    cols = lambda height: pl.BlockSpec((height, blk), lambda i: (0, i))
+    if parts == 8:
+        half = (4, SMALL, inner)
+        half_spec = pl.BlockSpec((4, SMALL, blk), lambda i: (0, 0, i))
+    else:
+        half = (high, inner)
+        half_spec = cols(high)
     return pl.pallas_call(
         functools.partial(conv_kernel, len(pins), parts),
-        in_specs=[pl.BlockSpec(memory_space=pltpu.SMEM)] + [WHOLE] * 14 + [ANY] * len(pins),
-        out_specs=[WHOLE] * 3,
+        grid=(inner // blk,),
+        in_specs=[pl.BlockSpec(memory_space=pltpu.SMEM)]
+        + [whole(value) for value in (*summed, *grads)]
+        + [cols(rows)] * 5
+        + [cols(ups.shape[0]), cols(conv_weight.shape[0]), cols(1)]
+        + [pl.BlockSpec((blk, rank), lambda i: (i, 0)), cols(count)]
+        + [ANY] * len(pins),
+        out_specs=[cols(rows), half_spec, half_spec],
         out_shape=[
             pltpu.HBM((rows, inner), BF16),
             pltpu.HBM(half, F32),
             pltpu.HBM(half, BF16),
         ],
-        scratch_shapes=[pltpu.VMEM(table, F32)],
+        scratch_shapes=[
+            pltpu.VMEM((high, blk), F32),
+            pltpu.VMEM((rows, count), BF16),
+            pltpu.VMEM((rows, rank), BF16),
+            pltpu.VMEM((SUB, LANES), F32),
+        ],
         compiler_params=pltpu.CompilerParams(vmem_limit_bytes=26 * MIB),
         name="conv",
     )(
-        place, *summed, *grads, mixed, gy, gmix, dsilu, prex, ups, in_hbm(conv_weight),
-        in_hbm(skip_gain[None]), in_hbm(w_down), in_hbm(w_keyq), *pins,
-    )
-
-
-def unpack_kernel(place, rank, count, taps, g0, g1, g2, g3, up, down, keyq, lines, table):
-    size = g0.shape[0]
-    pieces = [(0, g0, 0), (4, g1, 0), (2, g2, 0), (6, g2, 1)]
-    pieces += [(p, g3, i) for i, p in enumerate((1, 5, 3, 7))]
-    for p, source, i in pieces:
-        at = pl.ds(pl.multiple_of((place[0] ^ p) * size, SUB), size)
-        table[at, :] = source[i * size : (i + 1) * size, :].astype(F32)
-    up[...] = table[:rank, :]
-    down[...] = jnp.transpose(table[rank : 2 * rank, :])
-    keyq[...] = table[2 * rank : 2 * rank + count, :]
-    first = 2 * rank + count
-    lines[...] = table[first : first + lines.shape[0], :]
-
-
-def unpack(place, pieces, rank, count, taps):
-    inner = pieces[0].shape[1]
-    kernel = lambda place, *refs: unpack_kernel(place, rank, count, taps, *refs)
-    return pl.pallas_call(
-        kernel,
-        in_specs=[pl.BlockSpec(memory_space=pltpu.SMEM)] + [WHOLE] * 4,
-        out_specs=[WHOLE] * 4,
-        out_shape=[
-            jax.ShapeDtypeStruct((rank, inner), F32),
-            jax.ShapeDtypeStruct((inner, rank), F32),
-            jax.ShapeDtypeStruct((count, inner), F32),
-            jax.ShapeDtypeStruct((2 * SUB, inner), F32),
-        ],
-        scratch_shapes=[pltpu.VMEM((8 * SMALL, inner), F32)],
-        compiler_params=pltpu.CompilerParams(vmem_limit_bytes=16 * MIB),
-        name="unpack",
-    )(place, *pieces)
-
-
-def branch_kernel(place, gated, wo, tok, send, keep):
+        place, *summed, *grads, in_hbm(mixed), in_hbm(gy), in_hbm(gmix), in_hbm(dsilu),
+        in_hbm(prex), in_hbm(ups), in_hbm(conv_weight), in_hbm(skip_gain[None]), in_hbm(w_down),
+        in_hbm(w_keyq), *pins,
+    )
+
+
+def branch_kernel(pins, place, gated, wo, tok, *rest):
+    send, keep = rest[pins:]
     i = pl.program_id(0)
     value = mm(gated[...], wo[...])
 
@@ -642,12 +658,12 @@
         send[0, 0] = value.astype(BF16)
 
 
-def branch(place, gated, w_out, tokens, parts):
+def branch(place, gated, w_out, tokens, parts, pins):
     rows, inner = gated.shape
     width = w_out.shape[1]
     own = width // parts
     return pl.pallas_call(
-        branch_kernel,
+        functools.partial(branch_kernel, len(pins)),
         grid_spec=pltpu.PrefetchScalarGridSpec(
             num_scalar_prefetch=1,
             grid=(parts,),
@@ -655,7 +671,8 @@
                 pl.BlockSpec((rows, inner), lambda i, place: (0, 0)),
                 pl.BlockSpec((inner, own), lambda i, place: (0, place[1] ^ i)),
                 pl.BlockSpec((rows, own), lambda i, place: (0, place[1])),
-            ],
+            ]
+            + [ANY] * len(pins),
             out_specs=[
                 pl.BlockSpec((1, 1, rows, own), lambda i, place: (i // 2, 0, 0, 0)),
                 pl.BlockSpec((1, rows, own), lambda i, place: (i // 2, 0, 0)),
@@ -667,13 +684,18 @@
         ],
         compiler_params=pltpu.CompilerParams(vmem_limit_bytes=16 * MIB),
         name="branch",
-    )(place, in_hbm(gated), in_hbm(w_out), in_hbm(tokens))
+    )(place, in_hbm(gated), in_hbm(w_out), in_hbm(tokens), *pins)
 
 
 def input_kernel(
-    place, ids, weights, half_sent, prex, prez, wx, wz, tok, tok_own, cot, gain,
-    send, keep, stats, slope, shift, base, inv, dots,
+    pins, extra, place, ids, weights, half_sent, prex, prez, wx, wz, tok, tok_own, cot, gain, *rest
 ):
+    if extra:
+        keep_z, come_z = rest[:2]
+        grad_z = rest[pins + 2 + 6]
+        grad_z[...] = keep_z[...] + come_z[...].astype(F32)
+        rest = rest[2 : pins + 2 + 6] + rest[pins + 2 + 7 :]
+    send, keep, stats, slope, shift, base, inv, dots = rest[pins:]
     i = pl.program_id(0)
     rows, width = tok.shape
 
@@ -719,7 +741,7 @@
 
 def input_grad(
     place, group_ids, group_weights, half_sent, prex, prez, w_x, w_z, tokens, cotangent, norm_gain,
-    parts,
+    parts, extra, pins,
 ):
     rows, inner = prex.shape
     width = tokens.shape[1]
@@ -728,9 +750,12 @@
     part = pl.BlockSpec((own, inner), lambda i, place: (place[1] ^ i, 0))
     mine = pl.BlockSpec((rows, own), lambda i, place: (0, 0))
     smem = pl.BlockSpec(memory_space=pltpu.SMEM)
+    strip = lambda value: pl.BlockSpec(
+        (value.shape[0] // parts, value.shape[1]), lambda i, place: (i, 0)
+    )
     stat_rows = rows // LANES + width // LANES
     return pl.pallas_call(
-        input_kernel,
+        functools.partial(input_kernel, len(pins), len(extra)),
         grid_spec=pltpu.PrefetchScalarGridSpec(
             num_scalar_prefetch=1,
             grid=(parts,),
@@ -746,12 +771,15 @@
                 pl.BlockSpec((rows, own), lambda i, place: (0, place[1] ^ i)),
                 pl.BlockSpec((rows, own), lambda i, place: (0, place[1])),
                 pl.BlockSpec((1, own), lambda i, place: (0, place[1] ^ i)),
-            ],
+            ]
+            + [strip(value) for value in extra]
+            + [ANY] * len(pins),
             out_specs=[
                 pl.BlockSpec((1, 1, rows, own), lambda i, place: (i // 2, 1, 0, 0)),
                 pl.BlockSpec((1, rows, own), lambda i, place: (i // 2, 0, 0)),
             ]
-            + [whole((stat_rows, LANES)), mine, mine, mine],
+            + [whole((stat_rows, LANES)), mine, mine, mine]
+            + [strip(value) for value in extra[:1]],
             scratch_shapes=[pltpu.VMEM((rows, LANES), F32)] * 2,
         ),
         out_shape=[
@@ -759,52 +787,214 @@
             pltpu.HBM((parts // 2, rows, own), F32),
             jax.ShapeDtypeStruct((stat_rows, LANES), F32),
         ]
-        + [pltpu.HBM((rows, own), F32)] * 3,
+        + [pltpu.HBM((rows, own), F32)] * 3
+        + [jax.ShapeDtypeStruct(value.shape, F32) for value in extra[:1]],
         compiler_params=pltpu.CompilerParams(vmem_limit_bytes=24 * MIB),
         input_output_aliases={3: 0},
         name="inputs",
     )(
         place, group_ids, group_weights, in_hbm(half_sent), in_hbm(prex), in_hbm(prez), in_hbm(w_x), in_hbm(w_z), in_hbm(tokens),
-        in_hbm(tokens), in_hbm(cotangent), in_hbm(norm_gain[None]),
-    )
-
-
-def out_weight_kernel(pins, l0, l1, r0, r1, *rest):
-    keep, later, send = rest[pins:]
-    own = keep.shape[1]
-    total = mm_tn(l0[...], r0[...]) + mm_tn(l1[...], r1[...])
-    keep[...] = total[:, :own]
+        in_hbm(tokens), in_hbm(cotangent), in_hbm(norm_gain[None]), *extra, *pins,
+    )
+
+
+def middle_kernel(
+    place, gated, gated_far, up_own, up_a, up_b, every, wo, tok, small, small_come, *rest
+):
+    keep_out, later, send_out, send, keep, small_keep, small_send = rest[len(rest) - 7 :]
+    i = pl.program_id(0)
+
+    @pl.when(i == 0)
+    def _():
+        for j in range(2):
+            small_keep[j] = small[j] + small_come[j].astype(F32)
+            small_send[j] = (small[2 + j] + small_come[2 + j].astype(F32)).astype(BF16)
+
+    rows = gated.shape[0]
+    half = rows // 2
+    first = (place[1] & 1) * half
+    own = keep_out.shape[1]
+    total = mm_tn(gated[...], up_own[...])
+    total = total + mm_tn(gated_far[pl.ds(pl.multiple_of(first, half), half), :], up_a[...])
+    other = pl.ds(pl.multiple_of(half - first, half), half)
+    total = total + mm_tn(gated_far[other, :], up_b[...])
+    keep_out[...] = total[:, :own]
     later[...] = total[:, own : 2 * own]
-    send[...] = total[:, 2 * own :].astype(BF16)
-
-
-def out_weight(lefts, rights, pins):
-    rows, inner = lefts[0].shape
-    own = rights[0].shape[1] // 4
-    blk = 256
-    whole = lambda value: pl.BlockSpec(value.shape, lambda i: (0,) * value.ndim)
-    down = lambda wide: pl.BlockSpec((blk, wide), lambda i: (i, 0))
+    send_out[...] = total[:, 2 * own :].astype(BF16)
+
+    value = mm(every[...], wo[...])
+
+    @pl.when(i == 0)
+    def _():
+        keep[0] = value + tok[...].astype(F32)
+
+    @pl.when(i == 2)
+    def _():
+        keep[0] = value
+
+    @pl.when(i % 2 == 1)
+    def _():
+        send[0, 0] = value.astype(BF16)
+
+
+def middle(place, gated, gated_far, ups, w_out, tokens, small, small_come, parts, pins):
+    rows, inner = gated.shape
+    width = w_out.shape[1]
+    own = width // parts
+    blk = inner // parts
+    out = ups[0].shape[1] // 4
+    whole = lambda value: pl.BlockSpec(value.shape, lambda i, place: (0,) * value.ndim)
+    cols = pl.BlockSpec((rows, blk), lambda i, place: (0, i))
+    down = lambda wide: pl.BlockSpec((blk, wide), lambda i, place: (i, 0))
     return pl.pallas_call(
-        functools.partial(out_weight_kernel, len(pins)),
-        grid=(inner // blk,),
-        in_specs=[pl.BlockSpec((rows, blk), lambda i: (0, i))] * 2
-        + [whole(r) for r in rights]
-        + [ANY] * len(pins),
-        out_specs=[down(own), down(own), down(2 * own)],
+        middle_kernel,
+        grid_spec=pltpu.PrefetchScalarGridSpec(
+            num_scalar_prefetch=1,
+            grid=(parts,),
+            in_specs=[cols, cols]
+            + [whole(value) for value in (*ups, gated)]
+            + [
+                pl.BlockSpec((inner, own), lambda i, place: (0, place[1] ^ i)),
+                pl.BlockSpec((rows, own), lambda i, place: (0, place[1])),
+                whole(small),
+                whole(small_come),
+            ]
+            + [ANY] * len(pins),
+            out_specs=[
+                down(out),
+                down(out),
+                down(2 * out),
+                pl.BlockSpec((1, 1, rows, own), lambda i, place: (i // 2, 0, 0, 0)),
+                pl.BlockSpec((1, rows, own), lambda i, place: (i // 2, 0, 0)),
+            ]
+            + [pl.BlockSpec((2, SMALL, inner), lambda i, place: (0, 0, 0))] * 2,
+        ),
         out_shape=[
-            pltpu.HBM((inner, own), F32),
-            pltpu.HBM((inner, own), F32),
-            pltpu.HBM((inner, 2 * own), BF16),
+            pltpu.HBM((inner, out), F32),
+            pltpu.HBM((inner, out), F32),
+            pltpu.HBM((inner, 2 * out), BF16),
+            pltpu.HBM((parts // 2, 2, rows, own), BF16),
+            pltpu.HBM((parts // 2, rows, own), F32),
+            pltpu.HBM((2, SMALL, inner), F32),
+            pltpu.HBM((2, SMALL, inner), BF16),
         ],
-        compiler_params=pltpu.CompilerParams(vmem_limit_bytes=20 * MIB),
-        name="outw",
-    )(*[in_hbm(value) for value in (*lefts, *rights)], *pins)
-
-
-def in_weight_kernel(l0, l1, l2, l3, r0, r1, r2, r3, keep, send):
+        compiler_params=pltpu.CompilerParams(vmem_limit_bytes=36 * MIB),
+        name="middle",
+    )(
+        place, in_hbm(gated), gated_far, *ups, in_hbm(gated), in_hbm(w_out), in_hbm(tokens),
+        in_hbm(small), small_come, *pins,
+    )
+
+
+def finale_kernel(
+    rank, count, place, keep_x, come_x, keep_out, come_out, far_out, keep_a, keep_b, come_a,
+    come_b, far_a, far_b, stats, slope, shift, base, g0, g2, g3,
+    grad_x, grad_out, block, grad_in, up, down, keyq, conv, *rest,
+):
+    lines = rest[:3]
+    top, table, dots = rest[3:]
+    i = pl.program_id(0)
+
+    @pl.when(i == 0)
+    def _():
+        tall = jnp.transpose(jnp.concatenate([stats[...]] * (SUB // stats.shape[0]), axis=0))
+        for c in range(stats.shape[0]):
+            dots[c * LANES : (c + 1) * LANES, :] = jnp.broadcast_to(
+                tall[:, c : c + 1], (LANES, LANES)
+            )
+
+    grad_x[...] = keep_x[...] + come_x[...].astype(F32)
+    grad_out[...] = keep_out[...] + come_out[...].astype(F32) + far_out[...].astype(F32)
+    value = keep_a[0] + come_a[0, 0].astype(F32) + far_a[0].astype(F32)
+    block[...] = value.astype(BF16)
+    value = keep_b[0] + come_b[0, 0].astype(F32) + far_b[0].astype(F32)
+    some = value.shape[0]
+    dot = dots[pl.ds(pl.multiple_of(i * some, some), some), :][:, 0:1]
+    grad_in[...] = value * slope[...] - shift[...] * dot + base[...]
+
+    @pl.when(i == pl.num_programs(0) - 1)
+    def _():
+        size = g0.shape[0] // 2
+        pieces = [(0, g0, 0), (4, g0, 1), (2, g2, 0), (6, g2, 1)]
+        pieces += [(p, g3, i) for i, p in enumerate((1, 5, 3, 7))]
+        for p, source, i in pieces:
+            at = pl.ds(pl.multiple_of((place[0] ^ p) * size, SUB), size)
+            table[at, :] = source[i * size : (i + 1) * size, :].astype(F32)
+        up[...] = table[:rank, :]
+        down[...] = jnp.transpose(table[rank : 2 * rank, :])
+        keyq[...] = table[2 * rank : 2 * rank + count, :]
+        first = 2 * rank + count
+        conv[...] = table[first : first + conv.shape[0], :]
+        first += conv.shape[0]
+        for i, line in enumerate(lines):
+            line[...] = table[first + i : first + i + 1, :]
+        tops = table[first + len(lines) : first + len(lines) + 1, :]
+        tops = tops + table[first + len(lines) + 1 : first + len(lines) + 2, :]
+        top[...] = jnp.broadcast_to(jnp.max(tops, axis=1, keepdims=True), top.shape)
+
+
+def finale(
+    place, keep_x, come_x, keep_out, come_out, far_out, out_keep, keep, come, far, stats, slope,
+    shift, base, pieces, rank, count, taps,
+):
+    size, inner = keep_x.shape
+    rows, own = slope.shape
+    steps = 4
+    whole = lambda shape: pl.BlockSpec(shape, lambda i: (0,) * len(shape))
+    strip = lambda high, wide: pl.BlockSpec((high // steps, wide), lambda i: (i, 0))
+    kept = pl.BlockSpec((1, rows // steps, own), lambda i: (0, i, 0))
+    came = lambda j: pl.BlockSpec((1, 1, rows // steps, own), lambda i: (0, j, i, 0))
+    last = lambda j: pl.BlockSpec((1, rows // steps, own), lambda i: (j, i, 0))
+    out = keep_out.shape[1]
+    return pl.pallas_call(
+        functools.partial(finale_kernel, rank, count),
+        grid=(steps,),
+        in_specs=[pl.BlockSpec(memory_space=pltpu.SMEM)]
+        + [strip(size, inner)] * 2
+        + [strip(inner, out)] * 3
+        + [kept, kept, came(0), came(1), last(0), last(1)]
+        + [whole(stats.shape)]
+        + [strip(rows, own)] * 3
+        + [whole(piece.shape) for piece in pieces],
+        out_specs=[
+            strip(size, inner),
+            strip(inner, out),
+            strip(rows, own),
+            strip(rows, own),
+            whole((rank, inner)),
+            whole((inner, rank)),
+            whole((count, inner)),
+            whole((taps, inner)),
+            *[whole((1, inner))] * 3,
+            whole((SUB, LANES)),
+        ],
+        out_shape=[
+            jax.ShapeDtypeStruct((size, inner), F32),
+            jax.ShapeDtypeStruct((inner, out), F32),
+            jax.ShapeDtypeStruct((rows, own), BF16),
+            jax.ShapeDtypeStruct((rows, own), F32),
+            jax.ShapeDtypeStruct((rank, inner), F32),
+            jax.ShapeDtypeStruct((inner, rank), F32),
+            jax.ShapeDtypeStruct((count, inner), F32),
+            jax.ShapeDtypeStruct((taps, inner), F32),
+            *[jax.ShapeDtypeStruct((1, inner), F32)] * 3,
+            jax.ShapeDtypeStruct((SUB, LANES), F32),
+        ],
+        scratch_shapes=[pltpu.VMEM((8 * SMALL, inner), F32), pltpu.VMEM((rows, LANES), F32)],
+        compiler_params=pltpu.CompilerParams(vmem_limit_bytes=24 * MIB),
+        name="finale",
+    )(
+        place, in_hbm(keep_x), come_x, in_hbm(keep_out), come_out, far_out, in_hbm(out_keep),
+        in_hbm(keep), come, come, far, far, stats, in_hbm(slope), in_hbm(shift), in_hbm(base),
+        *pieces,
+    )
+
+
+def in_weight_kernel(pins, l0, l1, l2, l3, r0, r1, r2, r3, *rest):
+    keep, send = rest[pins:]
     i = pl.program_id(0)
     total = None
-    for left, right in ((l0[...], r0), (l1[0], r1), (l2[...], r2), (l3[...], r3)):
+    for left, right in ((l0[...], r0), (l1[...], r1), (l2[0], r2), (l3[...], r3)):
         term = mm_tn(left, right[...])
         total = term if total is None else total + term
 
@@ -817,16 +1007,17 @@
         keep[...] = total
 
 
-def in_weight(lefts, rights):
+def in_weight(lefts, rights, pins):
     rows, inner = rights[0].shape
     own = lefts[0].shape[1] // 2
     whole = lambda value: pl.BlockSpec(value.shape, lambda i: (0,) * value.ndim)
     side = pl.BlockSpec((rows, own), lambda i: (0, 1 - i))
     return pl.pallas_call(
-        in_weight_kernel,
+        functools.partial(in_weight_kernel, len(pins)),
         grid=(2,),
-        in_specs=[side, pl.BlockSpec((1, rows, own), lambda i: (0, 0, 1 - i)), side, side]
-        + [whole(r) for r in rights],
+        in_specs=[side, side, pl.BlockSpec((1, rows, own), lambda i: (0, 0, 1 - i)), side]
+        + [whole(r) for r in rights]
+        + [ANY] * len(pins),
         out_specs=[pl.BlockSpec((own, inner), lambda i: (0, 0))] * 2,
         out_shape=[
             pltpu.HBM((own, inner), F32),
@@ -834,7 +1025,7 @@
         ],
         compiler_params=pltpu.CompilerParams(vmem_limit_bytes=20 * MIB),
         name="inw",
-    )(*[in_hbm(value) for value in (*lefts, *rights)])
+    )(in_hbm(lefts[0]), *lefts[1:], in_hbm(rights[0]), *rights[1:], *pins)
 
 
 def split_bits(axis):
@@ -908,13 +1099,13 @@
         conv_weight, conv_bias, w_down, keyq_t, blocked,
     )
     summed = all_but_last(part, "state")
-    pins_back = pins_conv = ()
+    pins_back = pins_conv = pins_inputs = extra = ()
     if blocked:
         far, near, own, up_far, up_own = blocks
         far = swap(far, "dp", 2)
         near = swap(near, "dp", 1)
         up_far = swap(up_far, "dp", 4)
-        pins_back = (far, near)
+        pins_back = (far, near, up_far)
     else:
         norm_parts = exchange_cols(normed, "dp")
         up_parts = exchange_cols(upstream_b, "dp")
@@ -927,35 +1118,53 @@
         gated_far = swap(gated_b, "dp", 4)
         prez_far = swap(prez_b, "dp", 2)
         prez_near = swap(prez_b, "dp", 1)
-        sides = (own, far, near, swap(far[1], "dp", 1))
-        pins_conv = (gated_far, prez_far, prez_near, up_far, sides[3])
 
     gmix, pay, ups = scan_backward(
         place, summed, mixed_b, w_up, step_size, raw, grad_y, hist, last, peak, pins_back
     )
     grads = all_but_last(pay, "state")
-    half_sent, out_keep = branch(place, gated_b, w_out, tokens, parts)
+    if blocked:
+        up_parts = (up_own, up_far, swap(up_far, "state", 1))
+        (prez_far,) = after((prez_far,), (pay,))
+        prez_last = swap(prez_far, "dp", 1)
+        sides = (own, far, near, swap(near[1], "dp", 2))
+        pins_conv = (gated_far, up_parts[2], prez_near, sides[3])
 
     prex_b, small, small_send = conv_back(
         place, summed, grads, mixed_b, grad_y, gmix, dsilu, pre_x, ups, conv_weight, skip_gain,
         w_down, keyq_t, dp_size, pins_conv,
     )
 
-    def in_grad(value, far, near):
-        pieces = (value, far, near, swap(far, "dp", 1))
-        keep, send = in_weight(sides, pieces)
-        return keep + swap(send, "dp", 4).astype(F32)
-
     if blocked:
         prex_far = swap(prex_b, "dp", 2)
         prex_near = swap(prex_b, "dp", 1)
-        keep, later, send = out_weight((gated_b, gated_far), (up_own, up_far), ())
-        come = swap(send, "dp", 1).astype(F32)
+        keep_z, send_z = in_weight(sides, (prez_b, prez_far, prez_near, prez_last), (prex_b,))
+        come_z = swap(send_z, "dp", 4)
+        keep_out, later, send_out, half_sent, out_keep, small, small_send = middle(
+            place, gated_b, gated_far, up_parts, w_out, tokens, small,
+            swap(small_send, "dp", 1), parts, (send_z, prex_far, prex_near),
+        )
+        prex_last = swap(prex_far, "dp", 1)
+        come_out = swap(send_out, "dp", 1)
+        keep_x, send_x = in_weight(
+            sides, (prex_b, prex_far, prex_near, prex_last), (send_out, come_z)
+        )
+        come_x = swap(send_x, "dp", 4)
+        (small_send,) = after((small_send,), (send_x,))
+        small = small + swap(small_send, "dp", 2).astype(F32)
+        pins_inputs = (send_x,)
+        extra = (keep_z, come_z)
+    else:
+        half_sent, out_keep = branch(place, gated_b, w_out, tokens, parts, ())
+    send, keep, stats, slope, shift, base, *grad_wz = input_grad(
+        place, group_ids, group_weights, half_sent, prex_b, prez_b, w_x, w_z, tokens, cotangent,
+        norm_gain, parts, extra, pins_inputs,
+    )
+    if blocked:
+        (grad_wz,) = grad_wz
         cut = later.shape[1]
-        come_far = swap((later + come[:, cut:]).astype(BF16), "dp", 2)
-        grad_wout = keep + come[:, :cut] + come_far.astype(F32)
-        grad_wz = in_grad(prez_b, prez_far, prez_near)
-        grad_wx = in_grad(prex_b, prex_far, prex_near)
+        far_out = swap((later + come_out[:, cut:].astype(F32)).astype(BF16), "dp", 2)
+        send, stats, small = after((send, stats, small), (come_x, come_out))
     else:
 
         def weight_grad(value, left):
@@ -967,18 +1176,16 @@
         grad_wz = weight_grad(prez_b, False)
         grad_wx = weight_grad(prex_b, False)
 
-    send, keep, stats, slope, shift, base = input_grad(
-        place, group_ids, group_weights, half_sent, prex_b, prez_b, w_x, w_z, tokens, cotangent,
-        norm_gain, parts,
-    )
     come = swap(send, "state", 1)
     pair = jnp.stack([out_keep[1], keep[1]]) + come[1].astype(F32)
-    come_far = swap(pair.astype(BF16), "state", 2).astype(F32)
-    block_out = (out_keep[0] + come[0, 0].astype(F32) + come_far[0]).astype(BF16)
-    norm_grad = keep[0] + come[0, 1].astype(F32) + come_far[1]
+    come_far = swap(pair.astype(BF16), "state", 2)
     stats = all_sum(stats, "state")
-    row_stat = stats[: rows // LANES].reshape(rows, 1)
-    grad_in = norm_grad * slope - shift * row_stat + base
+    if not blocked:
+        block_out = out_keep[0] + come[0, 0].astype(F32) + come_far[0].astype(F32)
+        block_out = block_out.astype(BF16)
+        norm_grad = keep[0] + come[0, 1].astype(F32) + come_far[1].astype(F32)
+        row_stat = stats[: rows // LANES].reshape(rows, 1)
+        grad_in = norm_grad * slope - shift * row_stat + base
     gain_rows = own_width // LANES
     gain = lax.dynamic_slice_in_dim(
         stats, rows // LANES + state_index * gain_rows, gain_rows, 0
@@ -987,45 +1194,52 @@
     count = 2 * states
     rank = w_up.shape[0]
     if blocked:
-        small = small + swap(small_send, "dp", 1).astype(F32)
-        small = small[:2] + swap(small[2:].astype(BF16), "dp", 2).astype(F32)
-        small = small[0] + swap(small[1].astype(BF16), "dp", 4).astype(F32)
-        pieces = [small.astype(BF16)]
-        gathered = pieces[0]
-        for bit in (4, 2, 1):
+        small = lax.reduce_precision(small.reshape(-1, small.shape[-1]), 8, 7)
+        flipped = jnp.concatenate([small[SMALL:], small[:SMALL]], axis=0).astype(BF16)
+        gathered = (small + swap(flipped, "dp", 4).astype(F32)).astype(BF16)
+        gain = gain + swap(gain, "dp", 4)
+        pieces = [gathered]
+        for bit, pins in ((2, (come,)), (1, (come_far, far_out))):
             high = lax.reduce_precision(gain, 8, 7)
             rest = lax.reduce_precision(gain - high, 8, 7)
             line = jnp.concatenate([high.reshape(1, -1), rest.reshape(1, -1)], axis=1)
             tail = jnp.pad(line.astype(BF16), ((0, SUB - 1), (0, 0)))
-            come = swap(jnp.concatenate([gathered, tail], axis=0), "dp", bit)
-            pieces.append(come[:-SUB])
-            gathered = jnp.concatenate([gathered, come[:-SUB]], axis=0)
-            other = come[-SUB].astype(F32)
+            (whole,) = after((jnp.concatenate([gathered, tail], axis=0),), pins)
+            got = swap(whole, "dp", bit)
+            pieces.append(got[:-SUB])
+            gathered = jnp.concatenate([gathered, got[:-SUB]], axis=0)
+            other = got[-SUB].astype(F32)
             gain = (high + rest) + (other[:own_width] + other[own_width:]).reshape(gain.shape)
         grad_gain = gain.reshape(-1)
-        grad_up, down, keyq, lines = unpack(place, pieces, rank, count, taps)
+        grad_wx, grad_wout, block_out, grad_in, grad_up, down, keyq, *lines = finale(
+            place, keep_x, come_x, keep_out, come_out, far_out, out_keep, keep, come, come_far,
+            stats[: rows // LANES], slope, shift, base, pieces, rank, count, taps,
+        )
     else:
         small = all_sum(small, "dp")
         grad_up = small[:rank]
         down = small[rank : 2 * rank].T
         keyq = small[2 * rank : 2 * rank + count]
         lines = small[2 * rank + count :]
+        top = jnp.max(lines[taps + 3] + lines[taps + 4]).reshape(1, 1)
+        lines = (lines[:taps], *[lines[taps + i : taps + i + 1] for i in range(3)], top)
         grad_gain = all_sum(gain, "dp").reshape(-1)
+    grad_taps, grad_bias, grad_skip, grad_beta, top = lines
     return (
         block_out,
         grad_in,
         grad_gain,
         grad_wx,
         grad_wz,
-        lines[:taps],
-        lines[taps],
+        grad_taps,
+        grad_bias[0],
         down,
         grad_up,
-        lines[taps + 2],
+        grad_beta[0],
         keyq.T,
-        lines[taps + 1],
+        grad_skip[0],
         grad_wout,
-        jnp.max(lines[taps + 3] + lines[taps + 4]),
+        top[0, 0],
     )
 
 

time: 222 us -> 193 us (0.87)
  waiting for transfers between devices: 89 us -> 46.1 us
  local copies, waits for them, and re-layouts: 6.8 us -> 17.6 us
  Pallas kernels: 82.6 us -> 85.5 us
    ppermute x29 -> x30, waiting for transfers between devices: 89 us -> 46.1 us  [swap(): return lax.ppermute(value, axis, [(i, i ^ bit) for i in range(size)])]
    unnamed x62 -> x54, local copies, waits for them, and re-layouts: 6.02 us -> 12.5 us
    add x6 -> x1, other arithmetic: 5.8 us -> 0.76 us  [per_device(): small = small + swap(small_send, 'dp', 2).astype(F32)]
    slice x2, local copies, waits for them, and re-layouts: 0.07 us -> 3.77 us  [per_device(): pair = jnp.stack([out_keep[1], keep[1]]) + come[1].astype(F32)]
    convert_element_type x8 -> x5, other arithmetic: 0.82 us -> 3.76 us  [the longest x1 2.27 us: per_device(): (later + come_out[:, cut:].astype(F32)).astype(BF16)]
    pallas_call x7 -> x11, Pallas kernels: 36 us -> 38.2 us  [the longest x1 10.1 us: input_grad(): pl.pallas_call(functools.partial(input_kernel, len(pins), len(extra)), gr...]
    ppermute x29 -> x30, starting transfers between devices: 32.1 us -> 31.3 us  [swap(): return lax.ppermute(value, axis, [(i, i ^ bit) for i in range(size)])]
  transfers between devices with their start and end apart: 29 -> 30, of which waited for: 10 -> 11; matrix products, arithmetic and copies ran while one was open for 3% -> 6% of each run, Pallas kernels for 31% -> 37%
where the time goes in v2:
time: 193 us; the launch traced here: 191 us
  Pallas kernels  85.5 us (44%)
  waiting for transfers between devices  46.1 us (24%)
  starting transfers between devices  31.3 us (16%)
  local copies, waits for them, and re-layouts  17.6 us (9%)
  other arithmetic  9.22 us (5%)
    ppermute x30, waiting for transfers between devices, swap(): return lax.ppermute(value, axis, [(i, i ^ bit) for i in range(size)])  46.1 us
    ppermute x30, starting transfers between devices, swap(): return lax.ppermute(value, axis, [(i, i ^ bit) for i in range(size)])  31.3 us
    pallas_call x1, Pallas kernels, scan_backward(): pl.pallas_call(functools.partial(back_kernel, unroll, len(pins)), in_spec...  19.6 us
    unnamed x54, local copies, waits for them, and re-layouts  12.5 us
    pallas_call x1, Pallas kernels, scan_forward(): pl.pallas_call(functools.partial(scan_kernel, 4), in_specs=[WHOLE] * 8, o...  11.4 us
    pallas_call x1, Pallas kernels, input_grad(): pl.pallas_call(functools.partial(input_kernel, len(pins), len(extra)), gr...  10.1 us
    pallas_call x1, Pallas kernels, front(): pl.pallas_call(functools.partial(front_kernel, blocked), grid=(inner // b...  9.14 us
    pallas_call x1, Pallas kernels, middle(): pl.pallas_call(middle_kernel, grid_spec=pltpu.PrefetchScalarGridSpec(num_...  8.76 us
  transfers between devices with their start and end apart: 30, of which 11 were waited for; matrix products, arithmetic and copies ran while one was open for 6% of the time, Pallas kernels for 37%

profile of v2, /device:TPU:0, one launch (start us, length us, event | category | flops | bytes accessed | tf_op | source)
XLA Modules:
  0.0 191.3 jit_solution(1664984833578193849)
XLA Ops:
  2.0 9.1 %front.1 = (bf16[256,2048]{1,0:T(8,128)(2,1)}, bf16[256,2048]{1,0:T(8,128)(2,1)}, f32[256,1024]{1,0:T(8,128)}, bf16[256,1024]{1,0:T(8,128)(2,1)}, f32[256,1024]{...) custom-call(s32[2]{0:T(128)S(1)} %pad_add_fusion.place, ...), custom_call_target="tpu_custom_call" | custom-call | tf_op jit(solution)/shard_map/front/pallas_call | solution.py:167
  11.7 2.6 %collective-permute-start.1 = (bf16[2,256,512]{2,1,0:T(8,128)(2,1)}, bf16[2,256,512]{2,1,0:T(8,128)(2,1)S(1)}, u32[]{:S(2)}, u32[]{:S(2)}) collective-permute-start(bf16[2,256,512]{2,1,0:T(8,128)(2,1)} %get-tuple-element.76), channel_id=1, source_target_pairs={{0,4},{4,0},{8,12},{12,8},{16,20},{20,16},{24,28},{28,24},{1,5},{5... | collective-permute-start | bytes 1572872 | tf_op jit(solution)/shard_map/ppermute | solution.py:35
  14.3 1.6 collective-permute-start.4
  15.9 1.6 collective-permute-start
  17.5 2.6 %collective-permute-start.5 = (bf16[128,1024]{1,0:T(8,128)(2,1)}, bf16[128,1024]{1,0:T(8,128)(2,1)S(1)}, u32[]{:S(2)}, u32[]{:S(2)}) collective-permute-start(bf16[128,1024]{1,0:T(8,128)(2,1)} %get-tuple-element.89), channel_id=1, source_target_pairs={{0,16},{4,20},{8,24},{12,28},{16,0},{20,4},{24,8},{28,12},{1,17},{... | collective-permute-start | bytes 786440 | tf_op jit(solution)/shard_map/ppermute | solution.py:35
  20.0 7.1 %gate.1 = (f32[256,1024]{1,0:T(8,128)S(1)}, f32[256,1024]{1,0:T(8,128)S(1)}, f32[256,1024]{1,0:T(8,128)}) custom-call(bf16[256,2048]{1,0:T(8,128)(2,1)} %get-tuple-element.79.normed, bf16[256,2048]{1,0:T(8,128)(2,1)} %get-tuple-element.80.up, bf16[2048,1024]{1,0:T(8,128)(2,1)} %wz.3, bf16[1024,2048]{1,0:T(8,128)(2,1)} %wo.3), custom_call_target="tpu_custom_call" | custom-call | tf_op jit(solution)/shard_map/gate/pallas_call | solution.py:227
  27.2 11.4 %scan.1 = (bf16[256,1024]{1,0:T(8,128)(2,1)}, bf16[256,1024]{1,0:T(8,128)(2,1)}, f32[256,1024]{1,0:T(8,128)S(1)}, f32[256,1024]{1,0:T(8,128)S(1)}, f32[8,128]{1,...) custom-call(f32[320,128]{1,0:T(8,128)S(1)} %add.62.one, ...), custom_call_target="tpu_custom_call" | custom-call | tf_op jit(solution)/shard_map/scan/pallas_call | solution.py:342
  39.0 1.3 collective-permute-start.10
  40.7 19.6 %back.1 = (f32[256,1024]{1,0:T(8,128)}, f32[336,128]{1,0:T(8,128)S(1)}, f32[136,1024]{1,0:T(8,128)}) custom-call(s32[2]{0:T(128)S(1)} %pad_add_fusion.place, f32[320,128]{1,0:T(8,128)S(1)} %add.62.one, f32[320,128]{1,0:T(8,128)S(1)} %collective-permute-done.4.two, bf16[256,1024]{1,0:T(8,128)(2,1)} %get-tuple-element.78.mixed, bf16[128,1024]{1,0:T(8,128)(2,1)} %wup.3, ...), custom_call_target="tpu_custom_call" | custom-call | tf_op jit(solution)/shard_map/back/pallas_call | solution.py:496
  61.9 1.6 collective-permute-start.2
  65.7 5.2 %collective-permute-done.2.rest_3_.l3 = bf16[256,512]{1,0:T(8,128)(2,1)S(1)} collective-permute-done((bf16[256,512]{1,0:T(8,128)(2,1)}, bf16[256,512]{1,0:T(8,128)(2,1)S(1)}, u32[]{:S(2)}, u32[]{:S(2)}) %collective-permute-start.2) | collective-permute-done | bytes 262176 | tf_op jit(solution)/shard_map/ppermute | solution.py:35
  71.0 6.1 %conv.1 = (bf16[256,1024]{1,0:T(8,128)(2,1)}, f32[4,40,1024]{2,1,0:T(8,128)}, bf16[4,40,1024]{2,1,0:T(8,128)(2,1)}) custom-call(s32[2]{0:T(128)S(1)} %pad_add_fusion.place, f32[320,128]{1,0:T(8,128)S(1)} %add.62.one, f32[320,128]{1,0:T(8,128)S(1)} %collective-permute-done.4.two, f32[336,128]{1,0:T(8,128)} %add.63.grad_one, ...), custom_call_target="tpu_custom_call" | custom-call | tf_op jit(solution)/shard_map/conv/pallas_call | solution.py:613
  77.0 1.4 collective-permute-start.11
  79.1 1.3 collective-permute-start.14
  80.5 1.0 copy-done.4
  81.5 3.9 %inw.2 = (f32[256,1024]{1,0:T(8,128)}, bf16[256,1024]{1,0:T(8,128)(2,1)}) custom-call(bf16[256,512]{1,0:T(8,128)(2,1)} %get-tuple-element.74.l0, bf16[256,512]{1,0:T(8,128)(2,1)S(1)} %collective-permute-done.rest_0_.l1, bf16[2,256,512]{2,1,0:T(8,128)(2,1)S(1)} %collective-permute-done.1.rest_1_.l2, bf16[256,512]{1,0:T(8,128)(2,1)S(1)} %collective-permute-done.2.rest_3_.l3, ...), custom_call_target="tpu_custom_call" | custom-call | tf_op jit(solution)/shard_map/inw/pallas_call | solution.py:1015
  85.4 2.6 %collective-permute-start.17 = (bf16[256,1024]{1,0:T(8,128)(2,1)}, bf16[256,1024]{1,0:T(8,128)(2,1)S(1)}, u32[]{:S(2)}, u32[]{:S(2)}) collective-permute-start(bf16[256,1024]{1,0:T(8,128)(2,1)} %get-tuple-element.101.rest_0_), channel_id=1, source_target_pairs={{0,16},{4,20},{8,24},{12,28},{16,0},{20,4},{24,8},{28,12},{1,17},{... | collective-permute-start | bytes 1572872 | tf_op jit(solution)/shard_map/ppermute | solution.py:35
  87.9 7.9 %collective-permute-done.11.rest_1_.r1 = bf16[256,1024]{1,0:T(8,128)(2,1)S(1)} collective-permute-done((bf16[256,1024]{1,0:T(8,128)(2,1)}, bf16[256,1024]{1,0:T(8,128)(2,1)S(1)}, u32[]{:S(2)}, u32[]{:S(2)}) %collective-permute-start.11) | collective-permute-done | bytes 524320 | tf_op jit(solution)/shard_map/ppermute | solution.py:35
  96.6 3.4 %collective-permute-done.14.small_come = bf16[4,40,1024]{2,1,0:T(8,128)(2,1)S(1)} collective-permute-done((bf16[4,40,1024]{2,1,0:T(8,128)(2,1)}, bf16[4,40,1024]{2,1,0:T(8,128)(2,1)S(1)}, u32[]{:S(2)}, u32[]{:S(2)}) %collective-permute-start.14) | collective-permute-done | bytes 327712 | tf_op jit(solution)/shard_map/ppermute | solution.py:35
  100.0 1.0 copy-done.20
  101.0 8.8 %middle.1 = (f32[1024,256]{1,0:T(8,128)}, f32[1024,256]{1,0:T(8,128)}, bf16[1024,512]{1,0:T(8,128)(2,1)}, bf16[2,2,256,512]{3,2,1,0:T(8,128)(2,1)}, f32[2,256,51...) custom-call(s32[2]{0:T(128)S(1)} %pad_add_fusion.place, ...), custom_call_target="tpu_custom_call" | custom-call | tf_op jit(solution)/shard_map/middle/pallas_call | solution.py:849
  110.6 1.2 copy-done.15
  111.8 3.9 %inw.3 = (f32[256,1024]{1,0:T(8,128)}, bf16[256,1024]{1,0:T(8,128)(2,1)}) custom-call(bf16[256,512]{1,0:T(8,128)(2,1)} %get-tuple-element.74.l0, bf16[256,512]{1,0:T(8,128)(2,1)S(1)} %collective-permute-done.rest_0_.l1, bf16[2,256,512]{2,1,0:T(8,128)(2,1)S(1)} %collective-permute-done.1.rest_1_.l2, bf16[256,512]{1,0:T(8,128)(2,1)S(1)} %collective-permute-done.2.rest_3_.l3, ...), custom_call_target="tpu_custom_call" | custom-call | tf_op jit(solution)/shard_map/inw/pallas_call | solution.py:1015
  115.7 3.2 %collective-permute-start.18 = (bf16[256,1024]{1,0:T(8,128)(2,1)}, bf16[256,1024]{1,0:T(8,128)(2,1)S(1)}, u32[]{:S(2)}, u32[]{:S(2)}) collective-permute-start(bf16[256,1024]{1,0:T(8,128)(2,1)} %get-tuple-element.104.rest_2_.refs_1_), channel_id=1, source_target_pairs={{0,16},{4,20},{8,24},{12,28},{16,0},{20,4},{24,8},{28,12},{1,17},{... | collective-permute-start | bytes 1572872 | tf_op jit(solution)/shard_map/ppermute | solution.py:35
  119.5 1.9 slice.78
  121.4 1.0 copy-done.11
  122.5 1.2 copy-done.14
  123.7 10.1 %inputs.1 = (bf16[2,2,256,512]{3,2,1,0:T(8,128)(2,1)}, f32[2,256,512]{2,1,0:T(8,128)}, f32[18,128]{1,0:T(8,128)S(1)}, f32[256,512]{1,0:T(8,128)}, f32[256,512]{1...) custom-call(s32[2]{0:T(128)S(1)} %pad_add_fusion.place, s32[1]{0:T(128)S(6)} %copy.55.ids, ...), custom_call_target="tpu_custom_call", output_to_operand_aliasing={{0}: (3, {})} | custom-call | tf_op jit(solution)/shard_map/inputs/pallas_call | solution.py:757
  133.8 1.9 slice.79
  136.5 3.6 %collective-permute-done.18.refs_3_.come_x = bf16[256,1024]{1,0:T(8,128)(2,1)S(1)} collective-permute-done((bf16[256,1024]{1,0:T(8,128)(2,1)}, bf16[256,1024]{1,0:T(8,128)(2,1)S(1)}, u32[]{:S(2)}, u32[]{:S(2)}) %collective-permute-start.18) | collective-permute-done | bytes 524320 | tf_op jit(solution)/shard_map/ppermute | solution.py:35
  140.1 0.8 copy-done.12
  141.3 1.1 reduce-precision_convert_fusion.2
  144.2 2.9 %collective-permute-done.25 = f32[18,128]{1,0:T(8,128)S(1)} collective-permute-done((f32[18,128]{1,0:T(8,128)S(1)}, f32[18,128]{1,0:T(8,128)S(1)}, u32[]{:S(2)}, u32[]{:S(2)}) %collective-permute-start.25) | collective-permute-done | bytes 9248 | tf_op jit(solution)/shard_map/ppermute | solution.py:35
  147.2 2.3 %add_convert_fusion = bf16[1024,256]{1,0:T(8,128)(2,1)} fusion(f32[1024,256]{1,0:T(8,128)} %get-tuple-element.106, bf16[1024,512]{1,0:T(8,128)(2,1)} %copy-done.2), kind=kLoop, calls=%fused_computation.2 | loop fusion | flops 786432 | bytes 2097152 | tf_op jit(solution)/shard_map/convert_element_type | solution.py:1166
  149.4 2.5 %collective-permute-start.20 = (bf16[1024,256]{1,0:T(8,128)(2,1)}, bf16[1024,256]{1,0:T(8,128)(2,1)S(1)}, u32[]{:S(2)}, u32[]{:S(2)}) collective-permute-start(bf16[1024,256]{1,0:T(8,128)(2,1)} %add_convert_fusion), channel_id=1, source_target_pairs={{0,8},{4,12},{8,0},{12,4},{16,24},{20,28},{24,16},{28,20},{1,9},{5... | collective-permute-start | bytes 1572872 | tf_op jit(solution)/shard_map/ppermute | solution.py:35
  151.9 2.0 %collective-permute-done.27 = f32[4,128]{1,0:T(4,128)S(1)} collective-permute-done((f32[4,128]{1,0:T(4,128)S(1)}, f32[4,128]{1,0:T(4,128)S(1)}, u32[]{:S(2)}, u32[]{:S(2)}) %collective-permute-start.27) | collective-permute-done | bytes 2080 | tf_op jit(solution)/shard_map/ppermute | solution.py:35
  154.6 1.0 copy-done
  155.6 1.5 fusion
  157.1 1.6 collective-permute-start.23
  158.6 10.2 %collective-permute-done.28 = bf16[88,1024]{1,0:T(8,128)(2,1)S(1)} collective-permute-done((bf16[88,1024]{1,0:T(8,128)(2,1)}, bf16[88,1024]{1,0:T(8,128)(2,1)S(1)}, u32[]{:S(2)}, u32[]{:S(2)}) %collective-permute-start.28) | collective-permute-done | bytes 180256 | tf_op jit(solution)/shard_map/ppermute | solution.py:35
  169.0 0.8 pad_maximum_fusion.refs_0_
  169.7 1.2 collective-permute-done.23.refs_1_.far_a.far_b
  170.9 0.8 copy-done.5
  172.4 9.1 %collective-permute-done.29 = bf16[168,1024]{1,0:T(8,128)(2,1)S(1)} collective-permute-done((bf16[168,1024]{1,0:T(8,128)(2,1)}, bf16[168,1024]{1,0:T(8,128)(2,1)S(1)}, u32[]{:S(2)}, u32[]{:S(2)}) %collective-permute-start.29) | collective-permute-done | bytes 344096 | tf_op jit(solution)/shard_map/ppermute | solution.py:35
  182.2 1.0 copy-done.6
  183.2 1.0 copy-done.10
  184.2 1.0 copy-done.13
  185.3 5.5 %finale.1 = (f32[256,1024]{1,0:T(8,128)}, f32[1024,256]{1,0:T(8,128)}, bf16[256,512]{1,0:T(8,128)(2,1)}, f32[256,512]{1,0:T(8,128)}, f32[128,1024]{1,0:T(8,128)}...) custom-call(s32[2]{0:T(128)S(1)} %pad_add_fusion.place, ...), custom_call_target="tpu_custom_call" | custom-call | tf_op jit(solution)/shard_map/finale/pallas_call | solution.py:949
  (114 shorter events, 14.5 us)
Async XLA Ops:
  11.2 3.1 %collective-permute-start.3 = (f32[320,128]{1,0:T(8,128)S(1)}, f32[320,128]{1,0:T(8,128)S(1)}, u32[]{:S(2)}, u32[]{:S(2)}) collective-permute-start(f32[320,128]{1,0:T(8,128)S(1)} %get-tuple-element.77), channel_id=1, source_target_pairs={{0,1},{1,0},{2,3},{3,2},{4,5},{5,4},{6,7},{7,6},{8,9},{9,8},{10,11... | collective-permute-start | bytes 491528 | tf_op jit(solution)/shard_map/ppermute | solution.py:35
  11.7 29.0 %collective-permute-start.1 = (bf16[2,256,512]{2,1,0:T(8,128)(2,1)}, bf16[2,256,512]{2,1,0:T(8,128)(2,1)S(1)}, u32[]{:S(2)}, u32[]{:S(2)}) collective-permute-start(bf16[2,256,512]{2,1,0:T(8,128)(2,1)} %get-tuple-element.76), channel_id=1, source_target_pairs={{0,4},{4,0},{8,12},{12,8},{16,20},{20,16},{24,28},{28,24},{1,5},{5... | collective-permute-start | bytes 1572872 | tf_op jit(solution)/shard_map/ppermute | solution.py:35
  14.3 12.9 %collective-permute-start.4 = (f32[320,128]{1,0:T(8,128)S(1)}, f32[320,128]{1,0:T(8,128)S(1)}, u32[]{:S(2)}, u32[]{:S(2)}) collective-permute-start(f32[320,128]{1,0:T(8,128)S(1)} %add.62.one), channel_id=1, source_target_pairs={{0,2},{1,3},{2,0},{3,1},{4,6},{5,7},{6,4},{7,5},{8,10},{9,11},{10,... | collective-permute-start | bytes 491528 | tf_op jit(solution)/shard_map/ppermute | solution.py:35
  15.9 24.5 %collective-permute-start = (bf16[256,512]{1,0:T(8,128)(2,1)}, bf16[256,512]{1,0:T(8,128)(2,1)S(1)}, u32[]{:S(2)}, u32[]{:S(2)}) collective-permute-start(bf16[256,512]{1,0:T(8,128)(2,1)} %get-tuple-element.75), channel_id=1, source_target_pairs={{0,8},{4,12},{8,0},{12,4},{16,24},{20,28},{24,16},{28,20},{1,9},{5... | collective-permute-start | bytes 786440 | tf_op jit(solution)/shard_map/ppermute | solution.py:35
  17.5 23.2 %collective-permute-start.5 = (bf16[128,1024]{1,0:T(8,128)(2,1)}, bf16[128,1024]{1,0:T(8,128)(2,1)S(1)}, u32[]{:S(2)}, u32[]{:S(2)}) collective-permute-start(bf16[128,1024]{1,0:T(8,128)(2,1)} %get-tuple-element.89), channel_id=1, source_target_pairs={{0,16},{4,20},{8,24},{12,28},{16,0},{20,4},{24,8},{28,12},{1,17},{... | collective-permute-start | bytes 786440 | tf_op jit(solution)/shard_map/ppermute | solution.py:35
  38.5 25.6 %collective-permute-start.15 = (bf16[256,1024]{1,0:T(8,128)(2,1)}, bf16[256,1024]{1,0:T(8,128)(2,1)S(1)}, u32[]{:S(2)}, u32[]{:S(2)}) collective-permute-start(bf16[256,1024]{1,0:T(8,128)(2,1)} %get-tuple-element.96.r0.prez), channel_id=1, source_target_pairs={{0,8},{4,12},{8,0},{12,4},{16,24},{20,28},{24,16},{28,20},{1,9},{5... | collective-permute-start | bytes 1572872 | tf_op jit(solution)/shard_map/ppermute | solution.py:35
  39.0 31.9 %collective-permute-start.10 = (bf16[256,1024]{1,0:T(8,128)(2,1)}, bf16[256,1024]{1,0:T(8,128)(2,1)S(1)}, u32[]{:S(2)}, u32[]{:S(2)}) collective-permute-start(bf16[256,1024]{1,0:T(8,128)(2,1)} %get-tuple-element.96.r0.prez), channel_id=1, source_target_pairs={{0,4},{4,0},{8,12},{12,8},{16,20},{20,16},{24,28},{28,24},{1,5},{5... | collective-permute-start | bytes 1572872 | tf_op jit(solution)/shard_map/ppermute | solution.py:35
  40.3 30.6 %collective-permute-start.8 = (bf16[256,1024]{1,0:T(8,128)(2,1)}, bf16[256,1024]{1,0:T(8,128)(2,1)S(1)}, u32[]{:S(2)}, u32[]{:S(2)}) collective-permute-start(bf16[256,1024]{1,0:T(8,128)(2,1)} %get-tuple-element.95.gated.every), channel_id=1, source_target_pairs={{0,16},{4,20},{8,24},{12,28},{16,0},{20,4},{24,8},{28,12},{1,17},{... | collective-permute-start | bytes 1572872 | tf_op jit(solution)/shard_map/ppermute | solution.py:35
  40.7 19.6 %copy-start.16 = (bf16[128,1024]{1,0:T(8,128)(2,1)}, bf16[128,1024]{1,0:T(8,128)(2,1)S(1)}, u32[]{:S(2)}) copy-start(bf16[128,1024]{1,0:T(8,128)(2,1)S(1)} %collective-permute-done.5.rest_2_.up_a) | copy-start | bytes 786436
  40.7 24.3 %collective-permute-start.9 = (bf16[128,1024]{1,0:T(8,128)(2,1)S(1)}, bf16[128,1024]{1,0:T(8,128)(2,1)}, u32[]{:S(2)}, u32[]{:S(2)}) collective-permute-start(bf16[128,1024]{1,0:T(8,128)(2,1)S(1)} %collective-permute-done.5.rest_2_.up_a), channel_id=1, source_target_pairs={{0,1},{1,0},{2,3},{3,2},{4,5},{5,4},{6,7},{7,6},{8,9},{9,8},{10,11... | collective-permute-start | bytes 786440 | tf_op jit(solution)/shard_map/ppermute | solution.py:35
  60.3 3.8 %copy-start.18 = (f32[336,128]{1,0:T(8,128)}, f32[336,128]{1,0:T(8,128)S(1)}, u32[]{:S(2)}) copy-start(f32[336,128]{1,0:T(8,128)S(1)} %get-tuple-element.90.refs_1_) | copy-start | bytes 516100
  60.3 1.5 collective-permute-start.6
  61.9 9.1 %collective-permute-start.2 = (bf16[256,512]{1,0:T(8,128)(2,1)}, bf16[256,512]{1,0:T(8,128)(2,1)S(1)}, u32[]{:S(2)}, u32[]{:S(2)}) collective-permute-start(bf16[256,512]{1,0:T(8,128)(2,1)} %slice_bitcast_fusion.1), channel_id=1, source_target_pairs={{0,8},{4,12},{8,0},{12,4},{16,24},{20,28},{24,16},{28,20},{1,9},{5... | collective-permute-start | bytes 786440 | tf_op jit(solution)/shard_map/ppermute | solution.py:35
  64.2 6.8 %collective-permute-start.7 = (f32[336,128]{1,0:T(8,128)}, f32[336,128]{1,0:T(8,128)}, u32[]{:S(2)}, u32[]{:S(2)}) collective-permute-start(f32[336,128]{1,0:T(8,128)} %add.63.grad_one), channel_id=1, source_target_pairs={{0,2},{1,3},{2,0},{3,1},{4,6},{5,7},{6,4},{7,5},{8,10},{9,11},{10,... | collective-permute-start | bytes 516104 | tf_op jit(solution)/shard_map/ppermute | solution.py:35
  65.0 15.5 %copy-start.8 = (bf16[256,1024]{1,0:T(8,128)(2,1)S(1)}, bf16[256,1024]{1,0:T(8,128)(2,1)}, u32[]{:S(2)}) copy-start(bf16[256,1024]{1,0:T(8,128)(2,1)} %after.5.r1) | copy-start | bytes 1572868
  65.0 15.5 %collective-permute-start.16 = (bf16[256,1024]{1,0:T(8,128)(2,1)}, bf16[256,1024]{1,0:T(8,128)(2,1)S(1)}, u32[]{:S(2)}, u32[]{:S(2)}) collective-permute-start(bf16[256,1024]{1,0:T(8,128)(2,1)} %after.5.r1), channel_id=1, source_target_pairs={{0,4},{4,0},{8,12},{12,8},{16,20},{20,16},{24,28},{28,24},{1,5},{5... | collective-permute-start | bytes 1572872 | tf_op jit(solution)/shard_map/ppermute | solution.py:35
  70.9 29.1 %copy-start.17 = (bf16[128,1024]{1,0:T(8,128)(2,1)S(1)}, bf16[128,1024]{1,0:T(8,128)(2,1)}, u32[]{:S(2)}) copy-start(bf16[128,1024]{1,0:T(8,128)(2,1)} %copy-done.16) | copy-start | bytes 786436
  70.9 29.0 %copy-start.19 = (bf16[256,1024]{1,0:T(8,128)(2,1)S(1)}, bf16[256,1024]{1,0:T(8,128)(2,1)}, u32[]{:S(2)}) copy-start(bf16[256,1024]{1,0:T(8,128)(2,1)} %get-tuple-element.98.up_own) | copy-start | bytes 1572868
  77.0 18.8 %collective-permute-start.11 = (bf16[256,1024]{1,0:T(8,128)(2,1)}, bf16[256,1024]{1,0:T(8,128)(2,1)S(1)}, u32[]{:S(2)}, u32[]{:S(2)}) collective-permute-start(bf16[256,1024]{1,0:T(8,128)(2,1)} %get-tuple-element.97.rest_0_.r0.prex), channel_id=1, source_target_pairs={{0,8},{4,12},{8,0},{12,4},{16,24},{20,28},{24,16},{28,20},{1,9},{5... | collective-permute-start | bytes 1572872 | tf_op jit(solution)/shard_map/ppermute | solution.py:35
  78.4 21.6 %collective-permute-start.12 = (bf16[256,1024]{1,0:T(8,128)(2,1)}, bf16[256,1024]{1,0:T(8,128)(2,1)S(1)}, u32[]{:S(2)}, u32[]{:S(2)}) collective-permute-start(bf16[256,1024]{1,0:T(8,128)(2,1)} %get-tuple-element.97.rest_0_.r0.prex), channel_id=1, source_target_pairs={{0,4},{4,0},{8,12},{12,8},{16,20},{20,16},{24,28},{28,24},{1,5},{5... | collective-permute-start | bytes 1572872 | tf_op jit(solution)/shard_map/ppermute | solution.py:35
  79.1 20.8 %collective-permute-start.14 = (bf16[4,40,1024]{2,1,0:T(8,128)(2,1)}, bf16[4,40,1024]{2,1,0:T(8,128)(2,1)S(1)}, u32[]{:S(2)}, u32[]{:S(2)}) collective-permute-start(bf16[4,40,1024]{2,1,0:T(8,128)(2,1)} %get-tuple-element.100), channel_id=1, source_target_pairs={{0,4},{4,0},{8,12},{12,8},{16,20},{20,16},{24,28},{28,24},{1,5},{5... | collective-permute-start | bytes 983048 | tf_op jit(solution)/shard_map/ppermute | solution.py:35
  80.4 1.0 copy-start.4
  85.4 25.2 %collective-permute-start.17 = (bf16[256,1024]{1,0:T(8,128)(2,1)}, bf16[256,1024]{1,0:T(8,128)(2,1)S(1)}, u32[]{:S(2)}, u32[]{:S(2)}) collective-permute-start(bf16[256,1024]{1,0:T(8,128)(2,1)} %get-tuple-element.101.rest_0_), channel_id=1, source_target_pairs={{0,16},{4,20},{8,24},{12,28},{16,0},{20,4},{24,8},{28,12},{1,17},{... | collective-permute-start | bytes 1572872 | tf_op jit(solution)/shard_map/ppermute | solution.py:35
  95.8 14.7 %collective-permute-start.13 = (bf16[256,1024]{1,0:T(8,128)(2,1)S(1)}, bf16[256,1024]{1,0:T(8,128)(2,1)S(1)}, u32[]{:S(2)}, u32[]{:S(2)}) collective-permute-start(bf16[256,1024]{1,0:T(8,128)(2,1)S(1)} %collective-permute-done.11.rest_1_.r1), channel_id=1, source_target_pairs={{0,4},{4,0},{8,12},{12,8},{16,20},{20,16},{24,28},{28,24},{1,5},{5... | collective-permute-start | bytes 1572872 | tf_op jit(solution)/shard_map/ppermute | solution.py:35
  100.0 1.0 copy-start.20
  109.8 11.6 %copy-start.23 = (f32[8]{0:T(128)S(1)}, f32[8]{0:T(128)}, u32[]{:S(2)}) copy-start(f32[8]{0:T(128)} %weights.3) | copy-start | bytes 100
  109.8 30.3 %collective-permute-start.19 = (bf16[1024,512]{1,0:T(8,128)(2,1)}, bf16[1024,512]{1,0:T(8,128)(2,1)S(1)}, u32[]{:S(2)}, u32[]{:S(2)}) collective-permute-start(bf16[1024,512]{1,0:T(8,128)(2,1)} %get-tuple-element.102.rest_0_), channel_id=1, source_target_pairs={{0,4},{4,0},{8,12},{12,8},{16,20},{20,16},{24,28},{28,24},{1,5},{5... | collective-permute-start | bytes 3145736 | tf_op jit(solution)/shard_map/ppermute | solution.py:35
  110.5 1.3 copy-start.15
  115.7 24.5 %collective-permute-start.18 = (bf16[256,1024]{1,0:T(8,128)(2,1)}, bf16[256,1024]{1,0:T(8,128)(2,1)S(1)}, u32[]{:S(2)}, u32[]{:S(2)}) collective-permute-start(bf16[256,1024]{1,0:T(8,128)(2,1)} %get-tuple-element.104.rest_2_.refs_1_), channel_id=1, source_target_pairs={{0,16},{4,20},{8,24},{12,28},{16,0},{20,4},{24,8},{28,12},{1,17},{... | collective-permute-start | bytes 1572872 | tf_op jit(solution)/shard_map/ppermute | solution.py:35
  118.9 16.9 %collective-permute-start.21 = (bf16[2,40,1024]{2,1,0:T(8,128)(2,1)}, bf16[2,40,1024]{2,1,0:T(8,128)(2,1)S(1)}, u32[]{:S(2)}, u32[]{:S(2)}) collective-permute-start(bf16[2,40,1024]{2,1,0:T(8,128)(2,1)} %after.6), channel_id=1, source_target_pairs={{0,8},{4,12},{8,0},{12,4},{16,24},{20,28},{24,16},{28,20},{1,9},{5... | collective-permute-start | bytes 491528 | tf_op jit(solution)/shard_map/ppermute | solution.py:35
  122.5 1.2 copy-start.14
  123.7 12.0 %copy-start.25 = (f32[2,40,1024]{2,1,0:T(8,128)S(1)}, f32[2,40,1024]{2,1,0:T(8,128)}, u32[]{:S(2)}) copy-start(f32[2,40,1024]{2,1,0:T(8,128)} %get-tuple-element.113) | copy-start | bytes 983044
  133.8 6.3 %copy-start.21 = (f32[18,128]{1,0:T(8,128)}, f32[18,128]{1,0:T(8,128)S(1)}, u32[]{:S(2)}) copy-start(f32[18,128]{1,0:T(8,128)S(1)} %get-tuple-element.112.refs_1_) | copy-start | bytes 27652
  140.1 1.1 copy-start.2
  141.3 14.3 %copy-start.24 = (f32[1,256,512]{2,1,0:T(8,128)S(1)}, f32[1,256,512]{2,1,0:T(8,128)}, u32[]{:S(2)}) copy-start(f32[1,256,512]{2,1,0:T(8,128)} %slice.78) | copy-start | bytes 1572868
  141.3 1.4 collective-permute-start.24
  143.4 3.7 %collective-permute-start.25 = (f32[18,128]{1,0:T(8,128)S(1)}, f32[18,128]{1,0:T(8,128)S(1)}, u32[]{:S(2)}, u32[]{:S(2)}) collective-permute-start(f32[18,128]{1,0:T(8,128)S(1)} %add.67), channel_id=1, source_target_pairs={{0,2},{1,3},{2,0},{3,1},{4,6},{5,7},{6,4},{7,5},{8,10},{9,11},{10,... | collective-permute-start | bytes 27656 | tf_op jit(solution)/shard_map/ppermute | solution.py:35
  144.0 9.9 %collective-permute-start.26 = (bf16[80,1024]{1,0:T(8,128)(2,1)S(1)}, bf16[80,1024]{1,0:T(8,128)(2,1)S(1)}, u32[]{:S(2)}, u32[]{:S(2)}) collective-permute-start(bf16[80,1024]{1,0:T(8,128)(2,1)S(1)} %pad_maximum_fusion.2), channel_id=1, source_target_pairs={{0,16},{4,20},{8,24},{12,28},{16,0},{20,4},{24,8},{28,12},{1,17},{... | collective-permute-start | bytes 491528 | tf_op jit(solution)/shard_map/ppermute | solution.py:35
  144.1 10.5 %collective-permute-start.22 = (bf16[2,2,256,512]{3,2,1,0:T(8,128)(2,1)}, bf16[2,2,256,512]{3,2,1,0:T(8,128)(2,1)S(1)}, u32[]{:S(2)}, u32[]{:S(2)}) collective-permute-start(bf16[2,2,256,512]{3,2,1,0:T(8,128)(2,1)} %get-tuple-element.115), channel_id=1, source_target_pairs={{0,1},{1,0},{2,3},{3,2},{4,5},{5,4},{6,7},{7,6},{8,9},{9,8},{10,11... | collective-permute-start | bytes 3145736 | tf_op jit(solution)/shard_map/ppermute | solution.py:35
  147.1 6.8 %collective-permute-start.27 = (f32[4,128]{1,0:T(4,128)S(1)}, f32[4,128]{1,0:T(4,128)S(1)}, u32[]{:S(2)}, u32[]{:S(2)}) collective-permute-start(f32[4,128]{1,0:T(4,128)S(1)} %constant_dynamic-slice_fusion), channel_id=1, source_target_pairs={{0,16},{4,20},{8,24},{12,28},{16,0},{20,4},{24,8},{28,12},{1,17},{... | collective-permute-start | bytes 6152 | tf_op jit(solution)/shard_map/ppermute | solution.py:35
  149.4 32.7 %copy-start.3 = (bf16[1024,512]{1,0:T(8,128)(2,1)S(1)}, bf16[1024,512]{1,0:T(8,128)(2,1)}, u32[]{:S(2)}) copy-start(bf16[1024,512]{1,0:T(8,128)(2,1)} %copy-done.2) | copy-start | bytes 3145732
  149.4 20.3 %collective-permute-start.20 = (bf16[1024,256]{1,0:T(8,128)(2,1)}, bf16[1024,256]{1,0:T(8,128)(2,1)S(1)}, u32[]{:S(2)}, u32[]{:S(2)}) collective-permute-start(bf16[1024,256]{1,0:T(8,128)(2,1)} %add_convert_fusion), channel_id=1, source_target_pairs={{0,8},{4,12},{8,0},{12,4},{16,24},{20,28},{24,16},{28,20},{1,9},{5... | collective-permute-start | bytes 1572872 | tf_op jit(solution)/shard_map/ppermute | solution.py:35
  155.6 26.5 %copy-start.1 = (bf16[2,2,256,512]{3,2,1,0:T(8,128)(2,1)S(1)}, bf16[2,2,256,512]{3,2,1,0:T(8,128)(2,1)}, u32[]{:S(2)}) copy-start(bf16[2,2,256,512]{3,2,1,0:T(8,128)(2,1)} %copy-done) | copy-start | bytes 3145732
  155.6 13.2 %collective-permute-start.28 = (bf16[88,1024]{1,0:T(8,128)(2,1)}, bf16[88,1024]{1,0:T(8,128)(2,1)S(1)}, u32[]{:S(2)}, u32[]{:S(2)}) collective-permute-start(bf16[88,1024]{1,0:T(8,128)(2,1)} %after.8), channel_id=1, source_target_pairs={{0,8},{4,12},{8,0},{12,4},{16,24},{20,28},{24,16},{28,20},{1,9},{5... | collective-permute-start | bytes 540680 | tf_op jit(solution)/shard_map/ppermute | solution.py:35
  157.1 13.8 %collective-permute-start.23 = (bf16[2,256,512]{2,1,0:T(8,128)(2,1)S(1)}, bf16[2,256,512]{2,1,0:T(8,128)(2,1)S(1)}, u32[]{:S(2)}, u32[]{:S(2)}) collective-permute-start(bf16[2,256,512]{2,1,0:T(8,128)(2,1)S(1)} %fusion), channel_id=1, source_target_pairs={{0,2},{1,3},{2,0},{3,1},{4,6},{5,7},{6,4},{7,5},{8,10},{9,11},{10,... | collective-permute-start | bytes 1572872 | tf_op jit(solution)/shard_map/ppermute | solution.py:35
  169.7 1.2 copy-start.9
  171.7 9.8 %collective-permute-start.29 = (bf16[168,1024]{1,0:T(8,128)(2,1)}, bf16[168,1024]{1,0:T(8,128)(2,1)S(1)}, u32[]{:S(2)}, u32[]{:S(2)}) collective-permute-start(bf16[168,1024]{1,0:T(8,128)(2,1)} %after.9), channel_id=1, source_target_pairs={{0,4},{4,0},{8,12},{12,8},{16,20},{20,16},{24,28},{28,24},{1,5},{5... | collective-permute-start | bytes 1032200 | tf_op jit(solution)/shard_map/ppermute | solution.py:35
  182.2 1.0 copy-start.6
  (8 other events, 7.2 us)

commit v3 on v2

--- a/solution.py
+++ b/solution.py
@@ -154,7 +154,7 @@
     rows, width = tokens.shape
     inner = w_x.shape[1]
     rank, kq = w_down.shape[1], w_keyq.shape[0]
-    blk = min(inner, 256)
+    blk = min(inner, 512)
     whole = lambda shape: pl.BlockSpec(shape, lambda i: (0,) * len(shape))
     cols = lambda height: pl.BlockSpec((height, blk), lambda i: (0, i))
     smem = pl.BlockSpec(memory_space=pltpu.SMEM)
@@ -190,8 +190,8 @@
         ]
         + [whole(shape) for shape in shapes],
         out_shape=[
-            pltpu.HBM((rows, width), BF16),
-            pltpu.HBM((rows, width), BF16),
+            jax.ShapeDtypeStruct((rows, width), BF16),
+            jax.ShapeDtypeStruct((rows, width), BF16),
             pltpu.HBM((rows, inner), F32),
             pltpu.HBM((rows, inner), BF16),
             pltpu.HBM((rows, inner), F32),
@@ -199,7 +199,7 @@
         ]
         + [pltpu.HBM(shape, BF16) for shape in shapes],
         scratch_shapes=[pltpu.VMEM((kq, rows), F32)],
-        compiler_params=pltpu.CompilerParams(vmem_limit_bytes=26 * MIB),
+        compiler_params=pltpu.CompilerParams(vmem_limit_bytes=36 * MIB),
         name="front",
     )(
         place, group_ids, group_weights, in_hbm(tokens), in_hbm(cotangent),
@@ -221,7 +221,7 @@
 def gate(normed, upstream_b, w_z, w_out):
     rows, width = normed.shape
     inner = w_z.shape[1]
-    blk = min(inner, 256)
+    blk = min(inner, 512)
     whole = lambda shape: pl.BlockSpec(shape, lambda i: (0, 0))
     cols = lambda height: pl.BlockSpec((height, blk), lambda i: (0, i))
     return pl.pallas_call(
@@ -237,7 +237,7 @@
         out_shape=[jax.ShapeDtypeStruct((rows, inner), F32)] * 2 + [pltpu.HBM((rows, inner), F32)],
         compiler_params=pltpu.CompilerParams(vmem_limit_bytes=24 * MIB),
         name="gate",
-    )(in_hbm(normed), in_hbm(upstream_b), in_hbm(w_z), in_hbm(w_out))
+    )(normed, upstream_b, in_hbm(w_z), in_hbm(w_out))
 
 
 def key_query_of(one, two, rows, count):
@@ -304,7 +304,9 @@
             key = pick(kb, rows, n, t)
             query = pick(kb, rows, states + n, t)
             state = carried[n]
-            slots[block % 2, i, n] = state
+            if n % 2:
+                pair = jnp.concatenate([carried[n - 1], state], axis=0)
+                slots[block % 2, i, n // 2] = pair.astype(BF16)
             state = state + (size * key) * (mix - key * state)
             term = query * state
             sums[n % 4] = term if sums[n % 4] is None else sums[n % 4] + term
@@ -349,13 +351,13 @@
             full(F32),
             full(F32),
             jax.ShapeDtypeStruct((SUB, LANES), F32),
-            pltpu.HBM((rows, states, SUB, LANES), F32),
+            pltpu.HBM((rows, states // 2, 2 * SUB, LANES), BF16),
             jax.ShapeDtypeStruct((states, SUB, LANES), F32),
         ],
         scratch_shapes=[pltpu.VMEM((rows * SUB, LANES), F32)] * 3
         + [
             pltpu.VMEM((2 * states * rows, LANES), F32),
-            pltpu.VMEM((2, rows // 4, states, SUB, LANES), F32),
+            pltpu.VMEM((2, rows // 8, states // 2, 2 * SUB, LANES), BF16),
             pltpu.SemaphoreType.DMA((2,)),
         ],
         compiler_params=pltpu.CompilerParams(vmem_limit_bytes=26 * MIB),
@@ -418,7 +420,9 @@
         for n in range(states):
             key = pick(kb, rows, n, t)
             query = pick(kb, rows, states + n, t)
-            state = slots[block % 2, i, n]
+            if n % 2 == 0:
+                pair = slots[block % 2, i, n // 2].astype(F32)
+            state = pair[n % 2 * SUB : (n % 2 + 1) * SUB]
             full = query * grad + carried[n]
             by_key = full * key
             by_state = by_key * state
@@ -448,14 +452,14 @@
         if block >= 2:
             fetch(block - 2).start()
 
-    total_norm = jnp.zeros((rows, 1), F32)
+    total_norm = jnp.zeros((rows, LANES), F32)
     for j in range(SUB):
         at = slice(j * LANES, (j + 1) * LANES)
         drive_grad = lay_rows(sum_d, rows, j)
         size = step_in[:, at]
         grad_step = drive_grad * mixed[:, at].astype(F32) - lay_rows(sum_s, rows, j)
         gmix[:, at] = drive_grad * size
-        total_norm = total_norm - jnp.sum(grad_step * size * size, axis=1, keepdims=True)
+        total_norm = total_norm - grad_step * size * size
         raw = raw_in[:, at]
         plus = 1.0 + raw.astype(BF16).astype(F32) * norm
         pre = grad_step / (plus * plus) * raw * (1.0 - raw)
@@ -467,19 +471,20 @@
     rank_b = (one[:rows, :] + two[:rows, :]).astype(BF16)
     ups[:rank, :] = mm_tn(rank_b, preb[...])
 
-    source = lax.broadcasted_iota(jnp.int32, (LANES, LANES), 1)
+    blocks = [zk[pl.ds(n * span, rows), :].astype(BF16) for n in range(states)]
+    blocks += [zq[pl.ds(n * span + 1, rows), :].astype(BF16) for n in range(states)]
+    norm_high = total_norm.astype(BF16)
+    blocks += [norm_high, (total_norm - norm_high.astype(F32)).astype(BF16)]
+    shape = (LANES * len(blocks), LANES)
+    block = lax.broadcasted_iota(jnp.int32, shape, 0) // LANES
+    target = jnp.minimum(block, 2 * states)
+    weight = jnp.where(block < states, 2.0, 1.0)
+    chosen = jnp.where(target == lax.broadcasted_iota(jnp.int32, shape, 1), weight, 0.0)
+    table = mm(jnp.concatenate(blocks, axis=1), chosen.astype(BF16))
     lane = lax.broadcasted_iota(jnp.int32, (rows, LANES), 1)
     row = lax.broadcasted_iota(jnp.int32, (rows, LANES), 0)
-    table = jnp.where(lane == 2 * states, jnp.broadcast_to(total_norm, (rows, LANES)), 0.0)
     mark = (lane == 2 * states + 1) & (row == place[1])
     table = jnp.where(mark, jnp.broadcast_to(peak[0:1, :], (rows, LANES)), table)
-    for n in range(states):
-        table = table + mm(
-            zk[pl.ds(n * span, rows), :], jnp.where(source == n, 2.0, 0.0)
-        )
-        table = table + mm(
-            zq[pl.ds(n * span + 1, rows), :], jnp.where(source == states + n, 1.0, 0.0)
-        )
     flat = jnp.transpose(table)
     high = (pay.shape[0] - rows) * LANES // rows
     for c in range(rows // LANES):
@@ -517,7 +522,7 @@
             pltpu.VMEM((unroll * 2 * states * SUB, LANES), F32),
             pltpu.VMEM((states * span, LANES), F32),
             pltpu.VMEM((states * span, LANES), F32),
-            pltpu.VMEM((2, rows // 4, states, SUB, LANES), F32),
+            pltpu.VMEM((2, rows // 8, states // 2, 2 * SUB, LANES), BF16),
             pltpu.SemaphoreType.DMA((2,)),
         ],
         compiler_params=pltpu.CompilerParams(vmem_limit_bytes=32 * MIB),
@@ -600,7 +605,7 @@
 ):
     rows, inner = mixed.shape
     rank, count = w_down.shape[1], w_keyq.shape[0]
-    blk = min(inner, 256)
+    blk = min(inner, 512)
     high = 8 * SMALL
     whole = lambda value: pl.BlockSpec(value.shape, lambda i: (0,) * value.ndim)
     cols = lambda height: pl.BlockSpec((height, blk), lambda i: (0, i))
@@ -641,17 +646,17 @@
 
 
 def branch_kernel(pins, place, gated, wo, tok, *rest):
-    send, keep = rest[pins:]
+    send, keep, keep_far = rest[pins:]
     i = pl.program_id(0)
     value = mm(gated[...], wo[...])
 
     @pl.when(i == 0)
     def _():
-        keep[0] = value + tok[...].astype(F32)
+        keep[...] = value + tok[...].astype(F32)
 
     @pl.when(i == 2)
     def _():
-        keep[0] = value
+        keep_far[...] = value
 
     @pl.when(i % 2 == 1)
     def _():
@@ -675,12 +680,14 @@
             + [ANY] * len(pins),
             out_specs=[
                 pl.BlockSpec((1, 1, rows, own), lambda i, place: (i // 2, 0, 0, 0)),
-                pl.BlockSpec((1, rows, own), lambda i, place: (i // 2, 0, 0)),
+                pl.BlockSpec((rows, own), lambda i, place: (0, 0)),
+                pl.BlockSpec((rows, own), lambda i, place: (0, 0)),
             ],
         ),
         out_shape=[
             pltpu.HBM((parts // 2, 2, rows, own), BF16),
-            pltpu.HBM((parts // 2, rows, own), F32),
+            pltpu.HBM((rows, own), F32),
+            pltpu.HBM((rows, own), F32),
         ],
         compiler_params=pltpu.CompilerParams(vmem_limit_bytes=16 * MIB),
         name="branch",
@@ -692,10 +699,10 @@
 ):
     if extra:
         keep_z, come_z = rest[:2]
-        grad_z = rest[pins + 2 + 6]
+        grad_z = rest[pins + 2 + 7]
         grad_z[...] = keep_z[...] + come_z[...].astype(F32)
-        rest = rest[2 : pins + 2 + 6] + rest[pins + 2 + 7 :]
-    send, keep, stats, slope, shift, base, inv, dots = rest[pins:]
+        rest = rest[2 : pins + 2 + 7] + rest[pins + 2 + 8 :]
+    send, keep, keep_far, stats, slope, shift, base, inv, dots = rest[pins:]
     i = pl.program_id(0)
     rows, width = tok.shape
 
@@ -724,9 +731,13 @@
         shift[...] = unit * rms * (1.0 / width)
         base[...] = cot[...].astype(F32) * weights[ids[0]]
 
-    @pl.when(i % 2 == 0)
-    def _():
-        keep[0] = value
+    @pl.when(i == 0)
+    def _():
+        keep[...] = value
+
+    @pl.when(i == 2)
+    def _():
+        keep_far[...] = value
 
     @pl.when(i % 2 == 1)
     def _():
@@ -776,7 +787,8 @@
             + [ANY] * len(pins),
             out_specs=[
                 pl.BlockSpec((1, 1, rows, own), lambda i, place: (i // 2, 1, 0, 0)),
-                pl.BlockSpec((1, rows, own), lambda i, place: (i // 2, 0, 0)),
+                mine,
+                mine,
             ]
             + [whole((stat_rows, LANES)), mine, mine, mine]
             + [strip(value) for value in extra[:1]],
@@ -784,7 +796,8 @@
         ),
         out_shape=[
             pltpu.HBM((parts // 2, 2, rows, own), BF16),
-            pltpu.HBM((parts // 2, rows, own), F32),
+            pltpu.HBM((rows, own), F32),
+            pltpu.HBM((rows, own), F32),
             jax.ShapeDtypeStruct((stat_rows, LANES), F32),
         ]
         + [pltpu.HBM((rows, own), F32)] * 3
@@ -794,14 +807,15 @@
         name="inputs",
     )(
         place, group_ids, group_weights, in_hbm(half_sent), in_hbm(prex), in_hbm(prez), in_hbm(w_x), in_hbm(w_z), in_hbm(tokens),
-        in_hbm(tokens), in_hbm(cotangent), in_hbm(norm_gain[None]), *extra, *pins,
+        in_hbm(tokens), in_hbm(cotangent), in_hbm(norm_gain[None]),
+        *[in_hbm(value) for value in extra[:1]], *extra[1:], *pins,
     )
 
 
 def middle_kernel(
     place, gated, gated_far, up_own, up_a, up_b, every, wo, tok, small, small_come, *rest
 ):
-    keep_out, later, send_out, send, keep, small_keep, small_send = rest[len(rest) - 7 :]
+    keep_out, later, send_out, send, keep, keep_far, small_keep, small_send = rest[len(rest) - 8 :]
     i = pl.program_id(0)
 
     @pl.when(i == 0)
@@ -820,17 +834,18 @@
     total = total + mm_tn(gated_far[other, :], up_b[...])
     keep_out[...] = total[:, :own]
     later[...] = total[:, own : 2 * own]
-    send_out[...] = total[:, 2 * own :].astype(BF16)
+    send_out[0] = total[:, 2 * own : 3 * own].astype(BF16)
+    send_out[1] = total[:, 3 * own :].astype(BF16)
 
     value = mm(every[...], wo[...])
 
     @pl.when(i == 0)
     def _():
-        keep[0] = value + tok[...].astype(F32)
+        keep[...] = value + tok[...].astype(F32)
 
     @pl.when(i == 2)
     def _():
-        keep[0] = value
+        keep_far[...] = value
 
     @pl.when(i % 2 == 1)
     def _():
@@ -863,18 +878,20 @@
             out_specs=[
                 down(out),
                 down(out),
-                down(2 * out),
+                pl.BlockSpec((2, blk, out), lambda i, place: (0, i, 0)),
                 pl.BlockSpec((1, 1, rows, own), lambda i, place: (i // 2, 0, 0, 0)),
-                pl.BlockSpec((1, rows, own), lambda i, place: (i // 2, 0, 0)),
+                pl.BlockSpec((rows, own), lambda i, place: (0, 0)),
+                pl.BlockSpec((rows, own), lambda i, place: (0, 0)),
             ]
             + [pl.BlockSpec((2, SMALL, inner), lambda i, place: (0, 0, 0))] * 2,
         ),
         out_shape=[
             pltpu.HBM((inner, out), F32),
             pltpu.HBM((inner, out), F32),
-            pltpu.HBM((inner, 2 * out), BF16),
+            pltpu.HBM((2, inner, out), BF16),
             pltpu.HBM((parts // 2, 2, rows, own), BF16),
-            pltpu.HBM((parts // 2, rows, own), F32),
+            pltpu.HBM((rows, own), F32),
+            pltpu.HBM((rows, own), F32),
             pltpu.HBM((2, SMALL, inner), F32),
             pltpu.HBM((2, SMALL, inner), BF16),
         ],
@@ -904,10 +921,10 @@
             )
 
     grad_x[...] = keep_x[...] + come_x[...].astype(F32)
-    grad_out[...] = keep_out[...] + come_out[...].astype(F32) + far_out[...].astype(F32)
-    value = keep_a[0] + come_a[0, 0].astype(F32) + far_a[0].astype(F32)
+    grad_out[...] = keep_out[...] + come_out[0].astype(F32) + far_out[...].astype(F32)
+    value = keep_a[...] + come_a[0, 0].astype(F32) + far_a[0].astype(F32)
     block[...] = value.astype(BF16)
-    value = keep_b[0] + come_b[0, 0].astype(F32) + far_b[0].astype(F32)
+    value = keep_b[...] + come_b[0, 0].astype(F32) + far_b[0].astype(F32)
     some = value.shape[0]
     dot = dots[pl.ds(pl.multiple_of(i * some, some), some), :][:, 0:1]
     grad_in[...] = value * slope[...] - shift[...] * dot + base[...]
@@ -915,8 +932,8 @@
     @pl.when(i == pl.num_programs(0) - 1)
     def _():
         size = g0.shape[0] // 2
-        pieces = [(0, g0, 0), (4, g0, 1), (2, g2, 0), (6, g2, 1)]
-        pieces += [(p, g3, i) for i, p in enumerate((1, 5, 3, 7))]
+        pieces = [(0, g0, 0), (4, g0, 1), (1, g2, 0), (5, g2, 1)]
+        pieces += [(p, g3, i) for i, p in enumerate((2, 6, 3, 7))]
         for p, source, i in pieces:
             at = pl.ds(pl.multiple_of((place[0] ^ p) * size, SUB), size)
             table[at, :] = source[i * size : (i + 1) * size, :].astype(F32)
@@ -939,10 +956,10 @@
 ):
     size, inner = keep_x.shape
     rows, own = slope.shape
-    steps = 4
+    steps = 2
     whole = lambda shape: pl.BlockSpec(shape, lambda i: (0,) * len(shape))
     strip = lambda high, wide: pl.BlockSpec((high // steps, wide), lambda i: (i, 0))
-    kept = pl.BlockSpec((1, rows // steps, own), lambda i: (0, i, 0))
+    kept = strip(rows, own)
     came = lambda j: pl.BlockSpec((1, 1, rows // steps, own), lambda i: (0, j, i, 0))
     last = lambda j: pl.BlockSpec((1, rows // steps, own), lambda i: (j, i, 0))
     out = keep_out.shape[1]
@@ -951,7 +968,8 @@
         grid=(steps,),
         in_specs=[pl.BlockSpec(memory_space=pltpu.SMEM)]
         + [strip(size, inner)] * 2
-        + [strip(inner, out)] * 3
+        + [strip(inner, out)]
+        + [pl.BlockSpec((1, inner // steps, out), lambda i: (0, i, 0)), strip(inner, out)]
         + [kept, kept, came(0), came(1), last(0), last(1)]
         + [whole(stats.shape)]
         + [strip(rows, own)] * 3
@@ -981,11 +999,11 @@
             jax.ShapeDtypeStruct((SUB, LANES), F32),
         ],
         scratch_shapes=[pltpu.VMEM((8 * SMALL, inner), F32), pltpu.VMEM((rows, LANES), F32)],
-        compiler_params=pltpu.CompilerParams(vmem_limit_bytes=24 * MIB),
+        compiler_params=pltpu.CompilerParams(vmem_limit_bytes=32 * MIB),
         name="finale",
     )(
-        place, in_hbm(keep_x), come_x, in_hbm(keep_out), come_out, far_out, in_hbm(out_keep),
-        in_hbm(keep), come, come, far, far, stats, in_hbm(slope), in_hbm(shift), in_hbm(base),
+        place, in_hbm(keep_x), in_hbm(come_x), in_hbm(keep_out), in_hbm(come_out), in_hbm(far_out),
+        in_hbm(out_keep), in_hbm(keep), in_hbm(come), in_hbm(come), in_hbm(far), in_hbm(far), stats, in_hbm(slope), in_hbm(shift), in_hbm(base),
         *pieces,
     )
 
@@ -1138,33 +1156,36 @@
     if blocked:
         prex_far = swap(prex_b, "dp", 2)
         prex_near = swap(prex_b, "dp", 1)
-        keep_z, send_z = in_weight(sides, (prez_b, prez_far, prez_near, prez_last), (prex_b,))
+        keep_z, send_z = in_weight(
+            sides, (prez_b, prez_far, prez_near, prez_last), (in_hbm(prex_b),)
+        )
         come_z = swap(send_z, "dp", 4)
-        keep_out, later, send_out, half_sent, out_keep, small, small_send = middle(
+        keep_out, later, send_out, half_sent, out_keep, out_far, small, small_send = middle(
             place, gated_b, gated_far, up_parts, w_out, tokens, small,
-            swap(small_send, "dp", 1), parts, (send_z, prex_far, prex_near),
+            swap(small_send, "dp", 1), parts,
+            (in_hbm(send_z), prex_far, prex_near),
         )
         prex_last = swap(prex_far, "dp", 1)
-        come_out = swap(send_out, "dp", 1)
         keep_x, send_x = in_weight(
-            sides, (prex_b, prex_far, prex_near, prex_last), (send_out, come_z)
+            sides, (prex_b, prex_far, prex_near, prex_last), (in_hbm(send_out), come_z)
         )
         come_x = swap(send_x, "dp", 4)
-        (small_send,) = after((small_send,), (send_x,))
+        come_out = swap(send_out, "dp", 1)
+        (small_send,) = after((small_send,), (in_hbm(send_x),))
         small = small + swap(small_send, "dp", 2).astype(F32)
-        pins_inputs = (send_x,)
+        pins_inputs = (in_hbm(send_x),)
         extra = (keep_z, come_z)
     else:
-        half_sent, out_keep = branch(place, gated_b, w_out, tokens, parts, ())
-    send, keep, stats, slope, shift, base, *grad_wz = input_grad(
+        half_sent, out_keep, out_far = branch(place, gated_b, w_out, tokens, parts, ())
+    send, keep, keep_far, stats, slope, shift, base, *grad_wz = input_grad(
         place, group_ids, group_weights, half_sent, prex_b, prez_b, w_x, w_z, tokens, cotangent,
         norm_gain, parts, extra, pins_inputs,
     )
     if blocked:
         (grad_wz,) = grad_wz
-        cut = later.shape[1]
-        far_out = swap((later + come_out[:, cut:].astype(F32)).astype(BF16), "dp", 2)
-        send, stats, small = after((send, stats, small), (come_x, come_out))
+        far_send = (later + come_out[1].astype(F32)).astype(BF16)
+        far_out = swap(far_send, "dp", 2)
+        stats, small = after((stats, small), (in_hbm(come_x), in_hbm(come_out)))
     else:
 
         def weight_grad(value, left):
@@ -1177,13 +1198,13 @@
         grad_wx = weight_grad(prex_b, False)
 
     come = swap(send, "state", 1)
-    pair = jnp.stack([out_keep[1], keep[1]]) + come[1].astype(F32)
-    come_far = swap(pair.astype(BF16), "state", 2)
+    pair = [(a + b.astype(F32)).astype(BF16) for a, b in zip((out_far, keep_far), come[1])]
+    come_far = swap(jnp.stack(pair), "state", 2)
     stats = all_sum(stats, "state")
     if not blocked:
-        block_out = out_keep[0] + come[0, 0].astype(F32) + come_far[0].astype(F32)
+        block_out = out_keep + come[0, 0].astype(F32) + come_far[0].astype(F32)
         block_out = block_out.astype(BF16)
-        norm_grad = keep[0] + come[0, 1].astype(F32) + come_far[1].astype(F32)
+        norm_grad = keep + come[0, 1].astype(F32) + come_far[1].astype(F32)
         row_stat = stats[: rows // LANES].reshape(rows, 1)
         grad_in = norm_grad * slope - shift * row_stat + base
     gain_rows = own_width // LANES
@@ -1199,12 +1220,14 @@
         gathered = (small + swap(flipped, "dp", 4).astype(F32)).astype(BF16)
         gain = gain + swap(gain, "dp", 4)
         pieces = [gathered]
-        for bit, pins in ((2, (come,)), (1, (come_far, far_out))):
+        for bit, pins in ((1, (in_hbm(come), in_hbm(far_send))), (2, ())):
             high = lax.reduce_precision(gain, 8, 7)
             rest = lax.reduce_precision(gain - high, 8, 7)
             line = jnp.concatenate([high.reshape(1, -1), rest.reshape(1, -1)], axis=1)
             tail = jnp.pad(line.astype(BF16), ((0, SUB - 1), (0, 0)))
-            (whole,) = after((jnp.concatenate([gathered, tail], axis=0),), pins)
+            whole = jnp.concatenate([gathered, tail], axis=0)
+            if pins:
+                (whole,) = after((whole,), pins)
             got = swap(whole, "dp", bit)
             pieces.append(got[:-SUB])
             gathered = jnp.concatenate([gathered, got[:-SUB]], axis=0)

time: 193 us -> 180 us (0.933)
  local copies, waits for them, and re-layouts: 17.6 us -> 5.96 us
  waiting for transfers between devices: 46.1 us -> 54.8 us
  Pallas kernels: 85.5 us -> 81.2 us
  starting transfers between devices: 31.3 us -> 27.8 us
    ppermute x30, waiting for transfers between devices: 46.1 us -> 54.8 us  [swap(): return lax.ppermute(value, axis, [(i, i ^ bit) for i in range(size)])]
    unnamed x54 -> x32, local copies, waits for them, and re-layouts: 12.5 us -> 4.66 us
    slice x2 -> x0, local copies, waits for them, and re-layouts: 3.77 us -> none  [per_device(): pair = jnp.stack([out_keep[1], keep[1]]) + come[1].astype(F32)]
    ppermute x30, starting transfers between devices: 31.3 us -> 27.8 us  [swap(): return lax.ppermute(value, axis, [(i, i ^ bit) for i in range(size)])]
  transfers between devices with their start and end apart: 30 -> 30, of which waited for: 11 -> 13; matrix products, arithmetic and copies ran while one was open for 6% -> 5% of each run, Pallas kernels for 37% -> 38%
where the time goes in v3:
time: 180 us
  Pallas kernels  81.2 us (45%)
  waiting for transfers between devices  54.8 us (30%)
  starting transfers between devices  27.8 us (15%)
  other arithmetic  8.34 us (5%)
  local copies, waits for them, and re-layouts  5.96 us (3%)
    ppermute x30, waiting for transfers between devices, swap(): return lax.ppermute(value, axis, [(i, i ^ bit) for i in range(size)])  54.8 us
    ppermute x30, starting transfers between devices, swap(): return lax.ppermute(value, axis, [(i, i ^ bit) for i in range(size)])  27.8 us
    pallas_call x1, Pallas kernels, scan_backward(): pl.pallas_call(functools.partial(back_kernel, unroll, len(pins)), in_spec...  19.4 us
    pallas_call x1, Pallas kernels, scan_forward(): pl.pallas_call(functools.partial(scan_kernel, 4), in_specs=[WHOLE] * 8, o...  11 us
    pallas_call x1, Pallas kernels, input_grad(): pl.pallas_call(functools.partial(input_kernel, len(pins), len(extra)), gr...  10.3 us
    pallas_call x1, Pallas kernels, middle(): pl.pallas_call(middle_kernel, grid_spec=pltpu.PrefetchScalarGridSpec(num_...  8.45 us
    pallas_call x2, Pallas kernels, in_weight(): pl.pallas_call(functools.partial(in_weight_kernel, len(pins)), grid=(2,),...  7.73 us
    pallas_call x1, Pallas kernels, front(): pl.pallas_call(functools.partial(front_kernel, blocked), grid=(inner // b...  7.54 us
  transfers between devices with their start and end apart: 30, of which 13 were waited for; matrix products, arithmetic and copies ran while one was open for 5% of the time, Pallas kernels for 38%

profile of v3, /device:TPU:0, one launch (start us, length us, event | category | flops | bytes accessed | tf_op | source)
XLA Modules:
  0.0 179.6 jit_solution(17605813933586492268)
XLA Ops:
  2.0 7.5 %front.1 = (bf16[256,2048]{1,0:T(8,128)(2,1)S(1)}, bf16[256,2048]{1,0:T(8,128)(2,1)S(1)}, f32[256,1024]{1,0:T(8,128)}, bf16[256,1024]{1,0:T(8,128)(2,1)}, f32[25...) custom-call(s32[2]{0:T(128)S(1)} %pad_add_fusion.place, ...), custom_call_target="tpu_custom_call" | custom-call | tf_op jit(solution)/shard_map/front/pallas_call | solution.py:167
  10.1 2.6 %collective-permute-start.1 = (bf16[2,256,512]{2,1,0:T(8,128)(2,1)}, bf16[2,256,512]{2,1,0:T(8,128)(2,1)S(1)}, u32[]{:S(2)}, u32[]{:S(2)}) collective-permute-start(bf16[2,256,512]{2,1,0:T(8,128)(2,1)} %get-tuple-element.77), channel_id=1, source_target_pairs={{0,4},{4,0},{8,12},{12,8},{16,20},{20,16},{24,28},{28,24},{1,5},{5... | collective-permute-start | bytes 1572872 | tf_op jit(solution)/shard_map/ppermute | solution.py:35
  12.7 1.6 collective-permute-start.4
  14.3 1.6 collective-permute-start
  15.8 2.6 %collective-permute-start.5 = (bf16[128,1024]{1,0:T(8,128)(2,1)}, bf16[128,1024]{1,0:T(8,128)(2,1)S(1)}, u32[]{:S(2)}, u32[]{:S(2)}) collective-permute-start(bf16[128,1024]{1,0:T(8,128)(2,1)} %get-tuple-element.90), channel_id=1, source_target_pairs={{0,16},{4,20},{8,24},{12,28},{16,0},{20,4},{24,8},{28,12},{1,17},{... | collective-permute-start | bytes 786440 | tf_op jit(solution)/shard_map/ppermute | solution.py:35
  18.4 5.8 %gate.1 = (f32[256,1024]{1,0:T(8,128)S(1)}, f32[256,1024]{1,0:T(8,128)S(1)}, f32[256,1024]{1,0:T(8,128)}) custom-call(bf16[256,2048]{1,0:T(8,128)(2,1)S(1)} %get-tuple-element.80.normed, bf16[256,2048]{1,0:T(8,128)(2,1)S(1)} %get-tuple-element.81.up, bf16[2048,1024]{1,0:T(8,128)(2,1)} %wz.3, bf16[1024,2048]{1,0:T(8,128)(2,1)} %wo.3), custom_call_target="tpu_custom_call" | custom-call | tf_op jit(solution)/shard_map/gate/pallas_call | solution.py:227
  24.2 11.0 %scan.1 = (bf16[256,1024]{1,0:T(8,128)(2,1)}, bf16[256,1024]{1,0:T(8,128)(2,1)}, f32[256,1024]{1,0:T(8,128)S(1)}, f32[256,1024]{1,0:T(8,128)S(1)}, f32[8,128]{1,...) custom-call(f32[320,128]{1,0:T(8,128)S(1)} %add.65.one, ...), custom_call_target="tpu_custom_call" | custom-call | tf_op jit(solution)/shard_map/scan/pallas_call | solution.py:344
  35.7 1.3 collective-permute-start.10
  37.4 19.4 %back.1 = (f32[256,1024]{1,0:T(8,128)}, f32[336,128]{1,0:T(8,128)S(1)}, f32[136,1024]{1,0:T(8,128)}) custom-call(s32[2]{0:T(128)S(1)} %pad_add_fusion.place, f32[320,128]{1,0:T(8,128)S(1)} %add.65.one, f32[320,128]{1,0:T(8,128)S(1)} %collective-permute-done.4.two, bf16[256,1024]{1,0:T(8,128)(2,1)} %get-tuple-element.79.mixed, bf16[128,1024]{1,0:T(8,128)(2,1)} %wup.3, ...), custom_call_target="tpu_custom_call" | custom-call | tf_op jit(solution)/shard_map/back/pallas_call | solution.py:501
  57.3 0.7 slice_bitcast_fusion.3
  58.4 1.6 collective-permute-start.2
  60.0 0.7 add.66.grad_one
  61.5 0.7 collective-permute-start.16
  62.2 5.4 %collective-permute-done.2.rest_3_.l3 = bf16[256,512]{1,0:T(8,128)(2,1)S(1)} collective-permute-done((bf16[256,512]{1,0:T(8,128)(2,1)}, bf16[256,512]{1,0:T(8,128)(2,1)S(1)}, u32[]{:S(2)}, u32[]{:S(2)}) %collective-permute-start.2) | collective-permute-done | bytes 262176 | tf_op jit(solution)/shard_map/ppermute | solution.py:35
  67.6 5.8 %conv.1 = (bf16[256,1024]{1,0:T(8,128)(2,1)}, f32[4,40,1024]{2,1,0:T(8,128)}, bf16[4,40,1024]{2,1,0:T(8,128)(2,1)}) custom-call(s32[2]{0:T(128)S(1)} %pad_add_fusion.place, f32[320,128]{1,0:T(8,128)S(1)} %add.65.one, f32[320,128]{1,0:T(8,128)S(1)} %collective-permute-done.4.two, f32[336,128]{1,0:T(8,128)} %add.66.grad_one, ...), custom_call_target="tpu_custom_call" | custom-call | tf_op jit(solution)/shard_map/conv/pallas_call | solution.py:618
  73.4 1.2 collective-permute-start.11
  74.6 0.7 collective-permute-start.12
  75.3 1.3 collective-permute-start.14
  76.6 3.9 %inw.2 = (f32[256,1024]{1,0:T(8,128)}, bf16[256,1024]{1,0:T(8,128)(2,1)}) custom-call(bf16[256,512]{1,0:T(8,128)(2,1)} %get-tuple-element.75.l0, bf16[256,512]{1,0:T(8,128)(2,1)S(1)} %collective-permute-done.rest_0_.l1, bf16[2,256,512]{2,1,0:T(8,128)(2,1)S(1)} %collective-permute-done.1.rest_1_.l2, bf16[256,512]{1,0:T(8,128)(2,1)S(1)} %collective-permute-done.2.rest_3_.l3, ...), custom_call_target="tpu_custom_call" | custom-call | tf_op jit(solution)/shard_map/inw/pallas_call | solution.py:1033
  80.5 2.6 %collective-permute-start.17 = (bf16[256,1024]{1,0:T(8,128)(2,1)}, bf16[256,1024]{1,0:T(8,128)(2,1)S(1)}, u32[]{:S(2)}, u32[]{:S(2)}) collective-permute-start(bf16[256,1024]{1,0:T(8,128)(2,1)} %get-tuple-element.102.rest_0_), channel_id=1, source_target_pairs={{0,16},{4,20},{8,24},{12,28},{16,0},{20,4},{24,8},{28,12},{1,17},{... | collective-permute-start | bytes 1572872 | tf_op jit(solution)/shard_map/ppermute | solution.py:35
  83.1 10.2 %collective-permute-done.11.rest_1_.r1 = bf16[256,1024]{1,0:T(8,128)(2,1)S(1)} collective-permute-done((bf16[256,1024]{1,0:T(8,128)(2,1)}, bf16[256,1024]{1,0:T(8,128)(2,1)S(1)}, u32[]{:S(2)}, u32[]{:S(2)}) %collective-permute-start.11) | collective-permute-done | bytes 524320 | tf_op jit(solution)/shard_map/ppermute | solution.py:35
  93.3 0.7 collective-permute-start.13
  94.1 0.9 collective-permute-done.14.small_come
  94.9 8.4 %middle.1 = (f32[1024,256]{1,0:T(8,128)}, f32[1024,256]{1,0:T(8,128)}, bf16[2,1024,256]{2,1,0:T(8,128)(2,1)}, bf16[2,2,256,512]{3,2,1,0:T(8,128)(2,1)}, f32[256,...) custom-call(s32[2]{0:T(128)S(1)} %pad_add_fusion.place, ...), custom_call_target="tpu_custom_call" | custom-call | tf_op jit(solution)/shard_map/middle/pallas_call | solution.py:864
  103.4 0.8 collective-permute-start.19
  104.2 1.2 collective-permute-done.17.rest_1_
  105.4 2.3 %collective-permute-done.13.r3 = bf16[256,1024]{1,0:T(8,128)(2,1)S(1)} collective-permute-done((bf16[256,1024]{1,0:T(8,128)(2,1)S(1)}, bf16[256,1024]{1,0:T(8,128)(2,1)S(1)}, u32[]{:S(2)}, u32[]{:S(2)}) %collective-permute-start.13) | collective-permute-done | bytes 524320 | tf_op jit(solution)/shard_map/ppermute | solution.py:35
  107.8 3.9 %inw.3 = (f32[256,1024]{1,0:T(8,128)}, bf16[256,1024]{1,0:T(8,128)(2,1)}) custom-call(bf16[256,512]{1,0:T(8,128)(2,1)} %get-tuple-element.75.l0, bf16[256,512]{1,0:T(8,128)(2,1)S(1)} %collective-permute-done.rest_0_.l1, bf16[2,256,512]{2,1,0:T(8,128)(2,1)S(1)} %collective-permute-done.1.rest_1_.l2, bf16[256,512]{1,0:T(8,128)(2,1)S(1)} %collective-permute-done.2.rest_3_.l3, ...), custom_call_target="tpu_custom_call" | custom-call | tf_op jit(solution)/shard_map/inw/pallas_call | solution.py:1033
  111.6 2.5 %collective-permute-start.18 = (bf16[256,1024]{1,0:T(8,128)(2,1)}, bf16[256,1024]{1,0:T(8,128)(2,1)S(1)}, u32[]{:S(2)}, u32[]{:S(2)}) collective-permute-start(bf16[256,1024]{1,0:T(8,128)(2,1)} %get-tuple-element.105.rest_2_.refs_1_), channel_id=1, source_target_pairs={{0,16},{4,20},{8,24},{12,28},{16,0},{20,4},{24,8},{28,12},{1,17},{... | collective-permute-start | bytes 1572872 | tf_op jit(solution)/shard_map/ppermute | solution.py:35
  114.6 10.3 %inputs.1 = (bf16[2,2,256,512]{3,2,1,0:T(8,128)(2,1)}, f32[256,512]{1,0:T(8,128)}, f32[256,512]{1,0:T(8,128)}, f32[18,128]{1,0:T(8,128)S(1)}, f32[256,512]{1,0:T...) custom-call(s32[2]{0:T(128)S(1)} %pad_add_fusion.place, ...), custom_call_target="tpu_custom_call", output_to_operand_aliasing={{0}: (3, {})} | custom-call | tf_op jit(solution)/shard_map/inputs/pallas_call | solution.py:768
  125.5 0.7 collective-permute-done.23
  126.2 0.8 convert_add_fusion.3.refs_1_
  126.9 7.5 %collective-permute-done.18.refs_2_.come_x = bf16[256,1024]{1,0:T(8,128)(2,1)S(1)} collective-permute-done((bf16[256,1024]{1,0:T(8,128)(2,1)}, bf16[256,1024]{1,0:T(8,128)(2,1)S(1)}, u32[]{:S(2)}, u32[]{:S(2)}) %collective-permute-start.18) | collective-permute-done | bytes 524320 | tf_op jit(solution)/shard_map/ppermute | solution.py:35
  134.5 0.8 copy-done.10
  135.6 1.1 reduce-precision_convert_fusion.2
  137.0 0.7 add.71
  138.4 3.1 %collective-permute-done.25 = f32[18,128]{1,0:T(8,128)S(1)} collective-permute-done((f32[18,128]{1,0:T(8,128)S(1)}, f32[18,128]{1,0:T(8,128)S(1)}, u32[]{:S(2)}, u32[]{:S(2)}) %collective-permute-start.25) | collective-permute-done | bytes 9248 | tf_op jit(solution)/shard_map/ppermute | solution.py:35
  141.5 2.3 %fusion.refs_2_ = bf16[1024,256]{1,0:T(8,128)(2,1)} fusion(f32[1024,256]{1,0:T(8,128)} %get-tuple-element.107, bf16[2,1024,256]{2,1,0:T(8,128)(2,1)} %copy-done.8), kind=kLoop, calls=%fused_computation.1 | loop fusion | flops 786432 | bytes 2097152 | tf_op jit(solution)/shard_map/convert_element_type | solution.py:1186
  143.8 5.1 %collective-permute-done.27 = f32[4,128]{1,0:T(4,128)S(1)} collective-permute-done((f32[4,128]{1,0:T(4,128)S(1)}, f32[4,128]{1,0:T(4,128)S(1)}, u32[]{:S(2)}, u32[]{:S(2)}) %collective-permute-start.27) | collective-permute-done | bytes 2080 | tf_op jit(solution)/shard_map/ppermute | solution.py:35
  149.0 0.7 pad_maximum_fusion.2.refs_0_
  149.6 1.0 copy-done.7
  150.6 0.7 collective-permute-start.28
  151.3 5.6 %collective-permute-done.28 = bf16[88,1024]{1,0:T(8,128)(2,1)S(1)} collective-permute-done((bf16[88,1024]{1,0:T(8,128)(2,1)}, bf16[88,1024]{1,0:T(8,128)(2,1)S(1)}, u32[]{:S(2)}, u32[]{:S(2)}) %collective-permute-start.28) | collective-permute-done | bytes 180256 | tf_op jit(solution)/shard_map/ppermute | solution.py:35
  157.2 1.2 fusion.4
  158.5 1.6 collective-permute-start.22
  160.1 12.1 %collective-permute-done.29 = bf16[168,1024]{1,0:T(8,128)(2,1)S(1)} collective-permute-done((bf16[168,1024]{1,0:T(8,128)(2,1)S(1)}, bf16[168,1024]{1,0:T(8,128)(2,1)S(1)}, u32[]{:S(2)}, u32[]{:S(2)}) %collective-permute-start.29) | collective-permute-done | bytes 344096 | tf_op jit(solution)/shard_map/ppermute | solution.py:35
  172.8 0.8 copy-done.11
  173.9 5.3 %finale.1 = (f32[256,1024]{1,0:T(8,128)}, f32[1024,256]{1,0:T(8,128)}, bf16[256,512]{1,0:T(8,128)(2,1)}, f32[256,512]{1,0:T(8,128)}, f32[128,1024]{1,0:T(8,128)}...) custom-call(s32[2]{0:T(128)S(1)} %pad_add_fusion.place, ...), custom_call_target="tpu_custom_call" | custom-call | tf_op jit(solution)/shard_map/finale/pallas_call | solution.py:966
  (90 shorter events, 7.9 us)
Async XLA Ops:
  1.4 0.7 copy-start.5
  9.6 3.1 %collective-permute-start.3 = (f32[320,128]{1,0:T(8,128)S(1)}, f32[320,128]{1,0:T(8,128)S(1)}, u32[]{:S(2)}, u32[]{:S(2)}) collective-permute-start(f32[320,128]{1,0:T(8,128)S(1)} %get-tuple-element.78), channel_id=1, source_target_pairs={{0,1},{1,0},{2,3},{3,2},{4,5},{5,4},{6,7},{7,6},{8,9},{9,8},{10,11... | collective-permute-start | bytes 491528 | tf_op jit(solution)/shard_map/ppermute | solution.py:35
  10.1 27.3 %collective-permute-start.1 = (bf16[2,256,512]{2,1,0:T(8,128)(2,1)}, bf16[2,256,512]{2,1,0:T(8,128)(2,1)S(1)}, u32[]{:S(2)}, u32[]{:S(2)}) collective-permute-start(bf16[2,256,512]{2,1,0:T(8,128)(2,1)} %get-tuple-element.77), channel_id=1, source_target_pairs={{0,4},{4,0},{8,12},{12,8},{16,20},{20,16},{24,28},{28,24},{1,5},{5... | collective-permute-start | bytes 1572872 | tf_op jit(solution)/shard_map/ppermute | solution.py:35
  12.7 11.5 %collective-permute-start.4 = (f32[320,128]{1,0:T(8,128)S(1)}, f32[320,128]{1,0:T(8,128)S(1)}, u32[]{:S(2)}, u32[]{:S(2)}) collective-permute-start(f32[320,128]{1,0:T(8,128)S(1)} %add.65.one), channel_id=1, source_target_pairs={{0,2},{1,3},{2,0},{3,1},{4,6},{5,7},{6,4},{7,5},{8,10},{9,11},{10,... | collective-permute-start | bytes 491528 | tf_op jit(solution)/shard_map/ppermute | solution.py:35
  14.3 22.8 %collective-permute-start = (bf16[256,512]{1,0:T(8,128)(2,1)}, bf16[256,512]{1,0:T(8,128)(2,1)S(1)}, u32[]{:S(2)}, u32[]{:S(2)}) collective-permute-start(bf16[256,512]{1,0:T(8,128)(2,1)} %get-tuple-element.76), channel_id=1, source_target_pairs={{0,8},{4,12},{8,0},{12,4},{16,24},{20,28},{24,16},{28,20},{1,9},{5... | collective-permute-start | bytes 786440 | tf_op jit(solution)/shard_map/ppermute | solution.py:35
  15.8 21.5 %collective-permute-start.5 = (bf16[128,1024]{1,0:T(8,128)(2,1)}, bf16[128,1024]{1,0:T(8,128)(2,1)S(1)}, u32[]{:S(2)}, u32[]{:S(2)}) collective-permute-start(bf16[128,1024]{1,0:T(8,128)(2,1)} %get-tuple-element.90), channel_id=1, source_target_pairs={{0,16},{4,20},{8,24},{12,28},{16,0},{20,4},{24,8},{28,12},{1,17},{... | collective-permute-start | bytes 786440 | tf_op jit(solution)/shard_map/ppermute | solution.py:35
  35.2 25.5 %collective-permute-start.15 = (bf16[256,1024]{1,0:T(8,128)(2,1)}, bf16[256,1024]{1,0:T(8,128)(2,1)S(1)}, u32[]{:S(2)}, u32[]{:S(2)}) collective-permute-start(bf16[256,1024]{1,0:T(8,128)(2,1)} %get-tuple-element.97.r0.prez), channel_id=1, source_target_pairs={{0,8},{4,12},{8,0},{12,4},{16,24},{20,28},{24,16},{28,20},{1,9},{5... | collective-permute-start | bytes 1572872 | tf_op jit(solution)/shard_map/ppermute | solution.py:35
  35.7 31.9 %collective-permute-start.10 = (bf16[256,1024]{1,0:T(8,128)(2,1)}, bf16[256,1024]{1,0:T(8,128)(2,1)S(1)}, u32[]{:S(2)}, u32[]{:S(2)}) collective-permute-start(bf16[256,1024]{1,0:T(8,128)(2,1)} %get-tuple-element.97.r0.prez), channel_id=1, source_target_pairs={{0,4},{4,0},{8,12},{12,8},{16,20},{20,16},{24,28},{28,24},{1,5},{5... | collective-permute-start | bytes 1572872 | tf_op jit(solution)/shard_map/ppermute | solution.py:35
  37.0 30.6 %collective-permute-start.8 = (bf16[256,1024]{1,0:T(8,128)(2,1)}, bf16[256,1024]{1,0:T(8,128)(2,1)S(1)}, u32[]{:S(2)}, u32[]{:S(2)}) collective-permute-start(bf16[256,1024]{1,0:T(8,128)(2,1)} %get-tuple-element.96.gated.every), channel_id=1, source_target_pairs={{0,16},{4,20},{8,24},{12,28},{16,0},{20,4},{24,8},{28,12},{1,17},{... | collective-permute-start | bytes 1572872 | tf_op jit(solution)/shard_map/ppermute | solution.py:35
  37.4 24.1 %collective-permute-start.9 = (bf16[128,1024]{1,0:T(8,128)(2,1)S(1)}, bf16[128,1024]{1,0:T(8,128)(2,1)S(1)}, u32[]{:S(2)}, u32[]{:S(2)}) collective-permute-start(bf16[128,1024]{1,0:T(8,128)(2,1)S(1)} %collective-permute-done.5.rest_2_.up_a), channel_id=1, source_target_pairs={{0,1},{1,0},{2,3},{3,2},{4,5},{5,4},{6,7},{7,6},{8,9},{9,8},{10,11... | collective-permute-start | bytes 786440 | tf_op jit(solution)/shard_map/ppermute | solution.py:35
  56.7 3.9 %copy-start.2 = (f32[336,128]{1,0:T(8,128)}, f32[336,128]{1,0:T(8,128)S(1)}, u32[]{:S(2)}) copy-start(f32[336,128]{1,0:T(8,128)S(1)} %get-tuple-element.91.refs_1_) | copy-start | bytes 516100
  56.8 1.6 collective-permute-start.6
  58.4 9.2 %collective-permute-start.2 = (bf16[256,512]{1,0:T(8,128)(2,1)}, bf16[256,512]{1,0:T(8,128)(2,1)S(1)}, u32[]{:S(2)}, u32[]{:S(2)}) collective-permute-start(bf16[256,512]{1,0:T(8,128)(2,1)} %slice_bitcast_fusion.3), channel_id=1, source_target_pairs={{0,8},{4,12},{8,0},{12,4},{16,24},{20,28},{24,16},{28,20},{1,9},{5... | collective-permute-start | bytes 786440 | tf_op jit(solution)/shard_map/ppermute | solution.py:35
  60.7 0.8 copy-start
  60.7 6.9 %collective-permute-start.7 = (f32[336,128]{1,0:T(8,128)}, f32[336,128]{1,0:T(8,128)}, u32[]{:S(2)}, u32[]{:S(2)}) collective-permute-start(f32[336,128]{1,0:T(8,128)} %add.66.grad_one), channel_id=1, source_target_pairs={{0,2},{1,3},{2,0},{3,1},{4,6},{5,7},{6,4},{7,5},{8,10},{9,11},{10,... | collective-permute-start | bytes 516104 | tf_op jit(solution)/shard_map/ppermute | solution.py:35
  61.5 15.1 %copy-start.1 = (bf16[256,1024]{1,0:T(8,128)(2,1)S(1)}, bf16[256,1024]{1,0:T(8,128)(2,1)}, u32[]{:S(2)}) copy-start(bf16[256,1024]{1,0:T(8,128)(2,1)} %after.4.r1) | copy-start | bytes 1572868
  61.5 15.1 %collective-permute-start.16 = (bf16[256,1024]{1,0:T(8,128)(2,1)}, bf16[256,1024]{1,0:T(8,128)(2,1)S(1)}, u32[]{:S(2)}, u32[]{:S(2)}) collective-permute-start(bf16[256,1024]{1,0:T(8,128)(2,1)} %after.4.r1), channel_id=1, source_target_pairs={{0,4},{4,0},{8,12},{12,8},{16,20},{20,16},{24,28},{28,24},{1,5},{5... | collective-permute-start | bytes 1572872 | tf_op jit(solution)/shard_map/ppermute | solution.py:35
  67.6 27.3 %copy-start.3 = (bf16[256,1024]{1,0:T(8,128)(2,1)S(1)}, bf16[256,1024]{1,0:T(8,128)(2,1)}, u32[]{:S(2)}) copy-start(bf16[256,1024]{1,0:T(8,128)(2,1)} %get-tuple-element.99.up_own) | copy-start | bytes 1572868
  73.4 19.9 %collective-permute-start.11 = (bf16[256,1024]{1,0:T(8,128)(2,1)}, bf16[256,1024]{1,0:T(8,128)(2,1)S(1)}, u32[]{:S(2)}, u32[]{:S(2)}) collective-permute-start(bf16[256,1024]{1,0:T(8,128)(2,1)} %get-tuple-element.98.rest_0_.r0.prex), channel_id=1, source_target_pairs={{0,8},{4,12},{8,0},{12,4},{16,24},{20,28},{24,16},{28,20},{1,9},{5... | collective-permute-start | bytes 1572872 | tf_op jit(solution)/shard_map/ppermute | solution.py:35
  74.6 20.3 %collective-permute-start.12 = (bf16[256,1024]{1,0:T(8,128)(2,1)}, bf16[256,1024]{1,0:T(8,128)(2,1)S(1)}, u32[]{:S(2)}, u32[]{:S(2)}) collective-permute-start(bf16[256,1024]{1,0:T(8,128)(2,1)} %get-tuple-element.98.rest_0_.r0.prex), channel_id=1, source_target_pairs={{0,4},{4,0},{8,12},{12,8},{16,20},{20,16},{24,28},{28,24},{1,5},{5... | collective-permute-start | bytes 1572872 | tf_op jit(solution)/shard_map/ppermute | solution.py:35
  75.3 19.6 %collective-permute-start.14 = (bf16[4,40,1024]{2,1,0:T(8,128)(2,1)}, bf16[4,40,1024]{2,1,0:T(8,128)(2,1)S(1)}, u32[]{:S(2)}, u32[]{:S(2)}) collective-permute-start(bf16[4,40,1024]{2,1,0:T(8,128)(2,1)} %get-tuple-element.101), channel_id=1, source_target_pairs={{0,4},{4,0},{8,12},{12,8},{16,20},{20,16},{24,28},{28,24},{1,5},{5... | collective-permute-start | bytes 983048 | tf_op jit(solution)/shard_map/ppermute | solution.py:35
  80.5 24.9 %collective-permute-start.17 = (bf16[256,1024]{1,0:T(8,128)(2,1)}, bf16[256,1024]{1,0:T(8,128)(2,1)S(1)}, u32[]{:S(2)}, u32[]{:S(2)}) collective-permute-start(bf16[256,1024]{1,0:T(8,128)(2,1)} %get-tuple-element.102.rest_0_), channel_id=1, source_target_pairs={{0,16},{4,20},{8,24},{12,28},{16,0},{20,4},{24,8},{28,12},{1,17},{... | collective-permute-start | bytes 1572872 | tf_op jit(solution)/shard_map/ppermute | solution.py:35
  93.3 14.5 %collective-permute-start.13 = (bf16[256,1024]{1,0:T(8,128)(2,1)S(1)}, bf16[256,1024]{1,0:T(8,128)(2,1)S(1)}, u32[]{:S(2)}, u32[]{:S(2)}) collective-permute-start(bf16[256,1024]{1,0:T(8,128)(2,1)S(1)} %collective-permute-done.11.rest_1_.r1), channel_id=1, source_target_pairs={{0,4},{4,0},{8,12},{12,8},{16,20},{20,16},{24,28},{28,24},{1,5},{5... | collective-permute-start | bytes 1572872 | tf_op jit(solution)/shard_map/ppermute | solution.py:35
  103.4 11.2 %copy-start.6 = (f32[8]{0:T(128)S(1)}, f32[8]{0:T(128)}, u32[]{:S(2)}) copy-start(f32[8]{0:T(128)} %weights.3) | copy-start | bytes 100
  103.4 31.1 %collective-permute-start.19 = (bf16[2,1024,256]{2,1,0:T(8,128)(2,1)}, bf16[2,1024,256]{2,1,0:T(8,128)(2,1)S(1)}, u32[]{:S(2)}, u32[]{:S(2)}) collective-permute-start(bf16[2,1024,256]{2,1,0:T(8,128)(2,1)} %get-tuple-element.103.rest_0_), channel_id=1, source_target_pairs={{0,4},{4,0},{8,12},{12,8},{16,20},{20,16},{24,28},{28,24},{1,5},{5... | collective-permute-start | bytes 3145736 | tf_op jit(solution)/shard_map/ppermute | solution.py:35
  111.6 22.9 %collective-permute-start.18 = (bf16[256,1024]{1,0:T(8,128)(2,1)}, bf16[256,1024]{1,0:T(8,128)(2,1)S(1)}, u32[]{:S(2)}, u32[]{:S(2)}) collective-permute-start(bf16[256,1024]{1,0:T(8,128)(2,1)} %get-tuple-element.105.rest_2_.refs_1_), channel_id=1, source_target_pairs={{0,16},{4,20},{8,24},{12,28},{16,0},{20,4},{24,8},{28,12},{1,17},{... | collective-permute-start | bytes 1572872 | tf_op jit(solution)/shard_map/ppermute | solution.py:35
  114.1 12.1 %collective-permute-start.23 = (bf16[2,40,1024]{2,1,0:T(8,128)(2,1)}, bf16[2,40,1024]{2,1,0:T(8,128)(2,1)S(1)}, u32[]{:S(2)}, u32[]{:S(2)}) collective-permute-start(bf16[2,40,1024]{2,1,0:T(8,128)(2,1)} %after.5), channel_id=1, source_target_pairs={{0,8},{4,12},{8,0},{12,4},{16,24},{20,28},{24,16},{28,20},{1,9},{5... | collective-permute-start | bytes 491528 | tf_op jit(solution)/shard_map/ppermute | solution.py:35
  114.6 11.6 %copy-start.14 = (f32[2,40,1024]{2,1,0:T(8,128)S(1)}, f32[2,40,1024]{2,1,0:T(8,128)}, u32[]{:S(2)}) copy-start(f32[2,40,1024]{2,1,0:T(8,128)} %get-tuple-element.116) | copy-start | bytes 983044
  124.9 0.6 copy-start.4
  125.5 24.2 %collective-permute-start.21 = (bf16[2,2,256,512]{3,2,1,0:T(8,128)(2,1)}, bf16[2,2,256,512]{3,2,1,0:T(8,128)(2,1)S(1)}, u32[]{:S(2)}, u32[]{:S(2)}) collective-permute-start(bf16[2,2,256,512]{3,2,1,0:T(8,128)(2,1)} %get-tuple-element.112), channel_id=1, source_target_pairs={{0,1},{1,0},{2,3},{3,2},{4,5},{5,4},{6,7},{7,6},{8,9},{9,8},{10,11... | collective-permute-start | bytes 3145736 | tf_op jit(solution)/shard_map/ppermute | solution.py:35
  134.5 0.8 copy-start.10
  134.5 1.1 copy-start.8
  135.6 21.6 %copy-start.12 = (f32[256,512]{1,0:T(8,128)S(1)}, f32[256,512]{1,0:T(8,128)}, u32[]{:S(2)}) copy-start(f32[256,512]{1,0:T(8,128)} %get-tuple-element.113) | copy-start | bytes 1572868
  135.6 21.6 %copy-start.13 = (f32[256,512]{1,0:T(8,128)S(1)}, f32[256,512]{1,0:T(8,128)}, u32[]{:S(2)}) copy-start(f32[256,512]{1,0:T(8,128)} %get-tuple-element.114) | copy-start | bytes 1572868
  135.6 1.4 collective-permute-start.24
  137.7 3.7 %collective-permute-start.25 = (f32[18,128]{1,0:T(8,128)S(1)}, f32[18,128]{1,0:T(8,128)S(1)}, u32[]{:S(2)}, u32[]{:S(2)}) collective-permute-start(f32[18,128]{1,0:T(8,128)S(1)} %add.71), channel_id=1, source_target_pairs={{0,2},{1,3},{2,0},{3,1},{4,6},{5,7},{6,4},{7,5},{8,10},{9,11},{10,... | collective-permute-start | bytes 27656 | tf_op jit(solution)/shard_map/ppermute | solution.py:35
  138.3 10.6 %collective-permute-start.26 = (bf16[80,1024]{1,0:T(8,128)(2,1)S(1)}, bf16[80,1024]{1,0:T(8,128)(2,1)S(1)}, u32[]{:S(2)}, u32[]{:S(2)}) collective-permute-start(bf16[80,1024]{1,0:T(8,128)(2,1)S(1)} %pad_maximum_fusion.3), channel_id=1, source_target_pairs={{0,16},{4,20},{8,24},{12,28},{16,0},{20,4},{24,8},{28,12},{1,17},{... | collective-permute-start | bytes 491528 | tf_op jit(solution)/shard_map/ppermute | solution.py:35
  141.4 7.4 %collective-permute-start.27 = (f32[4,128]{1,0:T(4,128)S(1)}, f32[4,128]{1,0:T(4,128)S(1)}, u32[]{:S(2)}, u32[]{:S(2)}) collective-permute-start(f32[4,128]{1,0:T(4,128)S(1)} %constant_dynamic-slice_fusion), channel_id=1, source_target_pairs={{0,16},{4,20},{8,24},{12,28},{16,0},{20,4},{24,8},{28,12},{1,17},{... | collective-permute-start | bytes 6152 | tf_op jit(solution)/shard_map/ppermute | solution.py:35
  149.6 1.0 copy-start.7
  150.6 6.4 %collective-permute-start.28 = (bf16[88,1024]{1,0:T(8,128)(2,1)}, bf16[88,1024]{1,0:T(8,128)(2,1)S(1)}, u32[]{:S(2)}, u32[]{:S(2)}) collective-permute-start(bf16[88,1024]{1,0:T(8,128)(2,1)} %after.7), channel_id=1, source_target_pairs={{0,4},{4,0},{8,12},{12,8},{16,20},{20,16},{24,28},{28,24},{1,5},{5... | collective-permute-start | bytes 540680 | tf_op jit(solution)/shard_map/ppermute | solution.py:35
  151.3 21.5 %collective-permute-start.20 = (bf16[1024,256]{1,0:T(8,128)(2,1)}, bf16[1024,256]{1,0:T(8,128)(2,1)S(1)}, u32[]{:S(2)}, u32[]{:S(2)}) collective-permute-start(bf16[1024,256]{1,0:T(8,128)(2,1)} %fusion.refs_2_), channel_id=1, source_target_pairs={{0,8},{4,12},{8,0},{12,4},{16,24},{20,28},{24,16},{28,20},{1,9},{5... | collective-permute-start | bytes 1572872 | tf_op jit(solution)/shard_map/ppermute | solution.py:35
  157.1 15.0 %collective-permute-start.29 = (bf16[168,1024]{1,0:T(8,128)(2,1)S(1)}, bf16[168,1024]{1,0:T(8,128)(2,1)S(1)}, u32[]{:S(2)}, u32[]{:S(2)}) collective-permute-start(bf16[168,1024]{1,0:T(8,128)(2,1)S(1)} %pad_maximum_fusion.1), channel_id=1, source_target_pairs={{0,8},{4,12},{8,0},{12,4},{16,24},{20,28},{24,16},{28,20},{1,9},{5... | collective-permute-start | bytes 1032200 | tf_op jit(solution)/shard_map/ppermute | solution.py:35
  158.5 14.3 %collective-permute-start.22 = (bf16[2,256,512]{2,1,0:T(8,128)(2,1)S(1)}, bf16[2,256,512]{2,1,0:T(8,128)(2,1)S(1)}, u32[]{:S(2)}, u32[]{:S(2)}) collective-permute-start(bf16[2,256,512]{2,1,0:T(8,128)(2,1)S(1)} %pad_maximum_fusion), channel_id=1, source_target_pairs={{0,2},{1,3},{2,0},{3,1},{4,6},{5,7},{6,4},{7,5},{8,10},{9,11},{10,... | collective-permute-start | bytes 1572872 | tf_op jit(solution)/shard_map/ppermute | solution.py:35
  172.8 0.9 copy-start.11
  172.8 1.1 copy-start.9

commit v4 on v3

--- a/solution.py
+++ b/solution.py
@@ -1218,21 +1218,15 @@
         small = lax.reduce_precision(small.reshape(-1, small.shape[-1]), 8, 7)
         flipped = jnp.concatenate([small[SMALL:], small[:SMALL]], axis=0).astype(BF16)
         gathered = (small + swap(flipped, "dp", 4).astype(F32)).astype(BF16)
-        gain = gain + swap(gain, "dp", 4)
+        for bit in (4, 1, 2):
+            gain = gain + swap(gain, "dp", bit)
         pieces = [gathered]
-        for bit, pins in ((1, (in_hbm(come), in_hbm(far_send))), (2, ())):
-            high = lax.reduce_precision(gain, 8, 7)
-            rest = lax.reduce_precision(gain - high, 8, 7)
-            line = jnp.concatenate([high.reshape(1, -1), rest.reshape(1, -1)], axis=1)
-            tail = jnp.pad(line.astype(BF16), ((0, SUB - 1), (0, 0)))
-            whole = jnp.concatenate([gathered, tail], axis=0)
+        for bit, pins in ((1, ()), (2, ())):
             if pins:
-                (whole,) = after((whole,), pins)
-            got = swap(whole, "dp", bit)
-            pieces.append(got[:-SUB])
-            gathered = jnp.concatenate([gathered, got[:-SUB]], axis=0)
-            other = got[-SUB].astype(F32)
-            gain = (high + rest) + (other[:own_width] + other[own_width:]).reshape(gain.shape)
+                (gathered,) = after((gathered,), pins)
+            got = swap(gathered, "dp", bit)
+            pieces.append(got)
+            gathered = jnp.concatenate([gathered, got], axis=0)
         grad_gain = gain.reshape(-1)
         grad_wx, grad_wout, block_out, grad_in, grad_up, down, keyq, *lines = finale(
             place, keep_x, come_x, keep_out, come_out, far_out, out_keep, keep, come, come_far,

time: 180 us -> 173 us (0.961)
  waiting for transfers between devices: 54.8 us -> 46 us
  starting transfers between devices: 27.8 us -> 33.5 us
  other arithmetic: 8.34 us -> 5.68 us
    ppermute x30 -> x32, waiting for transfers between devices: 54.8 us -> 46 us  [swap(): return lax.ppermute(value, axis, [(i, i ^ bit) for i in range(size)])]
    ppermute x30 -> x32, starting transfers between devices: 27.8 us -> 33.5 us  [swap(): return lax.ppermute(value, axis, [(i, i ^ bit) for i in range(size)])]
    unnamed x32 -> x30, local copies, waits for them, and re-layouts: 4.66 us -> 3.66 us
  transfers between devices with their start and end apart: 30 -> 32, of which waited for: 13 -> 14; matrix products, arithmetic and copies ran while one was open for 5% -> 4% of each run, Pallas kernels for 38% -> 40%
where the time goes in v4:
time: 173 us
  Pallas kernels  81.1 us (47%)
  waiting for transfers between devices  46 us (27%)
  starting transfers between devices  33.5 us (19%)
  other arithmetic  5.68 us (3%)
  local copies, waits for them, and re-layouts  4.92 us (3%)
    ppermute x32, waiting for transfers between devices, swap(): return lax.ppermute(value, axis, [(i, i ^ bit) for i in range(size)])  46 us
    ppermute x32, starting transfers between devices, swap(): return lax.ppermute(value, axis, [(i, i ^ bit) for i in range(size)])  33.5 us
    pallas_call x1, Pallas kernels, scan_backward(): pl.pallas_call(functools.partial(back_kernel, unroll, len(pins)), in_spec...  19.4 us
    pallas_call x1, Pallas kernels, scan_forward(): pl.pallas_call(functools.partial(scan_kernel, 4), in_specs=[WHOLE] * 8, o...  10.9 us
    pallas_call x1, Pallas kernels, input_grad(): pl.pallas_call(functools.partial(input_kernel, len(pins), len(extra)), gr...  10.3 us
    pallas_call x1, Pallas kernels, middle(): pl.pallas_call(middle_kernel, grid_spec=pltpu.PrefetchScalarGridSpec(num_...  8.45 us
    pallas_call x2, Pallas kernels, in_weight(): pl.pallas_call(functools.partial(in_weight_kernel, len(pins)), grid=(2,),...  7.73 us
    pallas_call x1, Pallas kernels, front(): pl.pallas_call(functools.partial(front_kernel, blocked), grid=(inner // b...  7.54 us
  transfers between devices with their start and end apart: 32, of which 14 were waited for; matrix products, arithmetic and copies ran while one was open for 4% of the time, Pallas kernels for 40%

profile of v4, /device:TPU:0, one launch (start us, length us, event | category | flops | bytes accessed | tf_op | source)
XLA Modules:
  0.0 172.7 jit_solution(16806599887475183454)
XLA Ops:
  2.0 7.5 %front.1 = (bf16[256,2048]{1,0:T(8,128)(2,1)S(1)}, bf16[256,2048]{1,0:T(8,128)(2,1)S(1)}, f32[256,1024]{1,0:T(8,128)}, bf16[256,1024]{1,0:T(8,128)(2,1)}, f32[25...) custom-call(s32[2]{0:T(128)S(1)} %pad_add_fusion.place, ...), custom_call_target="tpu_custom_call" | custom-call | tf_op jit(solution)/shard_map/front/pallas_call | solution.py:167
  10.1 2.6 %collective-permute-start.1 = (bf16[2,256,512]{2,1,0:T(8,128)(2,1)}, bf16[2,256,512]{2,1,0:T(8,128)(2,1)S(1)}, u32[]{:S(2)}, u32[]{:S(2)}) collective-permute-start(bf16[2,256,512]{2,1,0:T(8,128)(2,1)} %get-tuple-element.77), channel_id=1, source_target_pairs={{0,4},{4,0},{8,12},{12,8},{16,20},{20,16},{24,28},{28,24},{1,5},{5... | collective-permute-start | bytes 1572872 | tf_op jit(solution)/shard_map/ppermute | solution.py:35
  12.7 1.6 collective-permute-start.4
  14.3 1.6 collective-permute-start
  15.8 2.6 %collective-permute-start.5 = (bf16[128,1024]{1,0:T(8,128)(2,1)}, bf16[128,1024]{1,0:T(8,128)(2,1)S(1)}, u32[]{:S(2)}, u32[]{:S(2)}) collective-permute-start(bf16[128,1024]{1,0:T(8,128)(2,1)} %get-tuple-element.90), channel_id=1, source_target_pairs={{0,16},{4,20},{8,24},{12,28},{16,0},{20,4},{24,8},{28,12},{1,17},{... | collective-permute-start | bytes 786440 | tf_op jit(solution)/shard_map/ppermute | solution.py:35
  18.4 5.8 %gate.1 = (f32[256,1024]{1,0:T(8,128)S(1)}, f32[256,1024]{1,0:T(8,128)S(1)}, f32[256,1024]{1,0:T(8,128)}) custom-call(bf16[256,2048]{1,0:T(8,128)(2,1)S(1)} %get-tuple-element.80.normed, bf16[256,2048]{1,0:T(8,128)(2,1)S(1)} %get-tuple-element.81.up, bf16[2048,1024]{1,0:T(8,128)(2,1)} %wz.3, bf16[1024,2048]{1,0:T(8,128)(2,1)} %wo.3), custom_call_target="tpu_custom_call" | custom-call | tf_op jit(solution)/shard_map/gate/pallas_call | solution.py:227
  24.2 10.9 %scan.1 = (bf16[256,1024]{1,0:T(8,128)(2,1)}, bf16[256,1024]{1,0:T(8,128)(2,1)}, f32[256,1024]{1,0:T(8,128)S(1)}, f32[256,1024]{1,0:T(8,128)S(1)}, f32[8,128]{1,...) custom-call(f32[320,128]{1,0:T(8,128)S(1)} %add.41.one, ...), custom_call_target="tpu_custom_call" | custom-call | tf_op jit(solution)/shard_map/scan/pallas_call | solution.py:344
  35.7 1.3 collective-permute-start.10
  37.3 19.4 %back.1 = (f32[256,1024]{1,0:T(8,128)}, f32[336,128]{1,0:T(8,128)S(1)}, f32[136,1024]{1,0:T(8,128)}) custom-call(s32[2]{0:T(128)S(1)} %pad_add_fusion.place, f32[320,128]{1,0:T(8,128)S(1)} %add.41.one, f32[320,128]{1,0:T(8,128)S(1)} %collective-permute-done.4.two, bf16[256,1024]{1,0:T(8,128)(2,1)} %get-tuple-element.79.mixed, bf16[128,1024]{1,0:T(8,128)(2,1)} %wup.3, ...), custom_call_target="tpu_custom_call" | custom-call | tf_op jit(solution)/shard_map/back/pallas_call | solution.py:501
  57.3 0.7 slice_bitcast_fusion.3
  58.3 1.6 collective-permute-start.2
  61.5 0.7 collective-permute-start.16
  62.2 5.4 %collective-permute-done.2.rest_3_.l3 = bf16[256,512]{1,0:T(8,128)(2,1)S(1)} collective-permute-done((bf16[256,512]{1,0:T(8,128)(2,1)}, bf16[256,512]{1,0:T(8,128)(2,1)S(1)}, u32[]{:S(2)}, u32[]{:S(2)}) %collective-permute-start.2) | collective-permute-done | bytes 262176 | tf_op jit(solution)/shard_map/ppermute | solution.py:35
  67.6 5.8 %conv.1 = (bf16[256,1024]{1,0:T(8,128)(2,1)}, f32[4,40,1024]{2,1,0:T(8,128)}, bf16[4,40,1024]{2,1,0:T(8,128)(2,1)}) custom-call(s32[2]{0:T(128)S(1)} %pad_add_fusion.place, f32[320,128]{1,0:T(8,128)S(1)} %add.41.one, f32[320,128]{1,0:T(8,128)S(1)} %collective-permute-done.4.two, f32[336,128]{1,0:T(8,128)} %add.42.grad_one, ...), custom_call_target="tpu_custom_call" | custom-call | tf_op jit(solution)/shard_map/conv/pallas_call | solution.py:618
  73.4 1.2 collective-permute-start.11
  74.6 0.7 collective-permute-start.12
  75.3 1.3 collective-permute-start.14
  76.6 3.9 %inw.2 = (f32[256,1024]{1,0:T(8,128)}, bf16[256,1024]{1,0:T(8,128)(2,1)}) custom-call(bf16[256,512]{1,0:T(8,128)(2,1)} %get-tuple-element.75.l0, bf16[256,512]{1,0:T(8,128)(2,1)S(1)} %collective-permute-done.rest_0_.l1, bf16[2,256,512]{2,1,0:T(8,128)(2,1)S(1)} %collective-permute-done.1.rest_1_.l2, bf16[256,512]{1,0:T(8,128)(2,1)S(1)} %collective-permute-done.2.rest_3_.l3, ...), custom_call_target="tpu_custom_call" | custom-call | tf_op jit(solution)/shard_map/inw/pallas_call | solution.py:1033
  80.5 2.6 %collective-permute-start.17 = (bf16[256,1024]{1,0:T(8,128)(2,1)}, bf16[256,1024]{1,0:T(8,128)(2,1)S(1)}, u32[]{:S(2)}, u32[]{:S(2)}) collective-permute-start(bf16[256,1024]{1,0:T(8,128)(2,1)} %get-tuple-element.102.rest_0_), channel_id=1, source_target_pairs={{0,16},{4,20},{8,24},{12,28},{16,0},{20,4},{24,8},{28,12},{1,17},{... | collective-permute-start | bytes 1572872 | tf_op jit(solution)/shard_map/ppermute | solution.py:35
  83.1 10.2 %collective-permute-done.11.rest_1_.r1 = bf16[256,1024]{1,0:T(8,128)(2,1)S(1)} collective-permute-done((bf16[256,1024]{1,0:T(8,128)(2,1)}, bf16[256,1024]{1,0:T(8,128)(2,1)S(1)}, u32[]{:S(2)}, u32[]{:S(2)}) %collective-permute-start.11) | collective-permute-done | bytes 524320 | tf_op jit(solution)/shard_map/ppermute | solution.py:35
  93.3 0.7 collective-permute-start.13
  94.1 0.8 collective-permute-done.14.small_come
  94.9 8.4 %middle.1 = (f32[1024,256]{1,0:T(8,128)}, f32[1024,256]{1,0:T(8,128)}, bf16[2,1024,256]{2,1,0:T(8,128)(2,1)}, bf16[2,2,256,512]{3,2,1,0:T(8,128)(2,1)}, f32[256,...) custom-call(s32[2]{0:T(128)S(1)} %pad_add_fusion.place, ...), custom_call_target="tpu_custom_call" | custom-call | tf_op jit(solution)/shard_map/middle/pallas_call | solution.py:864
  103.4 0.8 collective-permute-start.19
  104.2 1.2 collective-permute-done.17.rest_1_
  105.4 2.4 %collective-permute-done.13.r3 = bf16[256,1024]{1,0:T(8,128)(2,1)S(1)} collective-permute-done((bf16[256,1024]{1,0:T(8,128)(2,1)S(1)}, bf16[256,1024]{1,0:T(8,128)(2,1)S(1)}, u32[]{:S(2)}, u32[]{:S(2)}) %collective-permute-start.13) | collective-permute-done | bytes 524320 | tf_op jit(solution)/shard_map/ppermute | solution.py:35
  107.8 3.9 %inw.3 = (f32[256,1024]{1,0:T(8,128)}, bf16[256,1024]{1,0:T(8,128)(2,1)}) custom-call(bf16[256,512]{1,0:T(8,128)(2,1)} %get-tuple-element.75.l0, bf16[256,512]{1,0:T(8,128)(2,1)S(1)} %collective-permute-done.rest_0_.l1, bf16[2,256,512]{2,1,0:T(8,128)(2,1)S(1)} %collective-permute-done.1.rest_1_.l2, bf16[256,512]{1,0:T(8,128)(2,1)S(1)} %collective-permute-done.2.rest_3_.l3, ...), custom_call_target="tpu_custom_call" | custom-call | tf_op jit(solution)/shard_map/inw/pallas_call | solution.py:1033
  111.6 2.4 %collective-permute-start.18 = (bf16[256,1024]{1,0:T(8,128)(2,1)}, bf16[256,1024]{1,0:T(8,128)(2,1)S(1)}, u32[]{:S(2)}, u32[]{:S(2)}) collective-permute-start(bf16[256,1024]{1,0:T(8,128)(2,1)} %get-tuple-element.105.rest_2_.refs_1_), channel_id=1, source_target_pairs={{0,16},{4,20},{8,24},{12,28},{16,0},{20,4},{24,8},{28,12},{1,17},{... | collective-permute-start | bytes 1572872 | tf_op jit(solution)/shard_map/ppermute | solution.py:35
  114.6 10.3 %inputs.1 = (bf16[2,2,256,512]{3,2,1,0:T(8,128)(2,1)}, f32[256,512]{1,0:T(8,128)}, f32[256,512]{1,0:T(8,128)}, f32[18,128]{1,0:T(8,128)S(1)}, f32[256,512]{1,0:T...) custom-call(s32[2]{0:T(128)S(1)} %pad_add_fusion.place, ...), custom_call_target="tpu_custom_call", output_to_operand_aliasing={{0}: (3, {})} | custom-call | tf_op jit(solution)/shard_map/inputs/pallas_call | solution.py:768
  125.5 0.7 collective-permute-done.23
  126.2 0.8 convert_add_fusion.3.refs_1_
  126.9 7.6 %collective-permute-done.18.refs_2_.come_x = bf16[256,1024]{1,0:T(8,128)(2,1)S(1)} collective-permute-done((bf16[256,1024]{1,0:T(8,128)(2,1)}, bf16[256,1024]{1,0:T(8,128)(2,1)S(1)}, u32[]{:S(2)}, u32[]{:S(2)}) %collective-permute-start.18) | collective-permute-done | bytes 524320 | tf_op jit(solution)/shard_map/ppermute | solution.py:35
  134.5 0.8 copy-done.10
  135.6 1.1 reduce-precision_convert_fusion
  137.0 0.7 add.47
  138.3 1.5 fusion
  139.7 3.4 %collective-permute-start.20 = (bf16[1024,256]{1,0:T(8,128)(2,1)S(1)}, bf16[1024,256]{1,0:T(8,128)(2,1)S(1)}, u32[]{:S(2)}, u32[]{:S(2)}) collective-permute-start(bf16[1024,256]{1,0:T(8,128)(2,1)S(1)} %fusion), channel_id=1, source_target_pairs={{0,8},{4,12},{8,0},{12,4},{16,24},{20,28},{24,16},{28,20},{1,9},{5... | collective-permute-start | bytes 1572872 | tf_op jit(solution)/shard_map/ppermute | solution.py:35
  143.1 1.1 collective-permute-start.29
  144.2 3.7 %collective-permute-done.26 = bf16[80,1024]{1,0:T(8,128)(2,1)S(1)} collective-permute-done((bf16[80,1024]{1,0:T(8,128)(2,1)S(1)}, bf16[80,1024]{1,0:T(8,128)(2,1)S(1)}, u32[]{:S(2)}, u32[]{:S(2)}) %collective-permute-start.26) | collective-permute-done | bytes 163872 | tf_op jit(solution)/shard_map/ppermute | solution.py:35
  147.9 0.8 collective-permute-start.27
  149.6 4.2 %collective-permute-done.27.g2 = bf16[80,1024]{1,0:T(8,128)(2,1)S(1)} collective-permute-done((bf16[80,1024]{1,0:T(8,128)(2,1)S(1)}, bf16[80,1024]{1,0:T(8,128)(2,1)S(1)}, u32[]{:S(2)}, u32[]{:S(2)}) %collective-permute-start.27) | collective-permute-done | bytes 163872 | tf_op jit(solution)/shard_map/ppermute | solution.py:35
  153.9 1.6 collective-permute-done.29
  155.5 0.7 collective-permute-start.30
  156.2 2.9 %collective-permute-done.30 = f32[4,128]{1,0:T(4,128)S(1)} collective-permute-done((f32[4,128]{1,0:T(4,128)S(1)}, f32[4,128]{1,0:T(4,128)S(1)}, u32[]{:S(2)}, u32[]{:S(2)}) %collective-permute-start.30) | collective-permute-done | bytes 2080 | tf_op jit(solution)/shard_map/ppermute | solution.py:35
  159.1 1.5 collective-permute-start.31
  160.5 4.8 %collective-permute-done.31 = f32[4,128]{1,0:T(4,128)S(1)} collective-permute-done((f32[4,128]{1,0:T(4,128)S(1)}, f32[4,128]{1,0:T(4,128)S(1)}, u32[]{:S(2)}, u32[]{:S(2)}) %collective-permute-start.31) | collective-permute-done | bytes 2080 | tf_op jit(solution)/shard_map/ppermute | solution.py:35
  165.9 0.8 copy-done.11
  166.9 5.3 %finale.1 = (f32[256,1024]{1,0:T(8,128)}, f32[1024,256]{1,0:T(8,128)}, bf16[256,512]{1,0:T(8,128)(2,1)}, f32[256,512]{1,0:T(8,128)}, f32[128,1024]{1,0:T(8,128)}...) custom-call(s32[2]{0:T(128)S(1)} %pad_add_fusion.place, ...), custom_call_target="tpu_custom_call" | custom-call | tf_op jit(solution)/shard_map/finale/pallas_call | solution.py:966
  (80 shorter events, 9.1 us)
Async XLA Ops:
  1.4 0.7 copy-start.5
  9.6 3.1 %collective-permute-start.3 = (f32[320,128]{1,0:T(8,128)S(1)}, f32[320,128]{1,0:T(8,128)S(1)}, u32[]{:S(2)}, u32[]{:S(2)}) collective-permute-start(f32[320,128]{1,0:T(8,128)S(1)} %get-tuple-element.78), channel_id=1, source_target_pairs={{0,1},{1,0},{2,3},{3,2},{4,5},{5,4},{6,7},{7,6},{8,9},{9,8},{10,11... | collective-permute-start | bytes 491528 | tf_op jit(solution)/shard_map/ppermute | solution.py:35
  10.1 27.3 %collective-permute-start.1 = (bf16[2,256,512]{2,1,0:T(8,128)(2,1)}, bf16[2,256,512]{2,1,0:T(8,128)(2,1)S(1)}, u32[]{:S(2)}, u32[]{:S(2)}) collective-permute-start(bf16[2,256,512]{2,1,0:T(8,128)(2,1)} %get-tuple-element.77), channel_id=1, source_target_pairs={{0,4},{4,0},{8,12},{12,8},{16,20},{20,16},{24,28},{28,24},{1,5},{5... | collective-permute-start | bytes 1572872 | tf_op jit(solution)/shard_map/ppermute | solution.py:35
  12.7 11.5 %collective-permute-start.4 = (f32[320,128]{1,0:T(8,128)S(1)}, f32[320,128]{1,0:T(8,128)S(1)}, u32[]{:S(2)}, u32[]{:S(2)}) collective-permute-start(f32[320,128]{1,0:T(8,128)S(1)} %add.41.one), channel_id=1, source_target_pairs={{0,2},{1,3},{2,0},{3,1},{4,6},{5,7},{6,4},{7,5},{8,10},{9,11},{10,... | collective-permute-start | bytes 491528 | tf_op jit(solution)/shard_map/ppermute | solution.py:35
  14.3 22.7 %collective-permute-start = (bf16[256,512]{1,0:T(8,128)(2,1)}, bf16[256,512]{1,0:T(8,128)(2,1)S(1)}, u32[]{:S(2)}, u32[]{:S(2)}) collective-permute-start(bf16[256,512]{1,0:T(8,128)(2,1)} %get-tuple-element.76), channel_id=1, source_target_pairs={{0,8},{4,12},{8,0},{12,4},{16,24},{20,28},{24,16},{28,20},{1,9},{5... | collective-permute-start | bytes 786440 | tf_op jit(solution)/shard_map/ppermute | solution.py:35
  15.8 21.5 %collective-permute-start.5 = (bf16[128,1024]{1,0:T(8,128)(2,1)}, bf16[128,1024]{1,0:T(8,128)(2,1)S(1)}, u32[]{:S(2)}, u32[]{:S(2)}) collective-permute-start(bf16[128,1024]{1,0:T(8,128)(2,1)} %get-tuple-element.90), channel_id=1, source_target_pairs={{0,16},{4,20},{8,24},{12,28},{16,0},{20,4},{24,8},{28,12},{1,17},{... | collective-permute-start | bytes 786440 | tf_op jit(solution)/shard_map/ppermute | solution.py:35
  35.2 25.5 %collective-permute-start.15 = (bf16[256,1024]{1,0:T(8,128)(2,1)}, bf16[256,1024]{1,0:T(8,128)(2,1)S(1)}, u32[]{:S(2)}, u32[]{:S(2)}) collective-permute-start(bf16[256,1024]{1,0:T(8,128)(2,1)} %get-tuple-element.97.r0.prez), channel_id=1, source_target_pairs={{0,8},{4,12},{8,0},{12,4},{16,24},{20,28},{24,16},{28,20},{1,9},{5... | collective-permute-start | bytes 1572872 | tf_op jit(solution)/shard_map/ppermute | solution.py:35
  35.7 31.9 %collective-permute-start.10 = (bf16[256,1024]{1,0:T(8,128)(2,1)}, bf16[256,1024]{1,0:T(8,128)(2,1)S(1)}, u32[]{:S(2)}, u32[]{:S(2)}) collective-permute-start(bf16[256,1024]{1,0:T(8,128)(2,1)} %get-tuple-element.97.r0.prez), channel_id=1, source_target_pairs={{0,4},{4,0},{8,12},{12,8},{16,20},{20,16},{24,28},{28,24},{1,5},{5... | collective-permute-start | bytes 1572872 | tf_op jit(solution)/shard_map/ppermute | solution.py:35
  37.0 30.6 %collective-permute-start.8 = (bf16[256,1024]{1,0:T(8,128)(2,1)}, bf16[256,1024]{1,0:T(8,128)(2,1)S(1)}, u32[]{:S(2)}, u32[]{:S(2)}) collective-permute-start(bf16[256,1024]{1,0:T(8,128)(2,1)} %get-tuple-element.96.gated.every), channel_id=1, source_target_pairs={{0,16},{4,20},{8,24},{12,28},{16,0},{20,4},{24,8},{28,12},{1,17},{... | collective-permute-start | bytes 1572872 | tf_op jit(solution)/shard_map/ppermute | solution.py:35
  37.3 24.1 %collective-permute-start.9 = (bf16[128,1024]{1,0:T(8,128)(2,1)S(1)}, bf16[128,1024]{1,0:T(8,128)(2,1)S(1)}, u32[]{:S(2)}, u32[]{:S(2)}) collective-permute-start(bf16[128,1024]{1,0:T(8,128)(2,1)S(1)} %collective-permute-done.5.rest_2_.up_a), channel_id=1, source_target_pairs={{0,1},{1,0},{2,3},{3,2},{4,5},{5,4},{6,7},{7,6},{8,9},{9,8},{10,11... | collective-permute-start | bytes 786440 | tf_op jit(solution)/shard_map/ppermute | solution.py:35
  56.7 3.9 %copy-start.2 = (f32[336,128]{1,0:T(8,128)}, f32[336,128]{1,0:T(8,128)S(1)}, u32[]{:S(2)}) copy-start(f32[336,128]{1,0:T(8,128)S(1)} %get-tuple-element.91.refs_1_) | copy-start | bytes 516100
  56.7 1.6 collective-permute-start.6
  58.3 9.2 %collective-permute-start.2 = (bf16[256,512]{1,0:T(8,128)(2,1)}, bf16[256,512]{1,0:T(8,128)(2,1)S(1)}, u32[]{:S(2)}, u32[]{:S(2)}) collective-permute-start(bf16[256,512]{1,0:T(8,128)(2,1)} %slice_bitcast_fusion.3), channel_id=1, source_target_pairs={{0,8},{4,12},{8,0},{12,4},{16,24},{20,28},{24,16},{28,20},{1,9},{5... | collective-permute-start | bytes 786440 | tf_op jit(solution)/shard_map/ppermute | solution.py:35
  60.6 0.8 copy-start
  60.6 6.9 %collective-permute-start.7 = (f32[336,128]{1,0:T(8,128)}, f32[336,128]{1,0:T(8,128)}, u32[]{:S(2)}, u32[]{:S(2)}) collective-permute-start(f32[336,128]{1,0:T(8,128)} %add.42.grad_one), channel_id=1, source_target_pairs={{0,2},{1,3},{2,0},{3,1},{4,6},{5,7},{6,4},{7,5},{8,10},{9,11},{10,... | collective-permute-start | bytes 516104 | tf_op jit(solution)/shard_map/ppermute | solution.py:35
  61.5 15.2 %copy-start.1 = (bf16[256,1024]{1,0:T(8,128)(2,1)S(1)}, bf16[256,1024]{1,0:T(8,128)(2,1)}, u32[]{:S(2)}) copy-start(bf16[256,1024]{1,0:T(8,128)(2,1)} %after.3.r1) | copy-start | bytes 1572868
  61.5 15.1 %collective-permute-start.16 = (bf16[256,1024]{1,0:T(8,128)(2,1)}, bf16[256,1024]{1,0:T(8,128)(2,1)S(1)}, u32[]{:S(2)}, u32[]{:S(2)}) collective-permute-start(bf16[256,1024]{1,0:T(8,128)(2,1)} %after.3.r1), channel_id=1, source_target_pairs={{0,4},{4,0},{8,12},{12,8},{16,20},{20,16},{24,28},{28,24},{1,5},{5... | collective-permute-start | bytes 1572872 | tf_op jit(solution)/shard_map/ppermute | solution.py:35
  67.6 27.3 %copy-start.3 = (bf16[256,1024]{1,0:T(8,128)(2,1)S(1)}, bf16[256,1024]{1,0:T(8,128)(2,1)}, u32[]{:S(2)}) copy-start(bf16[256,1024]{1,0:T(8,128)(2,1)} %get-tuple-element.99.up_own) | copy-start | bytes 1572868
  73.4 19.9 %collective-permute-start.11 = (bf16[256,1024]{1,0:T(8,128)(2,1)}, bf16[256,1024]{1,0:T(8,128)(2,1)S(1)}, u32[]{:S(2)}, u32[]{:S(2)}) collective-permute-start(bf16[256,1024]{1,0:T(8,128)(2,1)} %get-tuple-element.98.rest_0_.r0.prex), channel_id=1, source_target_pairs={{0,8},{4,12},{8,0},{12,4},{16,24},{20,28},{24,16},{28,20},{1,9},{5... | collective-permute-start | bytes 1572872 | tf_op jit(solution)/shard_map/ppermute | solution.py:35
  74.6 20.3 %collective-permute-start.12 = (bf16[256,1024]{1,0:T(8,128)(2,1)}, bf16[256,1024]{1,0:T(8,128)(2,1)S(1)}, u32[]{:S(2)}, u32[]{:S(2)}) collective-permute-start(bf16[256,1024]{1,0:T(8,128)(2,1)} %get-tuple-element.98.rest_0_.r0.prex), channel_id=1, source_target_pairs={{0,4},{4,0},{8,12},{12,8},{16,20},{20,16},{24,28},{28,24},{1,5},{5... | collective-permute-start | bytes 1572872 | tf_op jit(solution)/shard_map/ppermute | solution.py:35
  75.3 19.6 %collective-permute-start.14 = (bf16[4,40,1024]{2,1,0:T(8,128)(2,1)}, bf16[4,40,1024]{2,1,0:T(8,128)(2,1)S(1)}, u32[]{:S(2)}, u32[]{:S(2)}) collective-permute-start(bf16[4,40,1024]{2,1,0:T(8,128)(2,1)} %get-tuple-element.101), channel_id=1, source_target_pairs={{0,4},{4,0},{8,12},{12,8},{16,20},{20,16},{24,28},{28,24},{1,5},{5... | collective-permute-start | bytes 983048 | tf_op jit(solution)/shard_map/ppermute | solution.py:35
  80.5 24.9 %collective-permute-start.17 = (bf16[256,1024]{1,0:T(8,128)(2,1)}, bf16[256,1024]{1,0:T(8,128)(2,1)S(1)}, u32[]{:S(2)}, u32[]{:S(2)}) collective-permute-start(bf16[256,1024]{1,0:T(8,128)(2,1)} %get-tuple-element.102.rest_0_), channel_id=1, source_target_pairs={{0,16},{4,20},{8,24},{12,28},{16,0},{20,4},{24,8},{28,12},{1,17},{... | collective-permute-start | bytes 1572872 | tf_op jit(solution)/shard_map/ppermute | solution.py:35
  93.3 14.5 %collective-permute-start.13 = (bf16[256,1024]{1,0:T(8,128)(2,1)S(1)}, bf16[256,1024]{1,0:T(8,128)(2,1)S(1)}, u32[]{:S(2)}, u32[]{:S(2)}) collective-permute-start(bf16[256,1024]{1,0:T(8,128)(2,1)S(1)} %collective-permute-done.11.rest_1_.r1), channel_id=1, source_target_pairs={{0,4},{4,0},{8,12},{12,8},{16,20},{20,16},{24,28},{28,24},{1,5},{5... | collective-permute-start | bytes 1572872 | tf_op jit(solution)/shard_map/ppermute | solution.py:35
  103.4 11.2 %copy-start.6 = (f32[8]{0:T(128)S(1)}, f32[8]{0:T(128)}, u32[]{:S(2)}) copy-start(f32[8]{0:T(128)} %weights.3) | copy-start | bytes 100
  103.4 31.1 %collective-permute-start.19 = (bf16[2,1024,256]{2,1,0:T(8,128)(2,1)}, bf16[2,1024,256]{2,1,0:T(8,128)(2,1)S(1)}, u32[]{:S(2)}, u32[]{:S(2)}) collective-permute-start(bf16[2,1024,256]{2,1,0:T(8,128)(2,1)} %get-tuple-element.103.rest_0_), channel_id=1, source_target_pairs={{0,4},{4,0},{8,12},{12,8},{16,20},{20,16},{24,28},{28,24},{1,5},{5... | collective-permute-start | bytes 3145736 | tf_op jit(solution)/shard_map/ppermute | solution.py:35
  111.6 22.8 %collective-permute-start.18 = (bf16[256,1024]{1,0:T(8,128)(2,1)}, bf16[256,1024]{1,0:T(8,128)(2,1)S(1)}, u32[]{:S(2)}, u32[]{:S(2)}) collective-permute-start(bf16[256,1024]{1,0:T(8,128)(2,1)} %get-tuple-element.105.rest_2_.refs_1_), channel_id=1, source_target_pairs={{0,16},{4,20},{8,24},{12,28},{16,0},{20,4},{24,8},{28,12},{1,17},{... | collective-permute-start | bytes 1572872 | tf_op jit(solution)/shard_map/ppermute | solution.py:35
  114.1 12.1 %collective-permute-start.23 = (bf16[2,40,1024]{2,1,0:T(8,128)(2,1)}, bf16[2,40,1024]{2,1,0:T(8,128)(2,1)S(1)}, u32[]{:S(2)}, u32[]{:S(2)}) collective-permute-start(bf16[2,40,1024]{2,1,0:T(8,128)(2,1)} %after.4), channel_id=1, source_target_pairs={{0,8},{4,12},{8,0},{12,4},{16,24},{20,28},{24,16},{28,20},{1,9},{5... | collective-permute-start | bytes 491528 | tf_op jit(solution)/shard_map/ppermute | solution.py:35
  114.6 11.6 %copy-start.14 = (f32[2,40,1024]{2,1,0:T(8,128)S(1)}, f32[2,40,1024]{2,1,0:T(8,128)}, u32[]{:S(2)}) copy-start(f32[2,40,1024]{2,1,0:T(8,128)} %get-tuple-element.116) | copy-start | bytes 983044
  124.9 0.6 copy-start.4
  125.5 23.3 %copy-start.12 = (f32[256,512]{1,0:T(8,128)S(1)}, f32[256,512]{1,0:T(8,128)}, u32[]{:S(2)}) copy-start(f32[256,512]{1,0:T(8,128)} %get-tuple-element.113) | copy-start | bytes 1572868
  125.5 23.3 %collective-permute-start.21 = (bf16[2,2,256,512]{3,2,1,0:T(8,128)(2,1)}, bf16[2,2,256,512]{3,2,1,0:T(8,128)(2,1)S(1)}, u32[]{:S(2)}, u32[]{:S(2)}) collective-permute-start(bf16[2,2,256,512]{3,2,1,0:T(8,128)(2,1)} %get-tuple-element.112), channel_id=1, source_target_pairs={{0,1},{1,0},{2,3},{3,2},{4,5},{5,4},{6,7},{7,6},{8,9},{9,8},{10,11... | collective-permute-start | bytes 3145736 | tf_op jit(solution)/shard_map/ppermute | solution.py:35
  134.5 0.8 copy-start.10
  134.5 1.1 copy-start.7
  135.6 13.2 %copy-start.13 = (f32[256,512]{1,0:T(8,128)S(1)}, f32[256,512]{1,0:T(8,128)}, u32[]{:S(2)}) copy-start(f32[256,512]{1,0:T(8,128)} %get-tuple-element.114) | copy-start | bytes 1572868
  135.6 1.4 collective-permute-start.24
  136.7 11.2 %collective-permute-start.26 = (bf16[80,1024]{1,0:T(8,128)(2,1)S(1)}, bf16[80,1024]{1,0:T(8,128)(2,1)S(1)}, u32[]{:S(2)}, u32[]{:S(2)}) collective-permute-start(bf16[80,1024]{1,0:T(8,128)(2,1)S(1)} %pad_maximum_fusion.2), channel_id=1, source_target_pairs={{0,16},{4,20},{8,24},{12,28},{16,0},{20,4},{24,8},{28,12},{1,17},{... | collective-permute-start | bytes 491528 | tf_op jit(solution)/shard_map/ppermute | solution.py:35
  137.7 5.4 %collective-permute-start.25 = (f32[18,128]{1,0:T(8,128)S(1)}, f32[18,128]{1,0:T(8,128)S(1)}, u32[]{:S(2)}, u32[]{:S(2)}) collective-permute-start(f32[18,128]{1,0:T(8,128)S(1)} %add.47), channel_id=1, source_target_pairs={{0,2},{1,3},{2,0},{3,1},{4,6},{5,7},{6,4},{7,5},{8,10},{9,11},{10,... | collective-permute-start | bytes 27656 | tf_op jit(solution)/shard_map/ppermute | solution.py:35
  139.7 26.1 %collective-permute-start.20 = (bf16[1024,256]{1,0:T(8,128)(2,1)S(1)}, bf16[1024,256]{1,0:T(8,128)(2,1)S(1)}, u32[]{:S(2)}, u32[]{:S(2)}) collective-permute-start(bf16[1024,256]{1,0:T(8,128)(2,1)S(1)} %fusion), channel_id=1, source_target_pairs={{0,8},{4,12},{8,0},{12,4},{16,24},{20,28},{24,16},{28,20},{1,9},{5... | collective-permute-start | bytes 1572872 | tf_op jit(solution)/shard_map/ppermute | solution.py:35
  143.1 12.4 %collective-permute-start.29 = (f32[4,128]{1,0:T(4,128)S(1)}, f32[4,128]{1,0:T(4,128)S(1)}, u32[]{:S(2)}, u32[]{:S(2)}) collective-permute-start(f32[4,128]{1,0:T(4,128)S(1)} %constant_dynamic-slice_fusion), channel_id=1, source_target_pairs={{0,16},{4,20},{8,24},{12,28},{16,0},{20,4},{24,8},{28,12},{1,17},{... | collective-permute-start | bytes 6152 | tf_op jit(solution)/shard_map/ppermute | solution.py:35
  147.9 5.9 %collective-permute-start.27 = (bf16[80,1024]{1,0:T(8,128)(2,1)S(1)}, bf16[80,1024]{1,0:T(8,128)(2,1)S(1)}, u32[]{:S(2)}, u32[]{:S(2)}) collective-permute-start(bf16[80,1024]{1,0:T(8,128)(2,1)S(1)} %fusion.3.g0), channel_id=1, source_target_pairs={{0,4},{4,0},{8,12},{12,8},{16,20},{20,16},{24,28},{28,24},{1,5},{5... | collective-permute-start | bytes 491528 | tf_op jit(solution)/shard_map/ppermute | solution.py:35
  148.8 17.1 %copy-start.8 = (bf16[2,2,256,512]{3,2,1,0:T(8,128)(2,1)}, bf16[2,2,256,512]{3,2,1,0:T(8,128)(2,1)S(1)}, u32[]{:S(2)}) copy-start(bf16[2,2,256,512]{3,2,1,0:T(8,128)(2,1)S(1)} %collective-permute-done.21.come_a.come_b) | copy-start | bytes 3145732
  149.0 16.9 %collective-permute-start.22 = (bf16[2,256,512]{2,1,0:T(8,128)(2,1)S(1)}, bf16[2,256,512]{2,1,0:T(8,128)(2,1)S(1)}, u32[]{:S(2)}, u32[]{:S(2)}) collective-permute-start(bf16[2,256,512]{2,1,0:T(8,128)(2,1)S(1)} %pad_maximum_fusion), channel_id=1, source_target_pairs={{0,2},{1,3},{2,0},{3,1},{4,6},{5,7},{6,4},{7,5},{8,10},{9,11},{10,... | collective-permute-start | bytes 1572872 | tf_op jit(solution)/shard_map/ppermute | solution.py:35
  153.8 12.0 %collective-permute-start.28 = (bf16[160,1024]{1,0:T(8,128)(2,1)S(1)}, bf16[160,1024]{1,0:T(8,128)(2,1)S(1)}, u32[]{:S(2)}, u32[]{:S(2)}) collective-permute-start(bf16[160,1024]{1,0:T(8,128)(2,1)S(1)} %pad_maximum_fusion.1), channel_id=1, source_target_pairs={{0,8},{4,12},{8,0},{12,4},{16,24},{20,28},{24,16},{28,20},{1,9},{5... | collective-permute-start | bytes 983048 | tf_op jit(solution)/shard_map/ppermute | solution.py:35
  155.5 3.6 %collective-permute-start.30 = (f32[4,128]{1,0:T(4,128)S(1)}, f32[4,128]{1,0:T(4,128)S(1)}, u32[]{:S(2)}, u32[]{:S(2)}) collective-permute-start(f32[4,128]{1,0:T(4,128)S(1)} %fusion.6), channel_id=1, source_target_pairs={{0,4},{4,0},{8,12},{12,8},{16,20},{20,16},{24,28},{28,24},{1,5},{5... | collective-permute-start | bytes 6152 | tf_op jit(solution)/shard_map/ppermute | solution.py:35
  159.1 6.2 %collective-permute-start.31 = (f32[4,128]{1,0:T(4,128)S(1)}, f32[4,128]{1,0:T(4,128)S(1)}, u32[]{:S(2)}, u32[]{:S(2)}) collective-permute-start(f32[4,128]{1,0:T(4,128)S(1)} %add.52), channel_id=1, source_target_pairs={{0,8},{4,12},{8,0},{12,4},{16,24},{20,28},{24,16},{28,20},{1,9},{5... | collective-permute-start | bytes 6152 | tf_op jit(solution)/shard_map/ppermute | solution.py:35
  165.9 0.9 copy-start.11
  165.9 1.0 copy-start.9

commit v5 on v4

--- a/solution.py
+++ b/solution.py
@@ -342,7 +342,7 @@
     rows, inner = mixed.shape
     full = lambda dtype: jax.ShapeDtypeStruct((rows, inner), dtype)
     return pl.pallas_call(
-        functools.partial(scan_kernel, 4),
+        functools.partial(scan_kernel, 8),
         in_specs=[WHOLE] * 8,
         out_specs=[WHOLE] * 5 + [pl.BlockSpec(memory_space=pl.ANY), WHOLE],
         out_shape=[
@@ -356,7 +356,7 @@
         ],
         scratch_shapes=[pltpu.VMEM((rows * SUB, LANES), F32)] * 3
         + [
-            pltpu.VMEM((2 * states * rows, LANES), F32),
+            pltpu.VMEM((2 * states * rows + SUB, LANES), F32),
             pltpu.VMEM((2, rows // 8, states // 2, 2 * SUB, LANES), BF16),
             pltpu.SemaphoreType.DMA((2,)),
         ],
@@ -373,7 +373,7 @@
     rows, inner = mixed.shape
     states = last.shape[0]
     rank = wup.shape[0]
-    span = zk.shape[0] // states
+    span = rows + SUB
     chunk = slots.shape[1]
     chunks = rows // chunk
 
@@ -516,12 +516,12 @@
             pltpu.VMEM((rows * SUB, LANES), F32),
             pltpu.VMEM((rows * SUB, LANES), F32),
             pltpu.VMEM((rows * SUB + SUB, LANES), F32),
-            pltpu.VMEM((2 * states * rows, LANES), F32),
+            pltpu.VMEM((2 * states * rows + SUB, LANES), F32),
             pltpu.VMEM((rows * SUB, LANES), F32),
             pltpu.VMEM((rows * SUB, LANES), F32),
-            pltpu.VMEM((unroll * 2 * states * SUB, LANES), F32),
-            pltpu.VMEM((states * span, LANES), F32),
-            pltpu.VMEM((states * span, LANES), F32),
+            pltpu.VMEM((unroll * 2 * states * SUB + SUB * SUB, LANES), F32),
+            pltpu.VMEM((states * span + span, LANES), F32),
+            pltpu.VMEM((states * span + span, LANES), F32),
             pltpu.VMEM((2, rows // 8, states // 2, 2 * SUB, LANES), BF16),
             pltpu.SemaphoreType.DMA((2,)),
         ],
@@ -1185,7 +1185,9 @@
         (grad_wz,) = grad_wz
         far_send = (later + come_out[1].astype(F32)).astype(BF16)
         far_out = swap(far_send, "dp", 2)
-        stats, small = after((stats, small), (in_hbm(come_x), in_hbm(come_out)))
+        small = lax.reduce_precision(small.reshape(-1, small.shape[-1]), 8, 7)
+        flipped = jnp.concatenate([small[SMALL:], small[:SMALL]], axis=0).astype(BF16)
+        stats, flipped = after((stats, flipped), (in_hbm(come_x), in_hbm(come_out)))
     else:
 
         def weight_grad(value, left):
@@ -1215,8 +1217,6 @@
     count = 2 * states
     rank = w_up.shape[0]
     if blocked:
-        small = lax.reduce_precision(small.reshape(-1, small.shape[-1]), 8, 7)
-        flipped = jnp.concatenate([small[SMALL:], small[:SMALL]], axis=0).astype(BF16)
         gathered = (small + swap(flipped, "dp", 4).astype(F32)).astype(BF16)
         for bit in (4, 1, 2):
             gain = gain + swap(gain, "dp", bit)

time: 173 us -> 173 us (level)
    unnamed x30 -> x28, local copies, waits for them, and re-layouts: 3.66 us -> 3.65 us
  transfers between devices with their start and end apart: 32 -> 32, of which waited for: 14 -> 13; matrix products, arithmetic and copies ran while one was open for 4% -> 4% of each run, Pallas kernels for 40% -> 39%
where the time goes in v5:
time: 173 us
  Pallas kernels  80.7 us (47%)
  waiting for transfers between devices  47.4 us (27%)
  starting transfers between devices  32.2 us (19%)
  other arithmetic  5.99 us (3%)
  local copies, waits for them, and re-layouts  4.9 us (3%)
    ppermute x32, waiting for transfers between devices, swap(): return lax.ppermute(value, axis, [(i, i ^ bit) for i in range(size)])  47.4 us
    ppermute x32, starting transfers between devices, swap(): return lax.ppermute(value, axis, [(i, i ^ bit) for i in range(size)])  32.2 us
    pallas_call x1, Pallas kernels, scan_backward(): pl.pallas_call(functools.partial(back_kernel, unroll, len(pins)), in_spec...  19.3 us
    pallas_call x1, Pallas kernels, scan_forward(): pl.pallas_call(functools.partial(scan_kernel, 8), in_specs=[WHOLE] * 8, o...  10.6 us
    pallas_call x1, Pallas kernels, input_grad(): pl.pallas_call(functools.partial(input_kernel, len(pins), len(extra)), gr...  10.3 us
    pallas_call x1, Pallas kernels, middle(): pl.pallas_call(middle_kernel, grid_spec=pltpu.PrefetchScalarGridSpec(num_...  8.45 us
    pallas_call x2, Pallas kernels, in_weight(): pl.pallas_call(functools.partial(in_weight_kernel, len(pins)), grid=(2,),...  7.73 us
    pallas_call x1, Pallas kernels, front(): pl.pallas_call(functools.partial(front_kernel, blocked), grid=(inner // b...  7.54 us
  transfers between devices with their start and end apart: 32, of which 13 were waited for; matrix products, arithmetic and copies ran while one was open for 4% of the time, Pallas kernels for 39%

profile of v5, /device:TPU:0, one launch (start us, length us, event | category | flops | bytes accessed | tf_op | source)
XLA Modules:
  0.0 172.8 jit_solution(13908335289272980124)
XLA Ops:
  2.0 7.5 %front.1 = (bf16[256,2048]{1,0:T(8,128)(2,1)S(1)}, bf16[256,2048]{1,0:T(8,128)(2,1)S(1)}, f32[256,1024]{1,0:T(8,128)}, bf16[256,1024]{1,0:T(8,128)(2,1)}, f32[25...) custom-call(s32[2]{0:T(128)S(1)} %pad_add_fusion.place, ...), custom_call_target="tpu_custom_call" | custom-call | tf_op jit(solution)/shard_map/front/pallas_call | solution.py:167
  10.1 2.6 %collective-permute-start.1 = (bf16[2,256,512]{2,1,0:T(8,128)(2,1)}, bf16[2,256,512]{2,1,0:T(8,128)(2,1)S(1)}, u32[]{:S(2)}, u32[]{:S(2)}) collective-permute-start(bf16[2,256,512]{2,1,0:T(8,128)(2,1)} %get-tuple-element.77), channel_id=1, source_target_pairs={{0,4},{4,0},{8,12},{12,8},{16,20},{20,16},{24,28},{28,24},{1,5},{5... | collective-permute-start | bytes 1572872 | tf_op jit(solution)/shard_map/ppermute | solution.py:35
  12.7 1.6 collective-permute-start.4
  14.3 1.6 collective-permute-start
  15.8 2.6 %collective-permute-start.5 = (bf16[128,1024]{1,0:T(8,128)(2,1)}, bf16[128,1024]{1,0:T(8,128)(2,1)S(1)}, u32[]{:S(2)}, u32[]{:S(2)}) collective-permute-start(bf16[128,1024]{1,0:T(8,128)(2,1)} %get-tuple-element.90), channel_id=1, source_target_pairs={{0,16},{4,20},{8,24},{12,28},{16,0},{20,4},{24,8},{28,12},{1,17},{... | collective-permute-start | bytes 786440 | tf_op jit(solution)/shard_map/ppermute | solution.py:35
  18.4 5.8 %gate.1 = (f32[256,1024]{1,0:T(8,128)S(1)}, f32[256,1024]{1,0:T(8,128)S(1)}, f32[256,1024]{1,0:T(8,128)}) custom-call(bf16[256,2048]{1,0:T(8,128)(2,1)S(1)} %get-tuple-element.80.normed, bf16[256,2048]{1,0:T(8,128)(2,1)S(1)} %get-tuple-element.81.up, bf16[2048,1024]{1,0:T(8,128)(2,1)} %wz.3, bf16[1024,2048]{1,0:T(8,128)(2,1)} %wo.3), custom_call_target="tpu_custom_call" | custom-call | tf_op jit(solution)/shard_map/gate/pallas_call | solution.py:227
  24.2 10.6 %scan.1 = (bf16[256,1024]{1,0:T(8,128)(2,1)}, bf16[256,1024]{1,0:T(8,128)(2,1)}, f32[256,1024]{1,0:T(8,128)S(1)}, f32[256,1024]{1,0:T(8,128)S(1)}, f32[8,128]{1,...) custom-call(f32[320,128]{1,0:T(8,128)S(1)} %add.41.one, ...), custom_call_target="tpu_custom_call" | custom-call | tf_op jit(solution)/shard_map/scan/pallas_call | solution.py:344
  35.4 1.3 collective-permute-start.10
  37.0 19.3 %back.1 = (f32[256,1024]{1,0:T(8,128)}, f32[336,128]{1,0:T(8,128)S(1)}, f32[136,1024]{1,0:T(8,128)}) custom-call(s32[2]{0:T(128)S(1)} %pad_add_fusion.place, f32[320,128]{1,0:T(8,128)S(1)} %add.41.one, f32[320,128]{1,0:T(8,128)S(1)} %collective-permute-done.4.two, bf16[256,1024]{1,0:T(8,128)(2,1)} %get-tuple-element.79.mixed, bf16[128,1024]{1,0:T(8,128)(2,1)} %wup.3, ...), custom_call_target="tpu_custom_call" | custom-call | tf_op jit(solution)/shard_map/back/pallas_call | solution.py:501
  56.9 0.7 slice_bitcast_fusion.3
  57.9 1.6 collective-permute-start.2
  59.5 0.7 add.42.grad_one
  61.0 0.7 collective-permute-start.16
  61.8 5.5 %collective-permute-done.2.rest_3_.l3 = bf16[256,512]{1,0:T(8,128)(2,1)S(1)} collective-permute-done((bf16[256,512]{1,0:T(8,128)(2,1)}, bf16[256,512]{1,0:T(8,128)(2,1)S(1)}, u32[]{:S(2)}, u32[]{:S(2)}) %collective-permute-start.2) | collective-permute-done | bytes 262176 | tf_op jit(solution)/shard_map/ppermute | solution.py:35
  67.3 5.7 %conv.1 = (bf16[256,1024]{1,0:T(8,128)(2,1)}, f32[4,40,1024]{2,1,0:T(8,128)}, bf16[4,40,1024]{2,1,0:T(8,128)(2,1)}) custom-call(s32[2]{0:T(128)S(1)} %pad_add_fusion.place, f32[320,128]{1,0:T(8,128)S(1)} %add.41.one, f32[320,128]{1,0:T(8,128)S(1)} %collective-permute-done.4.two, f32[336,128]{1,0:T(8,128)} %add.42.grad_one, ...), custom_call_target="tpu_custom_call" | custom-call | tf_op jit(solution)/shard_map/conv/pallas_call | solution.py:618
  73.0 1.1 collective-permute-start.11
  74.1 0.7 collective-permute-start.12
  74.8 1.3 collective-permute-start.14
  76.2 3.9 %inw.2 = (f32[256,1024]{1,0:T(8,128)}, bf16[256,1024]{1,0:T(8,128)(2,1)}) custom-call(bf16[256,512]{1,0:T(8,128)(2,1)} %get-tuple-element.75.l0, bf16[256,512]{1,0:T(8,128)(2,1)S(1)} %collective-permute-done.rest_0_.l1, bf16[2,256,512]{2,1,0:T(8,128)(2,1)S(1)} %collective-permute-done.1.rest_1_.l2, bf16[256,512]{1,0:T(8,128)(2,1)S(1)} %collective-permute-done.2.rest_3_.l3, ...), custom_call_target="tpu_custom_call" | custom-call | tf_op jit(solution)/shard_map/inw/pallas_call | solution.py:1033
  80.0 2.6 %collective-permute-start.17 = (bf16[256,1024]{1,0:T(8,128)(2,1)}, bf16[256,1024]{1,0:T(8,128)(2,1)S(1)}, u32[]{:S(2)}, u32[]{:S(2)}) collective-permute-start(bf16[256,1024]{1,0:T(8,128)(2,1)} %get-tuple-element.102.rest_0_), channel_id=1, source_target_pairs={{0,16},{4,20},{8,24},{12,28},{16,0},{20,4},{24,8},{28,12},{1,17},{... | collective-permute-start | bytes 1572872 | tf_op jit(solution)/shard_map/ppermute | solution.py:35
  82.6 10.4 %collective-permute-done.11.rest_1_.r1 = bf16[256,1024]{1,0:T(8,128)(2,1)S(1)} collective-permute-done((bf16[256,1024]{1,0:T(8,128)(2,1)}, bf16[256,1024]{1,0:T(8,128)(2,1)S(1)}, u32[]{:S(2)}, u32[]{:S(2)}) %collective-permute-start.11) | collective-permute-done | bytes 524320 | tf_op jit(solution)/shard_map/ppermute | solution.py:35
  93.1 0.7 collective-permute-start.13
  93.8 0.7 collective-permute-done.14.small_come
  94.5 8.4 %middle.1 = (f32[1024,256]{1,0:T(8,128)}, f32[1024,256]{1,0:T(8,128)}, bf16[2,1024,256]{2,1,0:T(8,128)(2,1)}, bf16[2,2,256,512]{3,2,1,0:T(8,128)(2,1)}, f32[256,...) custom-call(s32[2]{0:T(128)S(1)} %pad_add_fusion.place, ...), custom_call_target="tpu_custom_call" | custom-call | tf_op jit(solution)/shard_map/middle/pallas_call | solution.py:864
  102.9 0.8 collective-permute-start.19
  103.7 1.2 collective-permute-done.17.rest_1_
  105.0 3.0 %collective-permute-done.13.r3 = bf16[256,1024]{1,0:T(8,128)(2,1)S(1)} collective-permute-done((bf16[256,1024]{1,0:T(8,128)(2,1)S(1)}, bf16[256,1024]{1,0:T(8,128)(2,1)S(1)}, u32[]{:S(2)}, u32[]{:S(2)}) %collective-permute-start.13) | collective-permute-done | bytes 524320 | tf_op jit(solution)/shard_map/ppermute | solution.py:35
  107.9 3.9 %inw.3 = (f32[256,1024]{1,0:T(8,128)}, bf16[256,1024]{1,0:T(8,128)(2,1)}) custom-call(bf16[256,512]{1,0:T(8,128)(2,1)} %get-tuple-element.75.l0, bf16[256,512]{1,0:T(8,128)(2,1)S(1)} %collective-permute-done.rest_0_.l1, bf16[2,256,512]{2,1,0:T(8,128)(2,1)S(1)} %collective-permute-done.1.rest_1_.l2, bf16[256,512]{1,0:T(8,128)(2,1)S(1)} %collective-permute-done.2.rest_3_.l3, ...), custom_call_target="tpu_custom_call" | custom-call | tf_op jit(solution)/shard_map/inw/pallas_call | solution.py:1033
  112.0 2.2 %collective-permute-start.18 = (bf16[256,1024]{1,0:T(8,128)(2,1)}, bf16[256,1024]{1,0:T(8,128)(2,1)S(1)}, u32[]{:S(2)}, u32[]{:S(2)}) collective-permute-start(bf16[256,1024]{1,0:T(8,128)(2,1)} %get-tuple-element.105.rest_2_.refs_1_), channel_id=1, source_target_pairs={{0,16},{4,20},{8,24},{12,28},{16,0},{20,4},{24,8},{28,12},{1,17},{... | collective-permute-start | bytes 1572872 | tf_op jit(solution)/shard_map/ppermute | solution.py:35
  114.2 10.3 %inputs.1 = (bf16[2,2,256,512]{3,2,1,0:T(8,128)(2,1)}, f32[256,512]{1,0:T(8,128)}, f32[256,512]{1,0:T(8,128)}, f32[18,128]{1,0:T(8,128)S(1)}, f32[256,512]{1,0:T...) custom-call(s32[2]{0:T(128)S(1)} %pad_add_fusion.place, ...), custom_call_target="tpu_custom_call", output_to_operand_aliasing={{0}: (3, {})} | custom-call | tf_op jit(solution)/shard_map/inputs/pallas_call | solution.py:768
  125.2 0.7 pad_maximum_fusion.2.refs_1_
  125.8 10.0 %collective-permute-done.18.refs_2_.come_x = bf16[256,1024]{1,0:T(8,128)(2,1)S(1)} collective-permute-done((bf16[256,1024]{1,0:T(8,128)(2,1)}, bf16[256,1024]{1,0:T(8,128)(2,1)S(1)}, u32[]{:S(2)}, u32[]{:S(2)}) %collective-permute-start.18) | collective-permute-done | bytes 524320 | tf_op jit(solution)/shard_map/ppermute | solution.py:35
  135.8 0.8 copy-done.10
  136.9 1.4 collective-permute-done.24
  138.3 0.7 add.47
  139.6 1.5 fusion
  141.0 1.3 collective-permute-start.20
  142.8 1.6 collective-permute-start.29
  144.4 3.4 %collective-permute-done.26 = bf16[80,1024]{1,0:T(8,128)(2,1)S(1)} collective-permute-done((bf16[80,1024]{1,0:T(8,128)(2,1)}, bf16[80,1024]{1,0:T(8,128)(2,1)S(1)}, u32[]{:S(2)}, u32[]{:S(2)}) %collective-permute-start.26) | collective-permute-done | bytes 163872 | tf_op jit(solution)/shard_map/ppermute | solution.py:35
  147.8 0.8 collective-permute-start.27
  148.6 1.6 fusion.4
  150.8 3.1 %collective-permute-done.27.g2 = bf16[80,1024]{1,0:T(8,128)(2,1)S(1)} collective-permute-done((bf16[80,1024]{1,0:T(8,128)(2,1)S(1)}, bf16[80,1024]{1,0:T(8,128)(2,1)S(1)}, u32[]{:S(2)}, u32[]{:S(2)}) %collective-permute-start.27) | collective-permute-done | bytes 163872 | tf_op jit(solution)/shard_map/ppermute | solution.py:35
  154.1 0.8 collective-permute-start.30
  154.8 2.9 %collective-permute-done.30 = f32[4,128]{1,0:T(4,128)S(1)} collective-permute-done((f32[4,128]{1,0:T(4,128)S(1)}, f32[4,128]{1,0:T(4,128)S(1)}, u32[]{:S(2)}, u32[]{:S(2)}) %collective-permute-start.30) | collective-permute-done | bytes 2080 | tf_op jit(solution)/shard_map/ppermute | solution.py:35
  157.7 2.4 %collective-permute-start.31 = (f32[4,128]{1,0:T(4,128)S(1)}, f32[4,128]{1,0:T(4,128)S(1)}, u32[]{:S(2)}, u32[]{:S(2)}) collective-permute-start(f32[4,128]{1,0:T(4,128)S(1)} %add.52), channel_id=1, source_target_pairs={{0,8},{4,12},{8,0},{12,4},{16,24},{20,28},{24,16},{28,20},{1,9},{5... | collective-permute-start | bytes 6152 | tf_op jit(solution)/shard_map/ppermute | solution.py:35
  160.1 5.2 %collective-permute-done.31 = f32[4,128]{1,0:T(4,128)S(1)} collective-permute-done((f32[4,128]{1,0:T(4,128)S(1)}, f32[4,128]{1,0:T(4,128)S(1)}, u32[]{:S(2)}, u32[]{:S(2)}) %collective-permute-start.31) | collective-permute-done | bytes 2080 | tf_op jit(solution)/shard_map/ppermute | solution.py:35
  166.0 0.8 copy-done.11
  167.0 5.3 %finale.1 = (f32[256,1024]{1,0:T(8,128)}, f32[1024,256]{1,0:T(8,128)}, bf16[256,512]{1,0:T(8,128)(2,1)}, f32[256,512]{1,0:T(8,128)}, f32[128,1024]{1,0:T(8,128)}...) custom-call(s32[2]{0:T(128)S(1)} %pad_add_fusion.place, ...), custom_call_target="tpu_custom_call" | custom-call | tf_op jit(solution)/shard_map/finale/pallas_call | solution.py:966
  (77 shorter events, 8.1 us)
Async XLA Ops:
  1.4 0.7 copy-start.5
  9.6 3.1 %collective-permute-start.3 = (f32[320,128]{1,0:T(8,128)S(1)}, f32[320,128]{1,0:T(8,128)S(1)}, u32[]{:S(2)}, u32[]{:S(2)}) collective-permute-start(f32[320,128]{1,0:T(8,128)S(1)} %get-tuple-element.78), channel_id=1, source_target_pairs={{0,1},{1,0},{2,3},{3,2},{4,5},{5,4},{6,7},{7,6},{8,9},{9,8},{10,11... | collective-permute-start | bytes 491528 | tf_op jit(solution)/shard_map/ppermute | solution.py:35
  10.1 26.9 %collective-permute-start.1 = (bf16[2,256,512]{2,1,0:T(8,128)(2,1)}, bf16[2,256,512]{2,1,0:T(8,128)(2,1)S(1)}, u32[]{:S(2)}, u32[]{:S(2)}) collective-permute-start(bf16[2,256,512]{2,1,0:T(8,128)(2,1)} %get-tuple-element.77), channel_id=1, source_target_pairs={{0,4},{4,0},{8,12},{12,8},{16,20},{20,16},{24,28},{28,24},{1,5},{5... | collective-permute-start | bytes 1572872 | tf_op jit(solution)/shard_map/ppermute | solution.py:35
  12.7 11.5 %collective-permute-start.4 = (f32[320,128]{1,0:T(8,128)S(1)}, f32[320,128]{1,0:T(8,128)S(1)}, u32[]{:S(2)}, u32[]{:S(2)}) collective-permute-start(f32[320,128]{1,0:T(8,128)S(1)} %add.41.one), channel_id=1, source_target_pairs={{0,2},{1,3},{2,0},{3,1},{4,6},{5,7},{6,4},{7,5},{8,10},{9,11},{10,... | collective-permute-start | bytes 491528 | tf_op jit(solution)/shard_map/ppermute | solution.py:35
  14.3 22.4 %collective-permute-start = (bf16[256,512]{1,0:T(8,128)(2,1)}, bf16[256,512]{1,0:T(8,128)(2,1)S(1)}, u32[]{:S(2)}, u32[]{:S(2)}) collective-permute-start(bf16[256,512]{1,0:T(8,128)(2,1)} %get-tuple-element.76), channel_id=1, source_target_pairs={{0,8},{4,12},{8,0},{12,4},{16,24},{20,28},{24,16},{28,20},{1,9},{5... | collective-permute-start | bytes 786440 | tf_op jit(solution)/shard_map/ppermute | solution.py:35
  15.8 21.2 %collective-permute-start.5 = (bf16[128,1024]{1,0:T(8,128)(2,1)}, bf16[128,1024]{1,0:T(8,128)(2,1)S(1)}, u32[]{:S(2)}, u32[]{:S(2)}) collective-permute-start(bf16[128,1024]{1,0:T(8,128)(2,1)} %get-tuple-element.90), channel_id=1, source_target_pairs={{0,16},{4,20},{8,24},{12,28},{16,0},{20,4},{24,8},{28,12},{1,17},{... | collective-permute-start | bytes 786440 | tf_op jit(solution)/shard_map/ppermute | solution.py:35
  34.8 25.4 %collective-permute-start.15 = (bf16[256,1024]{1,0:T(8,128)(2,1)}, bf16[256,1024]{1,0:T(8,128)(2,1)S(1)}, u32[]{:S(2)}, u32[]{:S(2)}) collective-permute-start(bf16[256,1024]{1,0:T(8,128)(2,1)} %get-tuple-element.97.r0.prez), channel_id=1, source_target_pairs={{0,8},{4,12},{8,0},{12,4},{16,24},{20,28},{24,16},{28,20},{1,9},{5... | collective-permute-start | bytes 1572872 | tf_op jit(solution)/shard_map/ppermute | solution.py:35
  35.4 31.9 %collective-permute-start.10 = (bf16[256,1024]{1,0:T(8,128)(2,1)}, bf16[256,1024]{1,0:T(8,128)(2,1)S(1)}, u32[]{:S(2)}, u32[]{:S(2)}) collective-permute-start(bf16[256,1024]{1,0:T(8,128)(2,1)} %get-tuple-element.97.r0.prez), channel_id=1, source_target_pairs={{0,4},{4,0},{8,12},{12,8},{16,20},{20,16},{24,28},{28,24},{1,5},{5... | collective-permute-start | bytes 1572872 | tf_op jit(solution)/shard_map/ppermute | solution.py:35
  36.7 30.6 %collective-permute-start.8 = (bf16[256,1024]{1,0:T(8,128)(2,1)}, bf16[256,1024]{1,0:T(8,128)(2,1)S(1)}, u32[]{:S(2)}, u32[]{:S(2)}) collective-permute-start(bf16[256,1024]{1,0:T(8,128)(2,1)} %get-tuple-element.96.gated.every), channel_id=1, source_target_pairs={{0,16},{4,20},{8,24},{12,28},{16,0},{20,4},{24,8},{28,12},{1,17},{... | collective-permute-start | bytes 1572872 | tf_op jit(solution)/shard_map/ppermute | solution.py:35
  37.0 24.0 %collective-permute-start.9 = (bf16[128,1024]{1,0:T(8,128)(2,1)S(1)}, bf16[128,1024]{1,0:T(8,128)(2,1)S(1)}, u32[]{:S(2)}, u32[]{:S(2)}) collective-permute-start(bf16[128,1024]{1,0:T(8,128)(2,1)S(1)} %collective-permute-done.5.rest_2_.up_a), channel_id=1, source_target_pairs={{0,1},{1,0},{2,3},{3,2},{4,5},{5,4},{6,7},{7,6},{8,9},{9,8},{10,11... | collective-permute-start | bytes 786440 | tf_op jit(solution)/shard_map/ppermute | solution.py:35
  56.3 3.9 %copy-start.2 = (f32[336,128]{1,0:T(8,128)}, f32[336,128]{1,0:T(8,128)S(1)}, u32[]{:S(2)}) copy-start(f32[336,128]{1,0:T(8,128)S(1)} %get-tuple-element.91.refs_1_) | copy-start | bytes 516100
  56.3 1.6 collective-permute-start.6
  57.9 9.3 %collective-permute-start.2 = (bf16[256,512]{1,0:T(8,128)(2,1)}, bf16[256,512]{1,0:T(8,128)(2,1)S(1)}, u32[]{:S(2)}, u32[]{:S(2)}) collective-permute-start(bf16[256,512]{1,0:T(8,128)(2,1)} %slice_bitcast_fusion.3), channel_id=1, source_target_pairs={{0,8},{4,12},{8,0},{12,4},{16,24},{20,28},{24,16},{28,20},{1,9},{5... | collective-permute-start | bytes 786440 | tf_op jit(solution)/shard_map/ppermute | solution.py:35
  60.2 0.8 copy-start
  60.2 7.0 %collective-permute-start.7 = (f32[336,128]{1,0:T(8,128)}, f32[336,128]{1,0:T(8,128)}, u32[]{:S(2)}, u32[]{:S(2)}) collective-permute-start(f32[336,128]{1,0:T(8,128)} %add.42.grad_one), channel_id=1, source_target_pairs={{0,2},{1,3},{2,0},{3,1},{4,6},{5,7},{6,4},{7,5},{8,10},{9,11},{10,... | collective-permute-start | bytes 516104 | tf_op jit(solution)/shard_map/ppermute | solution.py:35
  61.0 15.1 %copy-start.1 = (bf16[256,1024]{1,0:T(8,128)(2,1)S(1)}, bf16[256,1024]{1,0:T(8,128)(2,1)}, u32[]{:S(2)}) copy-start(bf16[256,1024]{1,0:T(8,128)(2,1)} %after.3.r1) | copy-start | bytes 1572868
  61.0 15.1 %collective-permute-start.16 = (bf16[256,1024]{1,0:T(8,128)(2,1)}, bf16[256,1024]{1,0:T(8,128)(2,1)S(1)}, u32[]{:S(2)}, u32[]{:S(2)}) collective-permute-start(bf16[256,1024]{1,0:T(8,128)(2,1)} %after.3.r1), channel_id=1, source_target_pairs={{0,4},{4,0},{8,12},{12,8},{16,20},{20,16},{24,28},{28,24},{1,5},{5... | collective-permute-start | bytes 1572872 | tf_op jit(solution)/shard_map/ppermute | solution.py:35
  67.3 27.2 %copy-start.3 = (bf16[256,1024]{1,0:T(8,128)(2,1)S(1)}, bf16[256,1024]{1,0:T(8,128)(2,1)}, u32[]{:S(2)}) copy-start(bf16[256,1024]{1,0:T(8,128)(2,1)} %get-tuple-element.99.up_own) | copy-start | bytes 1572868
  73.0 20.0 %collective-permute-start.11 = (bf16[256,1024]{1,0:T(8,128)(2,1)}, bf16[256,1024]{1,0:T(8,128)(2,1)S(1)}, u32[]{:S(2)}, u32[]{:S(2)}) collective-permute-start(bf16[256,1024]{1,0:T(8,128)(2,1)} %get-tuple-element.98.rest_0_.r0.prex), channel_id=1, source_target_pairs={{0,8},{4,12},{8,0},{12,4},{16,24},{20,28},{24,16},{28,20},{1,9},{5... | collective-permute-start | bytes 1572872 | tf_op jit(solution)/shard_map/ppermute | solution.py:35
  74.1 20.3 %collective-permute-start.12 = (bf16[256,1024]{1,0:T(8,128)(2,1)}, bf16[256,1024]{1,0:T(8,128)(2,1)S(1)}, u32[]{:S(2)}, u32[]{:S(2)}) collective-permute-start(bf16[256,1024]{1,0:T(8,128)(2,1)} %get-tuple-element.98.rest_0_.r0.prex), channel_id=1, source_target_pairs={{0,4},{4,0},{8,12},{12,8},{16,20},{20,16},{24,28},{28,24},{1,5},{5... | collective-permute-start | bytes 1572872 | tf_op jit(solution)/shard_map/ppermute | solution.py:35
  74.8 19.6 %collective-permute-start.14 = (bf16[4,40,1024]{2,1,0:T(8,128)(2,1)}, bf16[4,40,1024]{2,1,0:T(8,128)(2,1)S(1)}, u32[]{:S(2)}, u32[]{:S(2)}) collective-permute-start(bf16[4,40,1024]{2,1,0:T(8,128)(2,1)} %get-tuple-element.101), channel_id=1, source_target_pairs={{0,4},{4,0},{8,12},{12,8},{16,20},{20,16},{24,28},{28,24},{1,5},{5... | collective-permute-start | bytes 983048 | tf_op jit(solution)/shard_map/ppermute | solution.py:35
  80.0 24.9 %collective-permute-start.17 = (bf16[256,1024]{1,0:T(8,128)(2,1)}, bf16[256,1024]{1,0:T(8,128)(2,1)S(1)}, u32[]{:S(2)}, u32[]{:S(2)}) collective-permute-start(bf16[256,1024]{1,0:T(8,128)(2,1)} %get-tuple-element.102.rest_0_), channel_id=1, source_target_pairs={{0,16},{4,20},{8,24},{12,28},{16,0},{20,4},{24,8},{28,12},{1,17},{... | collective-permute-start | bytes 1572872 | tf_op jit(solution)/shard_map/ppermute | solution.py:35
  93.1 14.9 %collective-permute-start.13 = (bf16[256,1024]{1,0:T(8,128)(2,1)S(1)}, bf16[256,1024]{1,0:T(8,128)(2,1)S(1)}, u32[]{:S(2)}, u32[]{:S(2)}) collective-permute-start(bf16[256,1024]{1,0:T(8,128)(2,1)S(1)} %collective-permute-done.11.rest_1_.r1), channel_id=1, source_target_pairs={{0,4},{4,0},{8,12},{12,8},{16,20},{20,16},{24,28},{28,24},{1,5},{5... | collective-permute-start | bytes 1572872 | tf_op jit(solution)/shard_map/ppermute | solution.py:35
  102.9 11.3 %copy-start.6 = (f32[8]{0:T(128)S(1)}, f32[8]{0:T(128)}, u32[]{:S(2)}) copy-start(f32[8]{0:T(128)} %weights.3) | copy-start | bytes 100
  102.9 32.9 %collective-permute-start.19 = (bf16[2,1024,256]{2,1,0:T(8,128)(2,1)}, bf16[2,1024,256]{2,1,0:T(8,128)(2,1)S(1)}, u32[]{:S(2)}, u32[]{:S(2)}) collective-permute-start(bf16[2,1024,256]{2,1,0:T(8,128)(2,1)} %get-tuple-element.103.rest_0_), channel_id=1, source_target_pairs={{0,4},{4,0},{8,12},{12,8},{16,20},{20,16},{24,28},{28,24},{1,5},{5... | collective-permute-start | bytes 3145736 | tf_op jit(solution)/shard_map/ppermute | solution.py:35
  111.8 13.3 %collective-permute-start.23 = (bf16[2,40,1024]{2,1,0:T(8,128)(2,1)}, bf16[2,40,1024]{2,1,0:T(8,128)(2,1)S(1)}, u32[]{:S(2)}, u32[]{:S(2)}) collective-permute-start(bf16[2,40,1024]{2,1,0:T(8,128)(2,1)} %after.4), channel_id=1, source_target_pairs={{0,8},{4,12},{8,0},{12,4},{16,24},{20,28},{24,16},{28,20},{1,9},{5... | collective-permute-start | bytes 491528 | tf_op jit(solution)/shard_map/ppermute | solution.py:35
  112.0 23.8 %collective-permute-start.18 = (bf16[256,1024]{1,0:T(8,128)(2,1)}, bf16[256,1024]{1,0:T(8,128)(2,1)S(1)}, u32[]{:S(2)}, u32[]{:S(2)}) collective-permute-start(bf16[256,1024]{1,0:T(8,128)(2,1)} %get-tuple-element.105.rest_2_.refs_1_), channel_id=1, source_target_pairs={{0,16},{4,20},{8,24},{12,28},{16,0},{20,4},{24,8},{28,12},{1,17},{... | collective-permute-start | bytes 1572872 | tf_op jit(solution)/shard_map/ppermute | solution.py:35
  114.2 10.9 %copy-start.13 = (f32[2,40,1024]{2,1,0:T(8,128)S(1)}, f32[2,40,1024]{2,1,0:T(8,128)}, u32[]{:S(2)}) copy-start(f32[2,40,1024]{2,1,0:T(8,128)} %get-tuple-element.116) | copy-start | bytes 983044
  124.5 0.6 copy-start.4
  125.1 23.5 %copy-start.12 = (f32[256,512]{1,0:T(8,128)S(1)}, f32[256,512]{1,0:T(8,128)}, u32[]{:S(2)}) copy-start(f32[256,512]{1,0:T(8,128)} %get-tuple-element.113) | copy-start | bytes 1572868
  125.1 23.5 %collective-permute-start.21 = (bf16[2,2,256,512]{3,2,1,0:T(8,128)(2,1)}, bf16[2,2,256,512]{3,2,1,0:T(8,128)(2,1)S(1)}, u32[]{:S(2)}, u32[]{:S(2)}) collective-permute-start(bf16[2,2,256,512]{3,2,1,0:T(8,128)(2,1)} %get-tuple-element.112), channel_id=1, source_target_pairs={{0,1},{1,0},{2,3},{3,2},{4,5},{5,4},{6,7},{7,6},{8,9},{9,8},{10,11... | collective-permute-start | bytes 3145736 | tf_op jit(solution)/shard_map/ppermute | solution.py:35
  135.8 0.8 copy-start.10
  135.8 1.1 copy-start.7
  136.9 1.4 collective-permute-start.24
  136.9 10.8 %collective-permute-start.26 = (bf16[80,1024]{1,0:T(8,128)(2,1)}, bf16[80,1024]{1,0:T(8,128)(2,1)S(1)}, u32[]{:S(2)}, u32[]{:S(2)}) collective-permute-start(bf16[80,1024]{1,0:T(8,128)(2,1)} %get-tuple-element.122), channel_id=1, source_target_pairs={{0,16},{4,20},{8,24},{12,28},{16,0},{20,4},{24,8},{28,12},{1,17},{... | collective-permute-start | bytes 491528 | tf_op jit(solution)/shard_map/ppermute | solution.py:35
  139.0 3.7 %collective-permute-start.25 = (f32[18,128]{1,0:T(8,128)S(1)}, f32[18,128]{1,0:T(8,128)S(1)}, u32[]{:S(2)}, u32[]{:S(2)}) collective-permute-start(f32[18,128]{1,0:T(8,128)S(1)} %add.47), channel_id=1, source_target_pairs={{0,2},{1,3},{2,0},{3,1},{4,6},{5,7},{6,4},{7,5},{8,10},{9,11},{10,... | collective-permute-start | bytes 27656 | tf_op jit(solution)/shard_map/ppermute | solution.py:35
  141.0 24.9 %collective-permute-start.20 = (bf16[1024,256]{1,0:T(8,128)(2,1)S(1)}, bf16[1024,256]{1,0:T(8,128)(2,1)S(1)}, u32[]{:S(2)}, u32[]{:S(2)}) collective-permute-start(bf16[1024,256]{1,0:T(8,128)(2,1)S(1)} %fusion), channel_id=1, source_target_pairs={{0,8},{4,12},{8,0},{12,4},{16,24},{20,28},{24,16},{28,20},{1,9},{5... | collective-permute-start | bytes 1572872 | tf_op jit(solution)/shard_map/ppermute | solution.py:35
  142.8 11.3 %collective-permute-start.29 = (f32[4,128]{1,0:T(4,128)S(1)}, f32[4,128]{1,0:T(4,128)S(1)}, u32[]{:S(2)}, u32[]{:S(2)}) collective-permute-start(f32[4,128]{1,0:T(4,128)S(1)} %constant_dynamic-slice_fusion), channel_id=1, source_target_pairs={{0,16},{4,20},{8,24},{12,28},{16,0},{20,4},{24,8},{28,12},{1,17},{... | collective-permute-start | bytes 6152 | tf_op jit(solution)/shard_map/ppermute | solution.py:35
  147.8 6.2 %collective-permute-start.27 = (bf16[80,1024]{1,0:T(8,128)(2,1)S(1)}, bf16[80,1024]{1,0:T(8,128)(2,1)S(1)}, u32[]{:S(2)}, u32[]{:S(2)}) collective-permute-start(bf16[80,1024]{1,0:T(8,128)(2,1)S(1)} %fusion.3.g0), channel_id=1, source_target_pairs={{0,4},{4,0},{8,12},{12,8},{16,20},{20,16},{24,28},{28,24},{1,5},{5... | collective-permute-start | bytes 491528 | tf_op jit(solution)/shard_map/ppermute | solution.py:35
  148.5 17.4 %copy-start.8 = (bf16[2,2,256,512]{3,2,1,0:T(8,128)(2,1)}, bf16[2,2,256,512]{3,2,1,0:T(8,128)(2,1)S(1)}, u32[]{:S(2)}) copy-start(bf16[2,2,256,512]{3,2,1,0:T(8,128)(2,1)S(1)} %collective-permute-done.21.come_a.come_b) | copy-start | bytes 3145732
  150.2 15.7 %collective-permute-start.22 = (bf16[2,256,512]{2,1,0:T(8,128)(2,1)S(1)}, bf16[2,256,512]{2,1,0:T(8,128)(2,1)S(1)}, u32[]{:S(2)}, u32[]{:S(2)}) collective-permute-start(bf16[2,256,512]{2,1,0:T(8,128)(2,1)S(1)} %pad_maximum_fusion), channel_id=1, source_target_pairs={{0,2},{1,3},{2,0},{3,1},{4,6},{5,7},{6,4},{7,5},{8,10},{9,11},{10,... | collective-permute-start | bytes 1572872 | tf_op jit(solution)/shard_map/ppermute | solution.py:35
  153.9 12.0 %collective-permute-start.28 = (bf16[160,1024]{1,0:T(8,128)(2,1)S(1)}, bf16[160,1024]{1,0:T(8,128)(2,1)S(1)}, u32[]{:S(2)}, u32[]{:S(2)}) collective-permute-start(bf16[160,1024]{1,0:T(8,128)(2,1)S(1)} %pad_maximum_fusion.1), channel_id=1, source_target_pairs={{0,8},{4,12},{8,0},{12,4},{16,24},{20,28},{24,16},{28,20},{1,9},{5... | collective-permute-start | bytes 983048 | tf_op jit(solution)/shard_map/ppermute | solution.py:35
  154.1 3.7 %collective-permute-start.30 = (f32[4,128]{1,0:T(4,128)S(1)}, f32[4,128]{1,0:T(4,128)S(1)}, u32[]{:S(2)}, u32[]{:S(2)}) collective-permute-start(f32[4,128]{1,0:T(4,128)S(1)} %fusion.7), channel_id=1, source_target_pairs={{0,4},{4,0},{8,12},{12,8},{16,20},{20,16},{24,28},{28,24},{1,5},{5... | collective-permute-start | bytes 6152 | tf_op jit(solution)/shard_map/ppermute | solution.py:35
  157.7 7.6 %collective-permute-start.31 = (f32[4,128]{1,0:T(4,128)S(1)}, f32[4,128]{1,0:T(4,128)S(1)}, u32[]{:S(2)}, u32[]{:S(2)}) collective-permute-start(f32[4,128]{1,0:T(4,128)S(1)} %add.52), channel_id=1, source_target_pairs={{0,8},{4,12},{8,0},{12,4},{16,24},{20,28},{24,16},{28,20},{1,9},{5... | collective-permute-start | bytes 6152 | tf_op jit(solution)/shard_map/ppermute | solution.py:35
  165.9 0.9 copy-start.11
  165.9 1.0 copy-start.9
